TPU v7x, 256 devices: a whole 4x4x8 slice. The times are simulated.
256 devices in a mesh: rows: 32 (over x, z_lo, core), cent: 8 (over y, z_hi).
Axes of the slice: x: 4, y: 4, z: 8 (z_hi: 2, z_lo: 4; z = z_hi * 4 + z_lo), core: 2. Of those that a mesh axis runs over, the one named last changes fastest.
Arguments:
- embeddings: bfloat16 [32768, 768], P('rows'), may hold values from -40 to 40
- centroids: bfloat16 [4096, 768], P('cent'), may hold values from -6 to 6
- codebooks: float32 [96, 8, 256], replicated, may hold values from -6 to 6
Outputs:
- new_centroids: float32 [4096, 768], P('cent')
- new_codebooks: float32 [96, 8, 256], replicated
All inputs are finite; a program needn't handle non-finite values.
Results may differ from a plain program's by a relative error of at most 0.001.
The roundings to bfloat16 on the way count: a program that leaves them out, or rounds other values in their place, can miss the bound.
Values sent between devices are 32-bit elements; how exact they have to be, the bound alone decides.
No kernel may reach another device: no remote copies, remote signals or barrier semaphores. Data moves between devices by JAX's collectives and lax.ppermute only.
A program may use at most 64 MiB of HBM per device.

v0:
```python
import math

import jax
import jax.numpy as jnp
from jax import lax
from jax.sharding import PartitionSpec as P


def codebook_sums(resid, codebooks):
    count = resid.shape[0]
    subspaces = codebooks.shape[0]
    group_size = 8
    groups = subspaces // group_size
    width = codebooks.shape[1]
    parts = resid.reshape(count, groups, group_size, width).transpose(1, 0, 2, 3)
    books = codebooks.reshape(groups, group_size, width, codebooks.shape[2])

    def one_group(pair):
        piece, book = pair
        dots = jnp.einsum("rmd,mdk->rmk", piece, book, precision=lax.Precision.HIGHEST)
        logits = dots - 0.5 * jnp.sum(book * book, axis=1)[None]
        weights = jax.nn.softmax(logits, axis=-1)
        sums = jnp.einsum("rmk,rmd->mdk", weights, piece, precision=lax.Precision.HIGHEST)
        return (sums, jnp.sum(weights, axis=0))

    sums, counts = lax.map(one_group, (parts, books))
    return (sums.reshape(codebooks.shape), counts.reshape(subspaces, codebooks.shape[2]))


def body(embeddings, centroids, codebooks):
    rows_here = embeddings.shape[0]
    width = embeddings.shape[1]
    cent_f = centroids.astype(jnp.float32)
    sq_norms = jnp.sum(cent_f * cent_f, axis=1)
    cross = lax.dot_general(
        embeddings, centroids, (((1,), (1,)), ((), ())), preferred_element_type=jnp.float32
    )
    logits = 3.0 * (cross - 0.5 * sq_norms[None, :]) / math.sqrt(width)
    top = lax.pmax(jnp.max(logits, axis=1), "cent")
    total = lax.psum(jnp.sum(jnp.exp(logits - top[:, None]), axis=1), "cent")
    weights = jnp.exp(logits - top[:, None]) / total[:, None]
    wb = weights.astype(jnp.bfloat16)
    mass = lax.dot_general(
        wb, embeddings, (((0,), (0,)), ((), ())), preferred_element_type=jnp.float32
    )
    counts = jnp.sum(weights, axis=0)
    share = rows_here // lax.axis_size("cent")
    recon_mine = lax.psum_scatter(
        jnp.dot(wb, centroids, preferred_element_type=jnp.float32),
        "cent",
        scatter_dimension=0,
        tiled=True,
    )
    begin = lax.axis_index("cent") * share
    mine = lax.dynamic_slice_in_dim(embeddings, begin, share, 0).astype(jnp.float32)
    resid = mine - recon_mine
    mass_all, counts_all = lax.psum((mass, counts), "rows")
    new_centroids = (mass_all + cent_f) / (counts_all[:, None] + 1.0)
    sums, tallies = codebook_sums(resid, codebooks)
    sums_all, tallies_all = lax.psum((sums, tallies), ("rows", "cent"))
    new_codebooks = (sums_all + codebooks) / (tallies_all[:, None, :] + 1.0)
    return (new_centroids, new_codebooks)


def solution(mesh):
    in_specs = (P("rows", None), P("cent", None), P())
    out_specs = (P("cent", None), P())
    return jax.shard_map(body, mesh=mesh, in_specs=in_specs, out_specs=out_specs, check_vma=False)
```

profile of v0, /device:TPU:1, one launch (start us, length us, event | category | flops | bytes accessed | tf_op | source)
XLA Modules:
  0.0 647.3 jit_solution(2075425391887159222)
XLA Ops:
  8.0 1.4 fusion.18
  9.4 2.6 fusion.15
  12.1 30.7 %pmax.7 = f32[1024]{0:T(1024)S(1)} all-reduce(f32[1024]{0:T(1024)S(1)} %get-tuple-element.46), channel_id=1, replica_groups=mesh['rows'=32,'cent'=8] {'cent'}, use_global_device_ids=true, to_apply=%region_2.0 | all-reduce | flops 1024 | bytes 8192 | tf_op jit(solution)/shard_map/pmax | solution.py:39
  43.3 20.4 %psum.35 = f32[1024]{0:T(1024)S(1)} all-reduce(f32[1024]{0:T(1024)S(1)} %fusion.17), channel_id=1, replica_groups=mesh['rows'=32,'cent'=8] {'cent'}, use_global_device_ids=true, to_apply=%region_4.0 | all-reduce | flops 1024 | bytes 8192 | tf_op jit(solution)/shard_map/psum | solution.py:40
  63.6 3.0 fusion.20
  66.7 3.8 fusion.22
  70.6 0.7 fusion.25
  71.3 79.1 %psum.37 = f32[512]{0:T(512)S(1)} all-reduce(f32[512]{0:T(512)S(1)} %fusion.25), channel_id=1, replica_groups=mesh['rows'=32,'cent'=8] {'rows'}, use_global_device_ids=true, to_apply=%region_7.0 | all-reduce | flops 512 | bytes 4096 | tf_op jit(solution)/shard_map/psum | solution.py:57
  150.3 33.8 %reduce-scatter.2.cloned.1.call-done = f32[128,768]{1,0:T(8,128)} async-done(((f32[1024,768]{1,0:T(8,128)}), f32[128,768]{1,0:T(8,128)}) %reduce-scatter.2.cloned.1.call-update) | async-done | bytes 393232 | tf_op jit(solution)/shard_map/reduce_scatter | solution.py:48
  184.2 1.1 convert_subtract_fusion
  185.4 80.1 %while.12 = (s32[]{:T(128)}, f32[12,8,8,256]{3,2,1,0:T(8,128)}, f32[12,8,256]{2,1,0:T(8,128)}, f32[12,128,8,8]{1,3,2,0:T(8,128)S(1)}, f32[12,8,8,256]{3,2,1,0:T(8,128)}, /*index=5*/s32[]{:T(128)}) while((s32[]{:T(128)}, f32[12,8,8,256]{3,2,1,0:T(8,128)}, f32[12,8,256]{2,1,0:T(8,128)}, f32[12,128,8,8]{1,3,2,0:T(8,128)S(1)}, ...), condition=%wide.region_14.15_spmd, body=%wide.region_9.14_spmd.sunk | while | flops 52719616 | bytes 4545097 | solution.py:26
  185.4 0.9 fusion.41
  186.3 3.0 fusion.42
  189.8 0.6 bitcast_dynamic-update-slice_fusion.2
  190.4 1.7 fusion.44
  192.1 0.9 fusion.41
  193.0 3.0 fusion.42
  196.5 0.6 bitcast_dynamic-update-slice_fusion.2
  197.1 1.7 fusion.44
  198.8 0.9 fusion.41
  199.6 3.0 fusion.42
  203.2 0.6 bitcast_dynamic-update-slice_fusion.2
  203.8 1.7 fusion.44
  205.4 0.9 fusion.41
  206.3 3.0 fusion.42
  209.8 0.6 bitcast_dynamic-update-slice_fusion.2
  210.4 1.7 fusion.44
  212.1 0.9 fusion.41
  213.0 3.0 fusion.42
  216.5 0.6 bitcast_dynamic-update-slice_fusion.2
  217.1 1.7 fusion.44
  218.8 0.9 fusion.41
  219.7 3.0 fusion.42
  223.2 0.6 bitcast_dynamic-update-slice_fusion.2
  223.8 1.7 fusion.44
  225.4 0.9 fusion.41
  226.3 3.0 fusion.42
  229.9 0.6 bitcast_dynamic-update-slice_fusion.2
  230.5 1.7 fusion.44
  232.1 0.9 fusion.41
  233.0 3.0 fusion.42
  236.5 0.6 bitcast_dynamic-update-slice_fusion.2
  237.1 1.7 fusion.44
  238.8 0.9 fusion.41
  239.7 3.0 fusion.42
  243.2 0.6 bitcast_dynamic-update-slice_fusion.2
  243.8 1.7 fusion.44
  245.5 0.9 fusion.41
  246.3 3.0 fusion.42
  249.9 0.6 bitcast_dynamic-update-slice_fusion.2
  250.5 1.7 fusion.44
  252.1 0.9 fusion.41
  253.0 3.0 fusion.42
  256.5 0.6 bitcast_dynamic-update-slice_fusion.2
  257.1 1.7 fusion.44
  258.8 0.9 fusion.41
  259.7 3.0 fusion.42
  263.2 0.6 bitcast_dynamic-update-slice_fusion.2
  263.8 1.7 fusion.44
  265.5 113.4 %all-reduce.4.cloned.1.call-done = f32[512,768]{1,0:T(8,128)} async-done(((f32[512,768]{1,0:T(8,128)}), f32[512,768]{1,0:T(8,128)}) %all-reduce.4.cloned.1.call-update) | async-done | bytes 1572880 | tf_op jit(solution)/shard_map/psum | solution.py:57
  378.9 2.8 fusion.19
  381.6 255.2 %all-reduce.6.cloned.1.call-done = (f32[96,8,256]{2,1,0:T(8,128)}, f32[96,256]{1,0:T(8,128)}) async-done(((f32[96,8,256]{2,1,0:T(8,128)}, f32[96,256]{1,0:T(8,128)}), (f32[96,8,256]{2,1,0:T(8,128)}, f32[96,256]{1,0:T(8,128)})) %all-reduce.6.cloned.1.call-update) | async-done | bytes 884752 | tf_op jit(solution)/shard_map/psum | solution.py:60
  636.8 0.9 broadcast_add_fusion
  637.7 2.1 add_divide_fusion
  (52 shorter events, 7.1 us)
Async XLA Ops:
  8.0 176.2 %reduce-scatter.2.cloned.1.call-start = ((), (), s32[]{:S(2)}) async-start(), calls=%async_computation.2 | async-start | bytes 3538944 | tf_op jit(solution)/shard_map/reduce_scatter | solution.py:48
  12.0 51.6 %copy-start = (bf16[512,768]{1,0:T(8,128)(2,1)S(1)}, bf16[512,768]{1,0:T(8,128)(2,1)}, u32[]{:S(2)}) copy-start(bf16[512,768]{1,0:T(8,128)(2,1)} %param.6) | copy-start | bytes 2359300
  66.6 312.2 %all-reduce.4.cloned.1.call-start = ((), (), s32[]{:S(2)}) async-start(), calls=%async_computation.1 | async-start | bytes 3145728 | tf_op jit(solution)/shard_map/psum | solution.py:57
  70.5 566.3 %all-reduce.6.cloned.1.call-start = ((), (), s32[]{:S(2)}) async-start(), calls=%async_computation.3 | async-start | bytes 1769472 | tf_op jit(solution)/shard_map/psum | solution.py:60
  265.5 372.2 %copy-start.1 = (f32[12,8,8,256]{3,2,1,0:T(8,128)S(1)}, f32[12,8,8,256]{3,2,1,0:T(8,128)}, u32[]{:S(2)}) copy-start(f32[12,8,8,256]{3,2,1,0:T(8,128)} %get-tuple-element.109) | copy-start | bytes 2359300
Sparse Core Ops, SparseCore 0:
  66.8 117.3 reduce-scatter.1
Sparse Core Ops, SparseCore 1:
  70.6 308.2 all-reduce.3
  384.9 251.9 all-reduce.5
where the time goes:
time: 649 us; the launch traced here: 647 us
  waiting for transfers between devices  402 us (62%)
  blocking collectives  130 us (20%)
  matrix products  65.3 us (10%)
  other arithmetic  26 us (4%)
  between operations  15.6 us (2%)
  local copies, waits for them, and re-layouts  7.38 us (1%)
    psum x1, waiting for transfers between devices, body(): sums_all, tallies_all = lax.psum((sums, tallies), ('rows', 'cent'))  255 us
    psum x1, waiting for transfers between devices, body(): mass_all, counts_all = lax.psum((mass, counts), 'rows')  113 us
    psum x1, blocking collectives, body(): mass_all, counts_all = lax.psum((mass, counts), 'rows')  79.1 us
    dot_general x12, matrix products, one_group(): jnp.einsum('rmd,mdk->rmk', piece, book, precision=lax.Precision.HIGHEST)  35.9 us
    reduce_scatter x1, waiting for transfers between devices, body(): lax.psum_scatter(jnp.dot(wb, centroids, preferred_element_type=jnp.float3...  33.8 us
    pmax x1, blocking collectives, body(): top = lax.pmax(jnp.max(logits, axis=1), 'cent')  30.7 us
    psum x1, blocking collectives, body(): total = lax.psum(jnp.sum(jnp.exp(logits - top[:, None]), axis=1), 'cent')  20.4 us
    dot_general x12, matrix products, one_group(): jnp.einsum('rmk,rmd->mdk', weights, piece, precision=lax.Precision.HIGHEST)  20 us
  transfers between devices with their start and end apart: 3, of which 3 were waited for; matrix products, arithmetic and copies ran while one was open for 14% of the time, Pallas kernels for 0%

commit v1 on v0

v1 whole, which is shorter than its diff:
```python
import itertools
import math

import jax
import jax.numpy as jnp
from jax import lax
from jax.experimental import pallas as pl
from jax.experimental.pallas import tpu as pltpu
from jax.sharding import PartitionSpec as P

NX, NY, NZL, NZH, NC = 4, 4, 4, 2, 2
BOTH = ("rows", "cent")
F32, BF16 = jnp.float32, jnp.bfloat16


def flat(x, y, zl, zh, c):
    return ((x * NZL + zl) * NC + c) * (NY * NZH) + (y * NZH + zh)


def hop(value, move):
    pairs = []
    for place in itertools.product(range(NX), range(NY), range(NZL), range(NZH), range(NC)):
        pairs.append((flat(*place), flat(*move(*place))))
    return lax.ppermute(value, BOTH, pairs)


def along_x(k):
    return lambda x, y, zl, zh, c: ((x + k) % NX, y, zl, zh, c)


def along_y(k):
    return lambda x, y, zl, zh, c: (x, (y + k) % NY, zl, zh, c)


def along_zl(k):
    return lambda x, y, zl, zh, c: (x, y, zl ^ k, zh, c)


def other_zh(x, y, zl, zh, c):
    return (x, y, zl, 1 - zh, c)


def other_core(x, y, zl, zh, c):
    return (x, y, zl, zh, 1 - c)


def call(kernel, out, args, smem=0, scratch=(), flops=0, limit=48):
    nbytes = sum(a.size * a.dtype.itemsize for a in args)
    specs = [pl.BlockSpec(memory_space=pltpu.SMEM)] * smem
    specs += [pl.BlockSpec(memory_space=pltpu.VMEM)] * (len(args) - smem)
    return pl.pallas_call(
        kernel,
        out_shape=out,
        in_specs=specs,
        out_specs=jax.tree.map(lambda _: pl.BlockSpec(memory_space=pltpu.VMEM), out),
        scratch_shapes=list(scratch),
        compiler_params=pltpu.CompilerParams(vmem_limit_bytes=limit * 1024 * 1024),
        cost_estimate=pl.CostEstimate(flops=flops, bytes_accessed=2 * nbytes, transcendentals=0),
    )(*args)


def shape(dims, dtype=F32):
    return jax.ShapeDtypeStruct(dims, dtype)


def dot(a, b, ca, cb):
    return lax.dot_general(a, b, (((ca,), (cb,)), ((), ())), preferred_element_type=F32)


def logits_kernel(emb_ref, cent_ref, p_ref, stat_ref):
    rows, width = emb_ref.shape
    cent = cent_ref[...]
    cent_f = cent.astype(F32)
    half_sq = 0.5 * jnp.sum(cent_f * cent_f, axis=1, keepdims=True)
    step = 256
    tops, sums = [], []
    for start in range(0, rows, step):
        cross = dot(cent, emb_ref[start : start + step, :], 1, 1)
        logits = (cross - half_sq) * (3.0 / math.sqrt(width))
        top = jnp.max(logits, axis=0, keepdims=True)
        p = jnp.exp(logits - top)
        p_ref[:, start : start + step] = p
        tops.append(top)
        sums.append(jnp.sum(p, axis=0, keepdims=True))
    block = jnp.concatenate(
        [
            jnp.concatenate(tops, axis=1).reshape(rows // 128, 128),
            jnp.concatenate(sums, axis=1).reshape(rows // 128, 128),
        ],
        axis=0,
    )
    for i in range(stat_ref.shape[0]):
        stat_ref[i] = block


def weights_kernel(place_ref, p_ref, mine_ref, stat_ref, cent_t_ref, wb_ref, count_ref, *out_refs):
    y, zh = place_ref[1], place_ref[3]
    half = stat_ref.shape[1] // 2
    tops = stat_ref[:, :half, :]
    top = jnp.max(tops, axis=0)
    total = jnp.sum(stat_ref[:, half:, :] * jnp.exp(tops - top[None]), axis=0)
    scale = jnp.exp(mine_ref[0, :half, :] - top) / total
    scale = scale.reshape(1, p_ref.shape[1])
    w = p_ref[...] * scale
    count_ref[...] = jnp.broadcast_to(jnp.sum(w, axis=1, keepdims=True), count_ref.shape)
    wb_ref[...] = w.astype(BF16)
    share = out_refs[0].shape[0]
    for part in range(2):
        for k in range(NY):
            side = (1 - zh) if part == 0 else zh
            start = ((y + k) % NY) * (NZH * share) + side * share
            piece = cent_t_ref[pl.ds(pl.multiple_of(start, 16), share), :]
            out_refs[part * NY + k][...] = dot(piece, wb_ref[...], 1, 0)


def mass_kernel(place_ref, wb_ref, count_ref, emb_ref, keep_ref, send_ref):
    c = place_ref[4]
    half, width = keep_ref.shape[0], emb_ref.shape[1]
    for ref, side in ((keep_ref, c), (send_ref, 1 - c)):
        here = pl.ds(pl.multiple_of(side * half, 16), half)
        ref[:, :width] = dot(wb_ref[here, :], emb_ref[...], 1, 0)
        ref[:, width:] = count_ref[here, :]


def pieces(v):
    hi = v.astype(BF16).astype(F32)
    rest = v - hi
    mid = rest.astype(BF16).astype(F32)
    return hi, mid, rest - mid


def codebook_kernel(emb_t_ref, a_ref, b_ref, c_ref, d_ref, e_ref, books_ref, out_ref):
    subspaces, depth, codes = books_ref.shape
    rows = emb_t_ref.shape[1]
    ones = jnp.where(lax.broadcasted_iota(jnp.int32, (2 * depth, rows), 0) < 3, 1.0, 0.0)
    for m in range(subspaces):
        at = slice(m * depth, (m + 1) * depth)
        recon = a_ref[at, :] + b_ref[at, :] + c_ref[at, :] + d_ref[at, :] + e_ref[at, :]
        r = emb_t_ref[at, :] - recon
        r0, r1, r2 = pieces(r)
        book = books_ref[m]
        k0, k1, k2 = pieces(book)
        s0, s1, s2 = pieces(-0.5 * jnp.sum(book * book, axis=0, keepdims=True))
        zero = jnp.zeros((2 * depth - 3, codes), F32)
        left = jnp.concatenate([k0, k0, k1, k0, k2, k1, s0, s1, s2, zero], axis=0).astype(BF16)
        right = jnp.concatenate([r0, r1, r0, r2, r0, r1, ones], axis=0).astype(BF16)
        logits = dot(left, right, 0, 0)
        p = jnp.exp(logits - jnp.max(logits, axis=0, keepdims=True))
        inv = 1.0 / jnp.sum(p, axis=0, keepdims=True)
        q0, q1, q2 = pieces(r * inv)
        i0, i1, i2 = pieces(jnp.broadcast_to(inv, (depth, rows)))
        scaled = jnp.concatenate([q0, q1, q2, i0, i1, i2], axis=0).astype(BF16)
        p_hi = p.astype(BF16)
        p_lo = (p - p_hi.astype(F32)).astype(BF16)
        high = dot(scaled, p_hi, 1, 1)
        low = dot(scaled, p_lo, 1, 1)
        mass = high[:depth] + (high[depth : 2 * depth] + (high[2 * depth : 3 * depth] + low[:depth]))
        mass = mass + low[depth : 2 * depth]
        o = 3 * depth
        count = high[o : o + 1] + (high[o + depth : o + depth + 1] + low[o : o + 1])
        count = count + high[o + 2 * depth : o + 2 * depth + 1] + low[o + depth : o + depth + 1]
        for d in range(depth):
            owner, slot = divmod(m * depth + d, 3)
            core, xz = divmod(owner, NX * NZL)
            row = xz * NC + core
            out_ref[row, slot : slot + 1, :] = mass[d : d + 1]
            out_ref[row, slot + 3 : slot + 4, :] = count


def update_kernel(parts_ref, book_ref, out_ref):
    total = jnp.sum(parts_ref[...], axis=0)
    new = (total[:3] + book_ref[:3]) / (total[3:6] + 1.0)
    tile = jnp.concatenate([new[:, :128], new[:, 128:], jnp.zeros((2, 128), F32)], axis=0)
    for i in range(out_ref.shape[0]):
        out_ref[i] = tile


def books_kernel(place_ref, mine_ref, theirs_ref, out_ref):
    core = place_ref[4]
    count = mine_ref.shape[0]
    group = NX * NZL

    def place(first_ref, second_ref):
        for side, ref in ((0, first_ref), (1, second_ref)):
            for i in range(count):
                cent, xz = divmod(i, group)
                row = (cent * NC + side) * group * 3 + xz * 3
                out_ref[row : row + 3, :128] = ref[i, :3, :]
                out_ref[row : row + 3, 128:] = ref[i, 3:6, :]

    @pl.when(core == 0)
    def _():
        place(mine_ref, theirs_ref)

    @pl.when(core == 1)
    def _():
        place(theirs_ref, mine_ref)


def centroids_kernel(place_ref, mine_ref, theirs_ref, out_ref):
    x, zl, c = place_ref[0], place_ref[2], place_ref[4]
    rows = mine_ref.shape[0] // (NX * NZL)
    for ref, side in ((mine_ref, c), (theirs_ref, 1 - c)):
        for kx in range(NX):
            for kz in range(NZL):
                spot = (side * NX + (x + NX - kx) % NX) * NZL + lax.bitwise_xor(zl, kz)
                at = (kx * NZL + kz) * rows
                out_ref[pl.ds(pl.multiple_of(spot * rows, 8), rows), :] = ref[at : at + rows, :]


def body(embeddings, centroids, codebooks):
    rows_here, width = embeddings.shape
    held = centroids.shape[0]
    subspaces, depth, codes = codebooks.shape
    row_at = lax.axis_index("rows")
    cent_at = lax.axis_index("cent")
    x, zl, c = row_at // (NZL * NC), (row_at // NC) % NZL, row_at % NC
    y, zh = cent_at // NZH, cent_at % NZH
    place = jnp.stack([x, y, zl, zh, c]).astype(jnp.int32)
    cents = NY * NZH
    share = width // cents

    p, stat = call(
        logits_kernel,
        (shape((held, rows_here)), shape((cents, 2 * rows_here // 128, 128))),
        (embeddings, centroids),
        flops=2 * rows_here * held * width,
    )
    stats = lax.all_to_all(stat, "cent", 0, 0, tiled=True)
    outs = call(
        weights_kernel,
        (shape((held, rows_here), BF16), shape((held, 128))) + (shape((share, rows_here)),) * 8,
        (place, p, stat, stats, centroids.T),
        smem=1,
        flops=2 * rows_here * held * width,
    )
    wb, counts, theirs, mine = outs[0], outs[1], outs[2:6], outs[6:10]
    steps = (1, -1, 2)
    got = [hop(theirs[k % NY], along_y(k)) for k in steps]
    got_mine = [hop(mine[k % NY], along_y(k)) for k in steps]
    peer = hop(theirs[0] + got[0] + got[1] + got[2], other_zh)

    keep, send = call(
        mass_kernel,
        (shape((held // 2, width + 128)),) * 2,
        (place, wb, counts, embeddings),
        smem=1,
        flops=2 * rows_here * held * width,
    )
    mass = keep + hop(send, other_core)
    groups = [
        [(xx * NZL + zz) * NC + cc for xx in range(NX) for zz in range(NZL)] for cc in range(NC)
    ]
    peers = NX * NZL
    piece_rows = held // (2 * peers)
    parts = lax.all_to_all(
        mass.reshape(peers, piece_rows, width + 128), "rows", 0, 0, tiled=True, axis_index_groups=groups
    )
    total = jnp.sum(parts, axis=0)
    first = c * (held // 2) + (x * NZL + zl) * piece_rows
    old = lax.dynamic_slice_in_dim(centroids, first, piece_rows, 0).astype(F32)
    new = (total[:, :width] + old) / (total[:, width : width + 1] + 1.0)

    emb_t = lax.dynamic_slice_in_dim(embeddings, cent_at * share, share, 1).T.astype(F32)
    per = subspaces // cents
    my_books = lax.dynamic_slice_in_dim(codebooks, cent_at * per, per, 0)
    sums = call(
        codebook_kernel,
        shape((NX * NZL * NC, 8, codes)),
        (emb_t, mine[0], *got_mine, peer, my_books),
        flops=4 * rows_here * per * codes * 64,
    )
    new_z = jnp.concatenate([new] + [hop(new, along_zl(k)) for k in (1, 2, 3)], axis=0)
    owner = c * peers + x * NZL + zl
    flat_books = jnp.pad(codebooks.reshape(subspaces * depth, codes), ((0, 8), (0, 0)))
    my_rows = lax.dynamic_slice_in_dim(flat_books, (cent_at * NC * peers + owner) * 3, 8, 0)
    all_parts = lax.all_to_all(sums, "rows", 0, 0, tiled=True)
    same_core = [
        [flat(xx, yy, zz, hh, cc) for yy in range(NY) for hh in range(NZH) for xx in range(NX) for zz in range(NZL)]
        for cc in range(NC)
    ]
    tile = call(update_kernel, shape((cents * peers, 8, 128)), (all_parts, my_rows))
    new_x = jnp.concatenate([new_z] + [hop(new_z, along_x(k)) for k in (1, 2, 3)], axis=0)
    new_other = hop(new_x, other_core)
    new_centroids = call(
        centroids_kernel, shape((held, width)), (place, new_x, new_other), smem=1
    )
    tiles = lax.all_to_all(tile, BOTH, 0, 0, tiled=True, axis_index_groups=same_core)
    tiles_other = hop(tiles, other_core)
    new_books = call(
        books_kernel, shape((subspaces * depth, codes)), (place, tiles, tiles_other), smem=1
    )
    return (new_centroids, new_books.reshape(codebooks.shape))


def solution(mesh):
    in_specs = (P("rows", None), P("cent", None), P())
    out_specs = (P("cent", None), P())
    return jax.shard_map(body, mesh=mesh, in_specs=in_specs, out_specs=out_specs, check_vma=False)
```

time: 649 us -> 162 us (0.25)
  waiting for transfers between devices: 402 us -> 59.3 us
  blocking collectives: 130 us -> 0 us
  matrix products: 65.3 us -> 0 us
  starting transfers between devices: 0.13 us -> 64.9 us
  other arithmetic: 26 us -> 4.56 us
  Pallas kernels: 0 us -> 21.1 us
  between operations: 15.6 us -> 0.89 us
    psum x2 -> x0, waiting for transfers between devices: 369 us -> none  [the longest x1 255 us: body(): sums_all, tallies_all = lax.psum((sums, tallies), ('rows', 'cent'))]
    psum x2 -> x0, blocking collectives: 99.5 us -> none  [the longest x1 79.1 us: body(): mass_all, counts_all = lax.psum((mass, counts), 'rows')]
    dot_general x27 -> x0, matrix products: 65.3 us -> none  [the longest x12 35.9 us: one_group(): jnp.einsum('rmd,mdk->rmk', piece, book, precision=lax.Precision.HIGHEST)]
    all_to_all x0 -> x4, starting transfers between devices: none -> 45.3 us  [the longest x1 19.1 us: body(): all_parts = lax.all_to_all(sums, 'rows', 0, 0, tiled=True)]
    ppermute x0 -> x16, waiting for transfers between devices: none -> 42.4 us  [hop(): return lax.ppermute(value, BOTH, pairs)]
    reduce_scatter x1 -> x0, waiting for transfers between devices: 33.8 us -> none  [body(): lax.psum_scatter(jnp.dot(wb, centroids, preferred_element_type=jnp.float3...]
    pmax x1 -> x0, blocking collectives: 30.7 us -> none  [body(): top = lax.pmax(jnp.max(logits, axis=1), 'cent')]
    pallas_call x0 -> x7, Pallas kernels: none -> 21.1 us  [call(): pl.pallas_call(kernel, out_shape=out, in_specs=specs, out_specs=jax.tree....]
  transfers between devices with their start and end apart: 3 -> 20, of which waited for: 3 -> 11; matrix products, arithmetic and copies ran while one was open for 14% -> 4% of each run, Pallas kernels for 0% -> 8%
where the time goes in v1:
time: 162 us; the launch traced here: 161 us
  starting transfers between devices  64.9 us (40%)
  waiting for transfers between devices  59.3 us (37%)
  Pallas kernels  21.1 us (13%)
  local copies, waits for them, and re-layouts  10.3 us (6%)
  other arithmetic  4.56 us (3%)
    ppermute x16, waiting for transfers between devices, hop(): return lax.ppermute(value, BOTH, pairs)  42.4 us
    pallas_call x7, Pallas kernels, call(): pl.pallas_call(kernel, out_shape=out, in_specs=specs, out_specs=jax.tree....  21.1 us
    ppermute x16, starting transfers between devices, hop(): return lax.ppermute(value, BOTH, pairs)  19.6 us
    all_to_all x1, starting transfers between devices, body(): all_parts = lax.all_to_all(sums, 'rows', 0, 0, tiled=True)  19.1 us
    all_to_all x1, starting transfers between devices, body(): stats = lax.all_to_all(stat, 'cent', 0, 0, tiled=True)  11.7 us
    all_to_all x1, starting transfers between devices, body(): lax.all_to_all(tile, BOTH, 0, 0, tiled=True, axis_index_groups=same_core)  8.89 us
    all_to_all x1, waiting for transfers between devices, body(): stats = lax.all_to_all(stat, 'cent', 0, 0, tiled=True)  8.68 us
    unnamed x31, local copies, waits for them, and re-layouts  8.14 us
  transfers between devices with their start and end apart: 20, of which 11 were waited for; matrix products, arithmetic and copies ran while one was open for 4% of the time, Pallas kernels for 8%

profile of v1, /device:TPU:1, one launch (start us, length us, event | category | flops | bytes accessed | tf_op | source)
XLA Modules:
  0.0 161.1 jit_solution(14431449916939496772)
XLA Ops:
  0.6 1.1 copy-done.1
  1.8 1.4 copy-done.3
  3.2 2.1 %shard_map.50 = (f32[512,1024]{1,0:T(8,128)S(1)}, f32[8,16,128]{2,1,0:T(8,128)}) custom-call(bf16[1024,768]{1,0:T(8,128)(2,1)S(1)} %copy-done.3, bf16[512,768]{1,0:T(8,128)(2,1)S(1)} %copy-done.1), custom_call_target="tpu_custom_call" | custom-call | flops 805306368 | bytes 4718592 | tf_op jit(solution)/shard_map/pallas_call | solution.py:51
  5.3 1.3 copy-done
  6.6 11.7 %all-to-all-start = ((f32[8,16,128]{2,1,0:T(8,128)}), f32[8,16,128]{2,1,0:T(8,128)S(1)}, u32[]{:S(2)}, u32[]{:S(2)}) async-start(f32[8,16,128]{2,1,0:T(8,128)} %get-tuple-element.17.mine_ref), calls=%async_computation | async-start | bytes 131072 | tf_op jit(solution)/shard_map/all_to_all | solution.py:229
  18.3 0.3 copy.7
  18.6 0.1 stack.23.place_ref
  18.7 8.7 %all-to-all-done.stat_ref = f32[8,16,128]{2,1,0:T(8,128)S(1)} async-done(((f32[8,16,128]{2,1,0:T(8,128)}), f32[8,16,128]{2,1,0:T(8,128)S(1)}, u32[]{:S(2)}, u32[]{:S(2)}) %all-to-all-start) | async-done | bytes 65568 | tf_op jit(solution)/shard_map/all_to_all | solution.py:229
  27.4 3.2 %shard_map.51 = (bf16[512,1024]{1,0:T(8,128)(2,1)S(1)}, f32[512,128]{1,0:T(8,128)S(1)}, f32[96,1024]{1,0:T(8,128)S(1)}, f32[96,1024]{1,0:T(8,128)S(1)}, f32[96,1...) custom-call(s32[5]{0:T(128)S(1)} %stack.23.place_ref, ...), custom_call_target="tpu_custom_call" | custom-call | flops 805306368 | bytes 6029352 | tf_op jit(solution)/shard_map/pallas_call | solution.py:51
  30.6 0.7 copy-done.5
  31.3 0.7 copy-done.7
  32.1 0.7 copy-done.9
  32.8 0.1 copy-done.10
  32.9 1.4 copy-done.4
  34.3 1.5 shard_map.52
  35.9 2.2 %collective-permute-start = (f32[256,896]{1,0:T(8,128)S(1)}, f32[256,896]{1,0:T(8,128)S(1)}, u32[]{:S(2)}, u32[]{:S(2)}) collective-permute-start(f32[256,896]{1,0:T(8,128)S(1)} %get-tuple-element.21), channel_id=1, source_target_pairs={{0,8},{8,0},{1,9},{9,1},{16,24},{24,16},{17,25},{25,17},{32,40},{4... | collective-permute-start | bytes 2752520 | tf_op jit(solution)/shard_map/ppermute | solution.py:24
  38.1 2.1 %collective-permute-done = f32[256,896]{1,0:T(8,128)S(1)} collective-permute-done((f32[256,896]{1,0:T(8,128)S(1)}, f32[256,896]{1,0:T(8,128)S(1)}, u32[]{:S(2)}, u32[]{:S(2)}) %collective-permute-start) | collective-permute-done | bytes 917536 | tf_op jit(solution)/shard_map/ppermute | solution.py:24
  40.2 1.0 add.63
  41.2 5.7 %all-to-all-start.1 = ((f32[16,16,896]{2,1,0:T(8,128)}), f32[16,16,896]{2,1,0:T(8,128)}, u32[]{:S(2)}, u32[]{:S(2)}) async-start(f32[16,16,896]{2,1,0:T(8,128)} %bitcast.12), calls=%async_computation.1 | async-start | bytes 1835008 | tf_op jit(solution)/shard_map/all_to_all | solution.py:256
  46.9 0.4 collective-permute-start.11
  47.2 2.4 %collective-permute-start.12 = (f32[96,1024]{1,0:T(8,128)}, f32[96,1024]{1,0:T(8,128)}, u32[]{:S(2)}, u32[]{:S(2)}) collective-permute-start(f32[96,1024]{1,0:T(8,128)} %copy-done.9), channel_id=1, source_target_pairs={{0,6},{8,14},{1,7},{9,15},{16,22},{24,30},{17,23},{25,31},{32,38},... | collective-permute-start | bytes 1179656 | tf_op jit(solution)/shard_map/ppermute | solution.py:24
  49.6 0.0 collective-permute-start.13
  49.6 3.0 %collective-permute-start.10 = (f32[96,1024]{1,0:T(8,128)S(1)}, f32[96,1024]{1,0:T(8,128)}, u32[]{:S(2)}, u32[]{:S(2)}) collective-permute-start(f32[96,1024]{1,0:T(8,128)S(1)} %copy-done.6), channel_id=1, source_target_pairs={{0,4},{8,12},{1,5},{9,13},{16,20},{24,28},{17,21},{25,29},{32,36},... | collective-permute-start | bytes 1179656 | tf_op jit(solution)/shard_map/ppermute | solution.py:24
  52.6 0.0 collective-permute-start.8
  52.6 6.5 %collective-permute-done.11 = f32[96,1024]{1,0:T(8,128)} collective-permute-done((f32[96,1024]{1,0:T(8,128)}, f32[96,1024]{1,0:T(8,128)}, u32[]{:S(2)}, u32[]{:S(2)}) %collective-permute-start.11) | collective-permute-done | bytes 393248 | tf_op jit(solution)/shard_map/ppermute | solution.py:24
  59.1 0.0 collective-permute-start.9
  59.1 0.0 collective-permute-done.12
  59.1 7.2 %collective-permute-done.13 = f32[96,1024]{1,0:T(8,128)} collective-permute-done((f32[96,1024]{1,0:T(8,128)S(1)}, f32[96,1024]{1,0:T(8,128)}, u32[]{:S(2)}, u32[]{:S(2)}) %collective-permute-start.13) | collective-permute-done | bytes 393248 | tf_op jit(solution)/shard_map/ppermute | solution.py:24
  66.3 2.1 %add_add_fusion = f32[96,1024]{1,0:T(8,128)} fusion(f32[96,1024]{1,0:T(8,128)} %collective-permute-done.13, f32[96,1024]{1,0:T(8,128)} %collective-permute-done.12, f32[96,1024]{1,0:T(8,128)S(1)} %get-tuple-element.26, f32[96,1024]{1,0:T(8,128)} %collective-permute-done.11), kind=kLoop, calls=%fused_computation.2 | loop fusion | flops 294912 | bytes 1966080 | tf_op jit(solution)/shard_map/add | solution.py:241
  68.4 0.5 collective-permute-start.14
  68.9 1.2 constant_dynamic-slice_fusion.1
  70.0 0.1 copy.9
  70.2 0.9 constant_dynamic-slice_fusion.books_ref
  71.1 3.6 %collective-permute-done.10.d_ref = f32[96,1024]{1,0:T(8,128)} collective-permute-done((f32[96,1024]{1,0:T(8,128)S(1)}, f32[96,1024]{1,0:T(8,128)}, u32[]{:S(2)}, u32[]{:S(2)}) %collective-permute-start.10) | collective-permute-done | bytes 393248 | tf_op jit(solution)/shard_map/ppermute | solution.py:24
  74.8 9.0 %collective-permute-done.8.b_ref = f32[96,1024]{1,0:T(8,128)} collective-permute-done((f32[96,1024]{1,0:T(8,128)S(1)}, f32[96,1024]{1,0:T(8,128)}, u32[]{:S(2)}, u32[]{:S(2)}) %collective-permute-start.8) | collective-permute-done | bytes 393248 | tf_op jit(solution)/shard_map/ppermute | solution.py:24
  83.8 0.0 collective-permute-done.9.c_ref
  83.8 0.0 collective-permute-done.14.e_ref
  83.8 10.0 %shard_map.54 = f32[32,8,256]{2,1,0:T(8,128)} custom-call(f32[96,1024]{1,0:T(8,128)S(1)} %convert_bitcast_fusion.emb_t_ref, f32[96,1024]{1,0:T(8,128)S(1)} %get-tuple-element.22.a_ref, f32[96,1024]{1,0:T(8,128)} %collective-permute-done.8.b_ref, f32[96,1024]{1,0:T(8,128)} %collective-permute-done.9.c_ref, f32[96,1024]{1,0:T(8,128)} %collective-permute-done.10.d_ref, ...), custom_call_target="tpu_custom_call" | custom-call | flops 805306368 | bytes 4915200 | tf_op jit(solution)/shard_map/pallas_call | solution.py:51
  93.7 0.0 all-to-all-done.1
  93.7 19.1 %all-to-all-start.2 = ((f32[32,8,256]{2,1,0:T(8,128)}), f32[32,8,256]{2,1,0:T(8,128)S(1)}, u32[]{:S(2)}, u32[]{:S(2)}) async-start(f32[32,8,256]{2,1,0:T(8,128)} %shard_map.54), calls=%async_computation.2 | async-start | bytes 524288 | tf_op jit(solution)/shard_map/all_to_all | solution.py:277
  112.9 1.2 reduce_sum.9
  114.1 0.1 fusion.1
  114.2 0.1 constant_dynamic-update-slice_fusion.6
  114.3 1.5 collective-permute-start.1
  115.8 2.1 %collective-permute-start.2 = (f32[16,768]{1,0:T(8,128)S(1)}, f32[16,768]{1,0:T(8,128)S(1)}, u32[]{:S(2)}, u32[]{:S(2)}) collective-permute-start(f32[16,768]{1,0:T(8,128)S(1)} %get-tuple-element.31), channel_id=1, source_target_pairs={{0,32},{8,40},{1,33},{9,41},{16,48},{24,56},{17,49},{25,57},{32,0}... | collective-permute-start | bytes 147464 | tf_op jit(solution)/shard_map/ppermute | solution.py:24
  117.9 0.1 collective-permute-start.3
  118.0 6.7 %all-to-all-done.2.parts_ref = f32[32,8,256]{2,1,0:T(8,128)S(1)} async-done(((f32[32,8,256]{2,1,0:T(8,128)}), f32[32,8,256]{2,1,0:T(8,128)S(1)}, u32[]{:S(2)}, u32[]{:S(2)}) %all-to-all-start.2) | async-done | bytes 262176 | tf_op jit(solution)/shard_map/all_to_all | solution.py:277
  124.7 0.9 shard_map.55
  125.6 8.9 %all-to-all-start.3 = ((f32[128,8,128]{2,1,0:T(8,128)}), f32[128,8,128]{2,1,0:T(8,128)S(1)}, u32[]{:S(2)}, u32[]{:S(2)}) async-start(f32[128,8,128]{2,1,0:T(8,128)} %shard_map.55), calls=%async_computation.3 | async-start | bytes 1048576 | tf_op jit(solution)/shard_map/all_to_all | solution.py:288
  134.5 0.0 collective-permute-done.1
  134.5 0.0 collective-permute-done.2
  134.5 0.0 collective-permute-done.3
  134.6 0.9 collective-permute-start.4
  135.4 2.4 %collective-permute-start.5 = (f32[64,768]{1,0:T(8,128)S(1)}, f32[64,768]{1,0:T(8,128)S(1)}, u32[]{:S(2)}, u32[]{:S(2)}) collective-permute-start(f32[64,768]{1,0:T(8,128)S(1)} %pad_maximum_fusion), channel_id=1, source_target_pairs={{0,128},{8,136},{1,129},{9,137},{16,144},{24,152},{17,145},{25,153... | collective-permute-start | bytes 589832 | tf_op jit(solution)/shard_map/ppermute | solution.py:24
  137.8 1.2 collective-permute-start.6
  139.0 5.6 %collective-permute-done.4 = f32[64,768]{1,0:T(8,128)S(1)} collective-permute-done((f32[64,768]{1,0:T(8,128)S(1)}, f32[64,768]{1,0:T(8,128)S(1)}, u32[]{:S(2)}, u32[]{:S(2)}) %collective-permute-start.4) | collective-permute-done | bytes 196640 | tf_op jit(solution)/shard_map/ppermute | solution.py:24
  144.7 6.7 %collective-permute-done.5 = f32[64,768]{1,0:T(8,128)S(1)} collective-permute-done((f32[64,768]{1,0:T(8,128)S(1)}, f32[64,768]{1,0:T(8,128)S(1)}, u32[]{:S(2)}, u32[]{:S(2)}) %collective-permute-start.5) | collective-permute-done | bytes 196640 | tf_op jit(solution)/shard_map/ppermute | solution.py:24
  151.4 0.0 collective-permute-done.6
  151.5 1.4 collective-permute-start.7
  152.8 1.5 all-to-all-done.3.mine_ref
  154.4 1.7 %collective-permute-start.15 = (f32[128,8,128]{2,1,0:T(8,128)S(1)}, f32[128,8,128]{2,1,0:T(8,128)S(1)}, u32[]{:S(2)}, u32[]{:S(2)}) collective-permute-start(f32[128,8,128]{2,1,0:T(8,128)S(1)} %all-to-all-done.3.mine_ref), channel_id=1, source_target_pairs={{0,8},{8,0},{1,9},{9,1},{16,24},{24,16},{17,25},{25,17},{32,40},{4... | collective-permute-start | bytes 1572872 | tf_op jit(solution)/shard_map/ppermute | solution.py:24
  156.1 1.5 collective-permute-done.15.theirs_ref
  157.6 1.7 %shard_map.56 = f32[768,256]{1,0:T(8,128)} custom-call(s32[5]{0:T(128)S(1)} %stack.23.place_ref, f32[128,8,128]{2,1,0:T(8,128)S(1)} %all-to-all-done.3.mine_ref, f32[128,8,128]{2,1,0:T(8,128)S(1)} %collective-permute-done.15.theirs_ref), custom_call_target="tpu_custom_call" | custom-call | bytes 2097192 | tf_op jit(solution)/shard_map/pallas_call | solution.py:51
  159.3 1.8 %shard_map.53 = f32[512,768]{1,0:T(8,128)} custom-call(s32[5]{0:T(128)S(1)} %stack.23.place_ref, f32[256,768]{1,0:T(8,128)S(1)} %constant_dynamic-update-slice_fusion.mine_ref, f32[256,768]{1,0:T(8,128)S(1)} %collective-permute-done.7.theirs_ref), custom_call_target="tpu_custom_call" | custom-call | bytes 3145768 | tf_op jit(solution)/shard_map/pallas_call | solution.py:51
  (26 shorter events, 0.1 us)
Async XLA Ops:
  0.6 1.1 copy-start.1
  1.8 1.4 copy-start.3
  3.2 15.1 %copy-start.2 = (bf16[512,768]{1,0:T(8,128)(2,1)S(1)}, bf16[512,768]{1,0:T(8,128)(2,1)}, u32[]{:S(2)}) copy-start(bf16[512,768]{1,0:T(8,128)(2,1)} %cent_ref.1) | copy-start | bytes 2359300
  5.3 1.4 copy-start
  6.6 20.8 %all-to-all-start = ((f32[8,16,128]{2,1,0:T(8,128)}), f32[8,16,128]{2,1,0:T(8,128)S(1)}, u32[]{:S(2)}, u32[]{:S(2)}) async-start(f32[8,16,128]{2,1,0:T(8,128)} %get-tuple-element.17.mine_ref), calls=%async_computation | async-start | bytes 131072 | tf_op jit(solution)/shard_map/all_to_all | solution.py:229
  30.6 0.8 copy-start.5
  31.3 0.8 copy-start.7
  32.1 0.7 copy-start.9
  32.1 0.9 copy-start.10
  32.9 1.4 copy-start.4
  35.9 4.3 %collective-permute-start = (f32[256,896]{1,0:T(8,128)S(1)}, f32[256,896]{1,0:T(8,128)S(1)}, u32[]{:S(2)}, u32[]{:S(2)}) collective-permute-start(f32[256,896]{1,0:T(8,128)S(1)} %get-tuple-element.21), channel_id=1, source_target_pairs={{0,8},{8,0},{1,9},{9,1},{16,24},{24,16},{17,25},{25,17},{32,40},{4... | collective-permute-start | bytes 2752520 | tf_op jit(solution)/shard_map/ppermute | solution.py:24
  41.2 8.4 %copy-start.8 = (f32[96,1024]{1,0:T(8,128)S(1)}, f32[96,1024]{1,0:T(8,128)}, u32[]{:S(2)}) copy-start(f32[96,1024]{1,0:T(8,128)} %copy-done.7) | copy-start | bytes 1179652
  41.2 8.4 %copy-start.6 = (f32[96,1024]{1,0:T(8,128)S(1)}, f32[96,1024]{1,0:T(8,128)}, u32[]{:S(2)}) copy-start(f32[96,1024]{1,0:T(8,128)} %copy-done.5) | copy-start | bytes 1179652
  41.2 52.5 %all-to-all-start.1 = ((f32[16,16,896]{2,1,0:T(8,128)}), f32[16,16,896]{2,1,0:T(8,128)}, u32[]{:S(2)}, u32[]{:S(2)}) async-start(f32[16,16,896]{2,1,0:T(8,128)} %bitcast.12), calls=%async_computation.1 | async-start | bytes 1835008 | tf_op jit(solution)/shard_map/all_to_all | solution.py:256
  46.9 12.2 %collective-permute-start.11 = (f32[96,1024]{1,0:T(8,128)}, f32[96,1024]{1,0:T(8,128)}, u32[]{:S(2)}, u32[]{:S(2)}) collective-permute-start(f32[96,1024]{1,0:T(8,128)} %copy-done.10), channel_id=1, source_target_pairs={{0,2},{8,10},{1,3},{9,11},{16,18},{24,26},{17,19},{25,27},{32,34},... | collective-permute-start | bytes 1179656 | tf_op jit(solution)/shard_map/ppermute | solution.py:24
  47.2 11.9 %collective-permute-start.12 = (f32[96,1024]{1,0:T(8,128)}, f32[96,1024]{1,0:T(8,128)}, u32[]{:S(2)}, u32[]{:S(2)}) collective-permute-start(f32[96,1024]{1,0:T(8,128)} %copy-done.9), channel_id=1, source_target_pairs={{0,6},{8,14},{1,7},{9,15},{16,22},{24,30},{17,23},{25,31},{32,38},... | collective-permute-start | bytes 1179656 | tf_op jit(solution)/shard_map/ppermute | solution.py:24
  49.6 16.7 %collective-permute-start.13 = (f32[96,1024]{1,0:T(8,128)S(1)}, f32[96,1024]{1,0:T(8,128)}, u32[]{:S(2)}, u32[]{:S(2)}) collective-permute-start(f32[96,1024]{1,0:T(8,128)S(1)} %copy-done.8), channel_id=1, source_target_pairs={{0,4},{8,12},{1,5},{9,13},{16,20},{24,28},{17,21},{25,29},{32,36},... | collective-permute-start | bytes 1179656 | tf_op jit(solution)/shard_map/ppermute | solution.py:24
  49.6 25.1 %collective-permute-start.10 = (f32[96,1024]{1,0:T(8,128)S(1)}, f32[96,1024]{1,0:T(8,128)}, u32[]{:S(2)}, u32[]{:S(2)}) collective-permute-start(f32[96,1024]{1,0:T(8,128)S(1)} %copy-done.6), channel_id=1, source_target_pairs={{0,4},{8,12},{1,5},{9,13},{16,20},{24,28},{17,21},{25,29},{32,36},... | collective-permute-start | bytes 1179656 | tf_op jit(solution)/shard_map/ppermute | solution.py:24
  52.6 31.2 %collective-permute-start.8 = (f32[96,1024]{1,0:T(8,128)S(1)}, f32[96,1024]{1,0:T(8,128)}, u32[]{:S(2)}, u32[]{:S(2)}) collective-permute-start(f32[96,1024]{1,0:T(8,128)S(1)} %get-tuple-element.23), channel_id=1, source_target_pairs={{0,2},{8,10},{1,3},{9,11},{16,18},{24,26},{17,19},{25,27},{32,34},... | collective-permute-start | bytes 1179656 | tf_op jit(solution)/shard_map/ppermute | solution.py:24
  59.1 24.7 %collective-permute-start.9 = (f32[96,1024]{1,0:T(8,128)S(1)}, f32[96,1024]{1,0:T(8,128)}, u32[]{:S(2)}, u32[]{:S(2)}) collective-permute-start(f32[96,1024]{1,0:T(8,128)S(1)} %get-tuple-element.24), channel_id=1, source_target_pairs={{0,6},{8,14},{1,7},{9,15},{16,22},{24,30},{17,23},{25,31},{32,38},... | collective-permute-start | bytes 1179656 | tf_op jit(solution)/shard_map/ppermute | solution.py:24
  68.4 15.4 %collective-permute-start.14 = (f32[96,1024]{1,0:T(8,128)}, f32[96,1024]{1,0:T(8,128)S(1)}, u32[]{:S(2)}, u32[]{:S(2)}) collective-permute-start(f32[96,1024]{1,0:T(8,128)} %add_add_fusion), channel_id=1, source_target_pairs={{0,1},{8,9},{1,0},{9,8},{16,17},{24,25},{17,16},{25,24},{32,33},{4... | collective-permute-start | bytes 1179656 | tf_op jit(solution)/shard_map/ppermute | solution.py:24
  93.7 24.3 %copy-start.11 = (f32[96,8,256]{2,1,0:T(8,128)S(1)}, f32[96,8,256]{2,1,0:T(8,128)}, u32[]{:S(2)}) copy-start(f32[96,8,256]{2,1,0:T(8,128)} %param.5) | copy-start | bytes 2359300
  93.7 31.0 %all-to-all-start.2 = ((f32[32,8,256]{2,1,0:T(8,128)}), f32[32,8,256]{2,1,0:T(8,128)S(1)}, u32[]{:S(2)}, u32[]{:S(2)}) async-start(f32[32,8,256]{2,1,0:T(8,128)} %shard_map.54), calls=%async_computation.2 | async-start | bytes 524288 | tf_op jit(solution)/shard_map/all_to_all | solution.py:277
  114.3 20.2 %collective-permute-start.1 = (f32[16,768]{1,0:T(8,128)S(1)}, f32[16,768]{1,0:T(8,128)S(1)}, u32[]{:S(2)}, u32[]{:S(2)}) collective-permute-start(f32[16,768]{1,0:T(8,128)S(1)} %get-tuple-element.31), channel_id=1, source_target_pairs={{0,16},{8,24},{1,17},{9,25},{16,0},{24,8},{17,1},{25,9},{32,48},{4... | collective-permute-start | bytes 147464 | tf_op jit(solution)/shard_map/ppermute | solution.py:24
  115.8 18.7 %collective-permute-start.2 = (f32[16,768]{1,0:T(8,128)S(1)}, f32[16,768]{1,0:T(8,128)S(1)}, u32[]{:S(2)}, u32[]{:S(2)}) collective-permute-start(f32[16,768]{1,0:T(8,128)S(1)} %get-tuple-element.31), channel_id=1, source_target_pairs={{0,32},{8,40},{1,33},{9,41},{16,48},{24,56},{17,49},{25,57},{32,0}... | collective-permute-start | bytes 147464 | tf_op jit(solution)/shard_map/ppermute | solution.py:24
  117.9 16.6 %collective-permute-start.3 = (f32[16,768]{1,0:T(8,128)S(1)}, f32[16,768]{1,0:T(8,128)S(1)}, u32[]{:S(2)}, u32[]{:S(2)}) collective-permute-start(f32[16,768]{1,0:T(8,128)S(1)} %get-tuple-element.31), channel_id=1, source_target_pairs={{0,48},{8,56},{1,49},{9,57},{16,32},{24,40},{17,33},{25,41},{32,16... | collective-permute-start | bytes 147464 | tf_op jit(solution)/shard_map/ppermute | solution.py:24
  125.6 28.8 %all-to-all-start.3 = ((f32[128,8,128]{2,1,0:T(8,128)}), f32[128,8,128]{2,1,0:T(8,128)S(1)}, u32[]{:S(2)}, u32[]{:S(2)}) async-start(f32[128,8,128]{2,1,0:T(8,128)} %shard_map.55), calls=%async_computation.3 | async-start | bytes 1048576 | tf_op jit(solution)/shard_map/all_to_all | solution.py:288
  134.6 10.1 %collective-permute-start.4 = (f32[64,768]{1,0:T(8,128)S(1)}, f32[64,768]{1,0:T(8,128)S(1)}, u32[]{:S(2)}, u32[]{:S(2)}) collective-permute-start(f32[64,768]{1,0:T(8,128)S(1)} %pad_maximum_fusion), channel_id=1, source_target_pairs={{0,64},{8,72},{1,65},{9,73},{16,80},{24,88},{17,81},{25,89},{32,96... | collective-permute-start | bytes 589832 | tf_op jit(solution)/shard_map/ppermute | solution.py:24
  135.4 16.0 %collective-permute-start.5 = (f32[64,768]{1,0:T(8,128)S(1)}, f32[64,768]{1,0:T(8,128)S(1)}, u32[]{:S(2)}, u32[]{:S(2)}) collective-permute-start(f32[64,768]{1,0:T(8,128)S(1)} %pad_maximum_fusion), channel_id=1, source_target_pairs={{0,128},{8,136},{1,129},{9,137},{16,144},{24,152},{17,145},{25,153... | collective-permute-start | bytes 589832 | tf_op jit(solution)/shard_map/ppermute | solution.py:24
  137.8 13.6 %collective-permute-start.6 = (f32[64,768]{1,0:T(8,128)S(1)}, f32[64,768]{1,0:T(8,128)S(1)}, u32[]{:S(2)}, u32[]{:S(2)}) collective-permute-start(f32[64,768]{1,0:T(8,128)S(1)} %pad_maximum_fusion), channel_id=1, source_target_pairs={{0,192},{8,200},{1,193},{9,201},{16,208},{24,216},{17,209},{25,217... | collective-permute-start | bytes 589832 | tf_op jit(solution)/shard_map/ppermute | solution.py:24
  151.5 7.8 %collective-permute-start.7 = (f32[256,768]{1,0:T(8,128)S(1)}, f32[256,768]{1,0:T(8,128)S(1)}, u32[]{:S(2)}, u32[]{:S(2)}) collective-permute-start(f32[256,768]{1,0:T(8,128)S(1)} %constant_dynamic-update-slice_fusion.mine_ref), channel_id=1, source_target_pairs={{0,8},{8,0},{1,9},{9,1},{16,24},{24,16},{17,25},{25,17},{32,40},{4... | collective-permute-start | bytes 2359304 | tf_op jit(solution)/shard_map/ppermute | solution.py:24
  154.4 3.2 %collective-permute-start.15 = (f32[128,8,128]{2,1,0:T(8,128)S(1)}, f32[128,8,128]{2,1,0:T(8,128)S(1)}, u32[]{:S(2)}, u32[]{:S(2)}) collective-permute-start(f32[128,8,128]{2,1,0:T(8,128)S(1)} %all-to-all-done.3.mine_ref), channel_id=1, source_target_pairs={{0,8},{8,0},{1,9},{9,1},{16,24},{24,16},{17,25},{25,17},{32,40},{4... | collective-permute-start | bytes 1572872 | tf_op jit(solution)/shard_map/ppermute | solution.py:24

commit v2 on v1

--- a/solution.py
+++ b/solution.py
@@ -25,7 +25,7 @@
 
 
 def along_x(k):
-    return lambda x, y, zl, zh, c: ((x + k) % NX, y, zl, zh, c)
+    return lambda x, y, zl, zh, c: (x ^ k, y, zl, zh, c)
 
 
 def along_y(k):
@@ -44,10 +44,11 @@
     return (x, y, zl, zh, 1 - c)
 
 
-def call(kernel, out, args, smem=0, scratch=(), flops=0, limit=48):
+def call(kernel, out, args, smem=0, scratch=(), flops=0, limit=12, hbm_in=0):
     nbytes = sum(a.size * a.dtype.itemsize for a in args)
     specs = [pl.BlockSpec(memory_space=pltpu.SMEM)] * smem
-    specs += [pl.BlockSpec(memory_space=pltpu.VMEM)] * (len(args) - smem)
+    specs += [pl.BlockSpec(memory_space=pl.ANY)] * hbm_in
+    specs += [pl.BlockSpec(memory_space=pltpu.VMEM)] * (len(args) - smem - hbm_in)
     return pl.pallas_call(
         kernel,
         out_shape=out,
@@ -67,15 +68,39 @@
     return lax.dot_general(a, b, (((ca,), (cb,)), ((), ())), preferred_element_type=F32)
 
 
-def logits_kernel(emb_ref, cent_ref, p_ref, stat_ref):
+def relative_blocks(place_ref):
+    x, zl, c = place_ref[0], place_ref[2], place_ref[4]
+    spots = []
+    for kc, kx, kz in itertools.product(range(NC), range(NX), range(NZL)):
+        spot = (lax.bitwise_xor(c, kc) * NX + lax.bitwise_xor(x, kx)) * NZL + lax.bitwise_xor(zl, kz)
+        spots.append(spot)
+    return spots
+
+
+def logits_kernel(place_ref, emb_ref, cent_ref, p_ref, stat_ref, held_ref, emb_buf, sems):
     rows, width = emb_ref.shape
-    cent = cent_ref[...]
+    step = 256
+    spots = relative_blocks(place_ref)
+    size = cent_ref.shape[0] // len(spots)
+    copies = []
+    for i, spot in enumerate(spots):
+        source = cent_ref.at[pl.ds(pl.multiple_of(spot * size, 16), size), :]
+        copies.append(pltpu.make_async_copy(source, held_ref.at[i * size : (i + 1) * size, :], sems.at[i]))
+    for i in range(rows // step):
+        at = slice(i * step, (i + 1) * step)
+        copies.append(pltpu.make_async_copy(emb_ref.at[at, :], emb_buf.at[at, :], sems.at[len(spots) + i]))
+    for copy in copies:
+        copy.start()
+    for copy in copies[: len(spots)]:
+        copy.wait()
+    cent = held_ref[...]
     cent_f = cent.astype(F32)
     half_sq = 0.5 * jnp.sum(cent_f * cent_f, axis=1, keepdims=True)
-    step = 256
     tops, sums = [], []
-    for start in range(0, rows, step):
-        cross = dot(cent, emb_ref[start : start + step, :], 1, 1)
+    for i in range(rows // step):
+        start = i * step
+        copies[len(spots) + i].wait()
+        cross = dot(cent, emb_buf[start : start + step, :], 1, 1)
         logits = (cross - half_sq) * (3.0 / math.sqrt(width))
         top = jnp.max(logits, axis=0, keepdims=True)
         p = jnp.exp(logits - top)
@@ -113,13 +138,32 @@
             out_refs[part * NY + k][...] = dot(piece, wb_ref[...], 1, 0)
 
 
-def mass_kernel(place_ref, wb_ref, count_ref, emb_ref, keep_ref, send_ref):
-    c = place_ref[4]
+def mass_kernel(place_ref, wb_ref, count_ref, emb_ref, keep_ref, send_ref, emb_t_ref, turned_ref):
     half, width = keep_ref.shape[0], emb_ref.shape[1]
-    for ref, side in ((keep_ref, c), (send_ref, 1 - c)):
-        here = pl.ds(pl.multiple_of(side * half, 16), half)
-        ref[:, :width] = dot(wb_ref[here, :], emb_ref[...], 1, 0)
-        ref[:, width:] = count_ref[here, :]
+    for ref, start in ((send_ref, half), (keep_ref, 0)):
+        ref[:, :width] = dot(wb_ref[start : start + half, :], emb_ref[...], 1, 0)
+        ref[:, width:] = count_ref[start : start + half, :]
+    share = emb_t_ref.shape[0]
+    turned_ref[...] = emb_ref[...].T
+    first = (place_ref[1] * NZH + place_ref[3]) * share
+    emb_t_ref[...] = turned_ref[pl.ds(pl.multiple_of(first, 16), share), :].astype(F32)
+
+
+def halve_kernel(mine_ref, got_ref, keep_ref, send_ref):
+    half = keep_ref.shape[0]
+    keep_ref[...] = mine_ref[:half, :] + got_ref[:half, :]
+    send_ref[...] = mine_ref[half:, :] + got_ref[half:, :]
+
+
+def centroid_kernel(mine_ref, got_ref, old_ref, out_ref):
+    rows, width = out_ref.shape
+    total = mine_ref[...] + got_ref[...]
+    old = old_ref[:rows, :].astype(F32)
+    out_ref[...] = (total[:, :width] + old) / (total[:, width : width + 1] + 1.0)
+
+
+def add_kernel(a_ref, b_ref, c_ref, d_ref, out_ref):
+    out_ref[...] = (a_ref[...] + b_ref[...]) + (c_ref[...] + d_ref[...])
 
 
 def pieces(v):
@@ -129,8 +173,14 @@
     return hi, mid, rest - mid
 
 
-def codebook_kernel(emb_t_ref, a_ref, b_ref, c_ref, d_ref, e_ref, books_ref, out_ref):
+def codebook_kernel(
+    place_ref, all_books_ref, emb_t_ref, a_ref, b_ref, c_ref, d_ref, e_ref, out_ref, books_ref, sem
+):
     subspaces, depth, codes = books_ref.shape
+    first = (place_ref[1] * NZH + place_ref[3]) * subspaces
+    copy = pltpu.make_async_copy(all_books_ref.at[pl.ds(first, subspaces)], books_ref, sem)
+    copy.start()
+    copy.wait()
     rows = emb_t_ref.shape[1]
     ones = jnp.where(lax.broadcasted_iota(jnp.int32, (2 * depth, rows), 0) < 3, 1.0, 0.0)
     for m in range(subspaces):
@@ -167,9 +217,17 @@
             out_ref[row, slot + 3 : slot + 4, :] = count
 
 
-def update_kernel(parts_ref, book_ref, out_ref):
+def update_kernel(place_ref, all_books_ref, parts_ref, out_ref, books_ref, sem):
+    x, y, zl, zh, c = (place_ref[i] for i in range(5))
+    share = books_ref.shape[0]
+    first = pl.multiple_of((y * NZH + zh) * share, 8)
+    copy = pltpu.make_async_copy(all_books_ref.at[pl.ds(first, share), :], books_ref, sem)
+    copy.start()
     total = jnp.sum(parts_ref[...], axis=0)
-    new = (total[:3] + book_ref[:3]) / (total[3:6] + 1.0)
+    copy.wait()
+    row = ((c * NX + x) * NZL + zl) * 3
+    old = jnp.concatenate([books_ref[pl.ds(row + i, 1), :] for i in range(3)], axis=0)
+    new = (total[:3] + old) / (total[3:6] + 1.0)
     tile = jnp.concatenate([new[:, :128], new[:, 128:], jnp.zeros((2, 128), F32)], axis=0)
     for i in range(out_ref.shape[0]):
         out_ref[i] = tile
@@ -198,14 +256,13 @@
 
 
 def centroids_kernel(place_ref, mine_ref, theirs_ref, out_ref):
-    x, zl, c = place_ref[0], place_ref[2], place_ref[4]
-    rows = mine_ref.shape[0] // (NX * NZL)
-    for ref, side in ((mine_ref, c), (theirs_ref, 1 - c)):
-        for kx in range(NX):
-            for kz in range(NZL):
-                spot = (side * NX + (x + NX - kx) % NX) * NZL + lax.bitwise_xor(zl, kz)
-                at = (kx * NZL + kz) * rows
-                out_ref[pl.ds(pl.multiple_of(spot * rows, 8), rows), :] = ref[at : at + rows, :]
+    spots = relative_blocks(place_ref)
+    half = len(spots) // 2
+    size = mine_ref.shape[0] // half
+    for i, spot in enumerate(spots):
+        ref = mine_ref if i < half else theirs_ref
+        at = (i % half) * size
+        out_ref[pl.ds(pl.multiple_of(spot * size, 8), size), :] = ref[at : at + size, :]
 
 
 def body(embeddings, centroids, codebooks):
@@ -220,17 +277,25 @@
     cents = NY * NZH
     share = width // cents
 
-    p, stat = call(
+    p, stat, ordered = call(
         logits_kernel,
-        (shape((held, rows_here)), shape((cents, 2 * rows_here // 128, 128))),
-        (embeddings, centroids),
+        (
+            shape((held, rows_here)),
+            shape((cents, 2 * rows_here // 128, 128)),
+            shape((held, width), BF16),
+        ),
+        (place, embeddings, centroids),
+        smem=1,
+        hbm_in=2,
+        scratch=(pltpu.VMEM((rows_here, width), BF16), pltpu.SemaphoreType.DMA((64,))),
+        limit=60,
         flops=2 * rows_here * held * width,
     )
     stats = lax.all_to_all(stat, "cent", 0, 0, tiled=True)
     outs = call(
         weights_kernel,
         (shape((held, rows_here), BF16), shape((held, 128))) + (shape((share, rows_here)),) * 8,
-        (place, p, stat, stats, centroids.T),
+        (place, p, stat, stats, ordered.T),
         smem=1,
         flops=2 * rows_here * held * width,
     )
@@ -238,48 +303,50 @@
     steps = (1, -1, 2)
     got = [hop(theirs[k % NY], along_y(k)) for k in steps]
     got_mine = [hop(mine[k % NY], along_y(k)) for k in steps]
-    peer = hop(theirs[0] + got[0] + got[1] + got[2], other_zh)
-
-    keep, send = call(
+    peer = hop(call(add_kernel, shape((share, rows_here)), (theirs[0], *got)), other_zh)
+
+    keep, send, emb_t = call(
         mass_kernel,
-        (shape((held // 2, width + 128)),) * 2,
+        (shape((held // 2, width + 128)),) * 2 + (shape((share, rows_here)),),
         (place, wb, counts, embeddings),
         smem=1,
+        scratch=(pltpu.VMEM((width, rows_here), BF16),),
         flops=2 * rows_here * held * width,
     )
-    mass = keep + hop(send, other_core)
-    groups = [
-        [(xx * NZL + zz) * NC + cc for xx in range(NX) for zz in range(NZL)] for cc in range(NC)
-    ]
+    for move in (other_core, along_x(2), along_x(1), along_zl(2)):
+        half = keep.shape[0] // 2
+        keep, send = call(
+            halve_kernel, (shape((half, width + 128)),) * 2, (keep, hop(send, move)), limit=4
+        )
+    new = call(
+        centroid_kernel, shape((half, width)), (keep, hop(send, along_zl(1)), ordered), limit=4
+    )
     peers = NX * NZL
-    piece_rows = held // (2 * peers)
-    parts = lax.all_to_all(
-        mass.reshape(peers, piece_rows, width + 128), "rows", 0, 0, tiled=True, axis_index_groups=groups
-    )
-    total = jnp.sum(parts, axis=0)
-    first = c * (held // 2) + (x * NZL + zl) * piece_rows
-    old = lax.dynamic_slice_in_dim(centroids, first, piece_rows, 0).astype(F32)
-    new = (total[:, :width] + old) / (total[:, width : width + 1] + 1.0)
-
-    emb_t = lax.dynamic_slice_in_dim(embeddings, cent_at * share, share, 1).T.astype(F32)
+
     per = subspaces // cents
-    my_books = lax.dynamic_slice_in_dim(codebooks, cent_at * per, per, 0)
     sums = call(
         codebook_kernel,
         shape((NX * NZL * NC, 8, codes)),
-        (emb_t, mine[0], *got_mine, peer, my_books),
-        flops=4 * rows_here * per * codes * 64,
+        (place, codebooks, emb_t, mine[0], *got_mine, peer),
+        smem=1,
+        hbm_in=1,
+        scratch=(pltpu.VMEM((per, depth, codes), F32), pltpu.SemaphoreType.DMA),
+        flops=64 * rows_here * per * codes * 64,
     )
     new_z = jnp.concatenate([new] + [hop(new, along_zl(k)) for k in (1, 2, 3)], axis=0)
-    owner = c * peers + x * NZL + zl
-    flat_books = jnp.pad(codebooks.reshape(subspaces * depth, codes), ((0, 8), (0, 0)))
-    my_rows = lax.dynamic_slice_in_dim(flat_books, (cent_at * NC * peers + owner) * 3, 8, 0)
     all_parts = lax.all_to_all(sums, "rows", 0, 0, tiled=True)
     same_core = [
         [flat(xx, yy, zz, hh, cc) for yy in range(NY) for hh in range(NZH) for xx in range(NX) for zz in range(NZL)]
         for cc in range(NC)
     ]
-    tile = call(update_kernel, shape((cents * peers, 8, 128)), (all_parts, my_rows))
+    tile = call(
+        update_kernel,
+        shape((cents * peers, 8, 128)),
+        (place, codebooks.reshape(subspaces * depth, codes), all_parts),
+        smem=1,
+        hbm_in=1,
+        scratch=(pltpu.VMEM((share, codes), F32), pltpu.SemaphoreType.DMA),
+    )
     new_x = jnp.concatenate([new_z] + [hop(new_z, along_x(k)) for k in (1, 2, 3)], axis=0)
     new_other = hop(new_x, other_core)
     new_centroids = call(

time: 162 us -> 164 us (1.012)
  waiting for transfers between devices: 59.3 us -> 68.7 us
  local copies, waits for them, and re-layouts: 10.3 us -> 5.18 us
  other arithmetic: 4.56 us -> 0.02 us
  Pallas kernels: 21.1 us -> 25.6 us
    ppermute x16 -> x20, waiting for transfers between devices: 42.4 us -> 61 us  [hop(): return lax.ppermute(value, BOTH, pairs)]
    ppermute x16 -> x20, starting transfers between devices: 19.6 us -> 26.5 us  [hop(): return lax.ppermute(value, BOTH, pairs)]
    all_to_all x1, waiting for transfers between devices: 6.73 us -> 0.01 us  [body(): all_parts = lax.all_to_all(sums, 'rows', 0, 0, tiled=True)]
    all_to_all x1, starting transfers between devices: 19.1 us -> 12.7 us  [body(): all_parts = lax.all_to_all(sums, 'rows', 0, 0, tiled=True)]
    all_to_all x1 -> x0, starting transfers between devices: 5.68 us -> none  [body(): lax.all_to_all(mass.reshape(peers, piece_rows, width + 128), 'rows', 0, 0...]
    unnamed x31 -> x18, local copies, waits for them, and re-layouts: 8.14 us -> 3.07 us
    pallas_call x7 -> x13, Pallas kernels: 21.1 us -> 25.6 us  [call(): pl.pallas_call(kernel, out_shape=out, in_specs=specs, out_specs=jax.tree....]
    all_to_all x1, starting transfers between devices: 8.89 us -> 12.4 us  [body(): lax.all_to_all(tile, BOTH, 0, 0, tiled=True, axis_index_groups=same_core)]
  transfers between devices with their start and end apart: 20 -> 23, of which waited for: 11 -> 10; matrix products, arithmetic and copies ran while one was open for 4% -> 1% of each run, Pallas kernels for 8% -> 8%
where the time goes in v2:
time: 164 us
  waiting for transfers between devices  68.7 us (42%)
  starting transfers between devices  63.4 us (39%)
  Pallas kernels  25.6 us (16%)
  local copies, waits for them, and re-layouts  5.18 us (3%)
    ppermute x20, waiting for transfers between devices, hop(): return lax.ppermute(value, BOTH, pairs)  61 us
    ppermute x20, starting transfers between devices, hop(): return lax.ppermute(value, BOTH, pairs)  26.5 us
    pallas_call x13, Pallas kernels, call(): pl.pallas_call(kernel, out_shape=out, in_specs=specs, out_specs=jax.tree....  25.6 us
    all_to_all x1, starting transfers between devices, body(): all_parts = lax.all_to_all(sums, 'rows', 0, 0, tiled=True)  12.7 us
    all_to_all x1, starting transfers between devices, body(): lax.all_to_all(tile, BOTH, 0, 0, tiled=True, axis_index_groups=same_core)  12.4 us
    all_to_all x1, starting transfers between devices, body(): stats = lax.all_to_all(stat, 'cent', 0, 0, tiled=True)  11.8 us
    all_to_all x1, waiting for transfers between devices, body(): stats = lax.all_to_all(stat, 'cent', 0, 0, tiled=True)  7.69 us
  transfers between devices with their start and end apart: 23, of which 10 were waited for; matrix products, arithmetic and copies ran while one was open for 1% of the time, Pallas kernels for 8%

profile of v2, /device:TPU:1, one launch (start us, length us, event | category | flops | bytes accessed | tf_op | source)
XLA Modules:
  0.0 163.8 jit_solution(3827033599735598234)
XLA Ops:
  0.7 0.7 stack.23.place_ref
  1.4 7.1 %shard_map.50 = (f32[512,1024]{1,0:T(8,128)}, f32[8,16,128]{2,1,0:T(8,128)}, bf16[512,768]{1,0:T(8,128)(2,1)}) custom-call(s32[5]{0:T(128)} %stack.23.place_ref, bf16[1024,768]{1,0:T(8,128)(2,1)} %emb_ref.3, bf16[512,768]{1,0:T(8,128)(2,1)} %cent_ref.1), custom_call_target="tpu_custom_call" | custom-call | flops 805306368 | bytes 4718632 | tf_op jit(solution)/shard_map/pallas_call | solution.py:52
  8.5 0.0 copy-start.3
  8.5 11.8 %all-to-all-start = ((f32[8,16,128]{2,1,0:T(8,128)}), f32[8,16,128]{2,1,0:T(8,128)S(1)}, u32[]{:S(2)}, u32[]{:S(2)}) async-start(f32[8,16,128]{2,1,0:T(8,128)} %get-tuple-element.27.mine_ref), calls=%async_computation | async-start | bytes 131072 | tf_op jit(solution)/shard_map/all_to_all | solution.py:294
  20.3 1.4 copy.5
  21.7 7.7 %all-to-all-done.stat_ref = f32[8,16,128]{2,1,0:T(8,128)S(1)} async-done(((f32[8,16,128]{2,1,0:T(8,128)}), f32[8,16,128]{2,1,0:T(8,128)S(1)}, u32[]{:S(2)}, u32[]{:S(2)}) %all-to-all-start) | async-done | bytes 65568 | tf_op jit(solution)/shard_map/all_to_all | solution.py:294
  29.4 0.0 copy-done.4
  29.4 1.6 copy-done.1
  31.0 2.1 %shard_map.51 = (bf16[512,1024]{1,0:T(8,128)(2,1)S(1)}, f32[512,128]{1,0:T(8,128)S(1)}, f32[96,1024]{1,0:T(8,128)S(1)}, f32[96,1024]{1,0:T(8,128)S(1)}, f32[96,1...) custom-call(s32[5]{0:T(128)S(1)} %copy-done.4, ...), custom_call_target="tpu_custom_call" | custom-call | flops 805306368 | bytes 6029352 | tf_op jit(solution)/shard_map/pallas_call | solution.py:52
  33.1 1.4 copy-done.5
  34.5 1.6 shard_map.52
  36.1 2.2 %collective-permute-start = (f32[256,896]{1,0:T(8,128)S(1)}, f32[256,896]{1,0:T(8,128)S(1)}, u32[]{:S(2)}, u32[]{:S(2)}) collective-permute-start(f32[256,896]{1,0:T(8,128)S(1)} %get-tuple-element.32), channel_id=1, source_target_pairs={{0,8},{8,0},{1,9},{9,1},{16,24},{24,16},{17,25},{25,17},{32,40},{4... | collective-permute-start | bytes 2752520 | tf_op jit(solution)/shard_map/ppermute | solution.py:24
  38.3 0.3 collective-permute-start.15
  38.6 2.4 %collective-permute-start.16 = (f32[96,1024]{1,0:T(8,128)S(1)}, f32[96,1024]{1,0:T(8,128)S(1)}, u32[]{:S(2)}, u32[]{:S(2)}) collective-permute-start(f32[96,1024]{1,0:T(8,128)S(1)} %get-tuple-element.48), channel_id=1, source_target_pairs={{0,6},{8,14},{1,7},{9,15},{16,22},{24,30},{17,23},{25,31},{32,38},... | collective-permute-start | bytes 1179656 | tf_op jit(solution)/shard_map/ppermute | solution.py:24
  41.0 0.0 collective-permute-start.17
  41.0 0.6 collective-permute-start.12
  41.6 16.7 %collective-permute-done.15.b_ref = f32[96,1024]{1,0:T(8,128)S(1)} collective-permute-done((f32[96,1024]{1,0:T(8,128)S(1)}, f32[96,1024]{1,0:T(8,128)S(1)}, u32[]{:S(2)}, u32[]{:S(2)}) %collective-permute-start.15) | collective-permute-done | bytes 393248 | tf_op jit(solution)/shard_map/ppermute | solution.py:24
  58.2 0.0 collective-permute-start.13
  58.2 0.0 collective-permute-done.16.c_ref
  58.2 0.0 collective-permute-start.14
  58.3 0.0 collective-permute-done.17.d_ref
  58.3 0.0 copy-start.2
  58.3 0.1 shard_map.59
  58.4 0.6 collective-permute-start.18
  58.9 0.0 collective-permute-done.got_ref
  58.9 0.1 shard_map.53
  59.0 3.0 %collective-permute-start.1 = (f32[128,896]{1,0:T(8,128)S(1)}, f32[128,896]{1,0:T(8,128)S(1)}, u32[]{:S(2)}, u32[]{:S(2)}) collective-permute-start(f32[128,896]{1,0:T(8,128)S(1)} %get-tuple-element.34), channel_id=1, source_target_pairs={{0,128},{8,136},{1,129},{9,137},{16,144},{24,152},{17,145},{25,153... | collective-permute-start | bytes 1376264 | tf_op jit(solution)/shard_map/ppermute | solution.py:24
  62.0 5.5 %collective-permute-done.12.b_ref = f32[96,1024]{1,0:T(8,128)S(1)} collective-permute-done((f32[96,1024]{1,0:T(8,128)S(1)}, f32[96,1024]{1,0:T(8,128)S(1)}, u32[]{:S(2)}, u32[]{:S(2)}) %collective-permute-start.12) | collective-permute-done | bytes 393248 | tf_op jit(solution)/shard_map/ppermute | solution.py:24
  67.5 0.0 collective-permute-done.13.c_ref
  67.5 7.4 %collective-permute-done.14.d_ref = f32[96,1024]{1,0:T(8,128)S(1)} collective-permute-done((f32[96,1024]{1,0:T(8,128)S(1)}, f32[96,1024]{1,0:T(8,128)S(1)}, u32[]{:S(2)}, u32[]{:S(2)}) %collective-permute-start.14) | collective-permute-done | bytes 393248 | tf_op jit(solution)/shard_map/ppermute | solution.py:24
  75.0 0.0 collective-permute-done.18.e_ref
  75.0 9.4 %shard_map.60 = f32[32,8,256]{2,1,0:T(8,128)} custom-call(s32[5]{0:T(128)S(1)} %copy-done.4, f32[96,8,256]{2,1,0:T(8,128)S(1)} %copy-done.2, f32[96,1024]{1,0:T(8,128)S(1)} %get-tuple-element.41.emb_t_ref, f32[96,1024]{1,0:T(8,128)S(1)} %get-tuple-element.42.a_ref, f32[96,1024]{1,0:T(8,128)S(1)} %collective-permute-done.12.b_ref, ...), custom_call_target="tpu_custom_call" | custom-call | flops 12884901888 | bytes 6291496 | tf_op jit(solution)/shard_map/pallas_call | solution.py:52
  84.4 12.7 %all-to-all-start.1 = ((f32[32,8,256]{2,1,0:T(8,128)}), f32[32,8,256]{2,1,0:T(8,128)S(1)}, u32[]{:S(2)}, u32[]{:S(2)}) async-start(f32[32,8,256]{2,1,0:T(8,128)} %shard_map.60), calls=%async_computation.1 | async-start | bytes 524288 | tf_op jit(solution)/shard_map/all_to_all | solution.py:337
  97.1 0.0 collective-permute-done.1.got_ref
  97.1 0.1 shard_map.54
  97.2 1.5 collective-permute-start.2
  98.7 8.3 %collective-permute-done.2.got_ref = f32[64,896]{1,0:T(8,128)S(1)} collective-permute-done((f32[64,896]{1,0:T(8,128)S(1)}, f32[64,896]{1,0:T(8,128)S(1)}, u32[]{:S(2)}, u32[]{:S(2)}) %collective-permute-start.2) | collective-permute-done | bytes 229408 | tf_op jit(solution)/shard_map/ppermute | solution.py:24
  107.0 2.4 %collective-permute-start.3 = (f32[32,896]{1,0:T(8,128)S(1)}, f32[32,896]{1,0:T(8,128)S(1)}, u32[]{:S(2)}, u32[]{:S(2)}) collective-permute-start(f32[32,896]{1,0:T(8,128)S(1)} %get-tuple-element.38), channel_id=1, source_target_pairs={{0,32},{8,40},{1,33},{9,41},{16,48},{24,56},{17,49},{25,57},{32,0}... | collective-permute-start | bytes 344072 | tf_op jit(solution)/shard_map/ppermute | solution.py:24
  109.4 4.6 %collective-permute-done.3.got_ref = f32[32,896]{1,0:T(8,128)S(1)} collective-permute-done((f32[32,896]{1,0:T(8,128)S(1)}, f32[32,896]{1,0:T(8,128)S(1)}, u32[]{:S(2)}, u32[]{:S(2)}) %collective-permute-start.3) | collective-permute-done | bytes 114720 | tf_op jit(solution)/shard_map/ppermute | solution.py:24
  114.1 2.0 %collective-permute-start.4 = (f32[16,896]{1,0:T(8,128)S(1)}, f32[16,896]{1,0:T(8,128)S(1)}, u32[]{:S(2)}, u32[]{:S(2)}) collective-permute-start(f32[16,896]{1,0:T(8,128)S(1)} %get-tuple-element.40), channel_id=1, source_target_pairs={{0,16},{8,24},{1,17},{9,25},{16,0},{24,8},{17,1},{25,9},{32,48},{4... | collective-permute-start | bytes 172040 | tf_op jit(solution)/shard_map/ppermute | solution.py:24
  116.0 0.0 all-to-all-done.1.parts_ref
  116.0 1.6 shard_map.61
  117.6 12.4 %all-to-all-start.2 = ((f32[128,8,128]{2,1,0:T(8,128)}), f32[128,8,128]{2,1,0:T(8,128)S(1)}, u32[]{:S(2)}, u32[]{:S(2)}) async-start(f32[128,8,128]{2,1,0:T(8,128)} %shard_map.61), calls=%async_computation.2 | async-start | bytes 1048576 | tf_op jit(solution)/shard_map/all_to_all | solution.py:355
  130.0 0.0 collective-permute-done.4.got_ref
  130.0 0.1 shard_map.57
  130.1 2.4 %collective-permute-start.7 = (f32[16,768]{1,0:T(8,128)S(1)}, f32[16,768]{1,0:T(8,128)S(1)}, u32[]{:S(2)}, u32[]{:S(2)}) collective-permute-start(f32[16,768]{1,0:T(8,128)S(1)} %shard_map.57), channel_id=1, source_target_pairs={{0,48},{8,56},{1,49},{9,57},{16,32},{24,40},{17,33},{25,41},{32,16... | collective-permute-start | bytes 147464 | tf_op jit(solution)/shard_map/ppermute | solution.py:24
  132.5 0.0 collective-permute-start.6
  132.6 1.2 collective-permute-start.5
  133.7 7.2 %collective-permute-done.7 = f32[16,768]{1,0:T(8,128)S(1)} collective-permute-done((f32[16,768]{1,0:T(8,128)S(1)}, f32[16,768]{1,0:T(8,128)S(1)}, u32[]{:S(2)}, u32[]{:S(2)}) %collective-permute-start.7) | collective-permute-done | bytes 49184 | tf_op jit(solution)/shard_map/ppermute | solution.py:24
  141.0 3.8 %collective-permute-done.6 = f32[16,768]{1,0:T(8,128)S(1)} collective-permute-done((f32[16,768]{1,0:T(8,128)S(1)}, f32[16,768]{1,0:T(8,128)S(1)}, u32[]{:S(2)}, u32[]{:S(2)}) %collective-permute-start.6) | collective-permute-done | bytes 49184 | tf_op jit(solution)/shard_map/ppermute | solution.py:24
  144.7 0.0 collective-permute-done.5
  144.7 2.5 %collective-permute-start.10 = (f32[64,768]{1,0:T(8,128)S(1)}, f32[64,768]{1,0:T(8,128)S(1)}, u32[]{:S(2)}, u32[]{:S(2)}) collective-permute-start(f32[64,768]{1,0:T(8,128)S(1)} %pad_maximum_fusion), channel_id=1, source_target_pairs={{0,192},{8,200},{1,193},{9,201},{16,208},{24,216},{17,209},{25,217... | collective-permute-start | bytes 589832 | tf_op jit(solution)/shard_map/ppermute | solution.py:24
  147.3 0.9 collective-permute-start.9
  148.1 0.0 collective-permute-start.8
  148.2 5.7 %collective-permute-done.8 = f32[64,768]{1,0:T(8,128)S(1)} collective-permute-done((f32[64,768]{1,0:T(8,128)S(1)}, f32[64,768]{1,0:T(8,128)S(1)}, u32[]{:S(2)}, u32[]{:S(2)}) %collective-permute-start.8) | collective-permute-done | bytes 196640 | tf_op jit(solution)/shard_map/ppermute | solution.py:24
  153.8 0.0 collective-permute-done.9
  153.9 0.0 collective-permute-done.10
  153.9 4.5 %collective-permute-start.11 = (f32[256,768]{1,0:T(8,128)S(1)}, f32[256,768]{1,0:T(8,128)S(1)}, u32[]{:S(2)}, u32[]{:S(2)}) collective-permute-start(f32[256,768]{1,0:T(8,128)S(1)} %constant_dynamic-update-slice_fusion.mine_ref), channel_id=1, source_target_pairs={{0,8},{8,0},{1,9},{9,1},{16,24},{24,16},{17,25},{25,17},{32,40},{4... | collective-permute-start | bytes 2359304 | tf_op jit(solution)/shard_map/ppermute | solution.py:24
  158.4 0.0 all-to-all-done.2.mine_ref
  158.4 0.1 collective-permute-start.19
  158.5 1.8 %collective-permute-done.11.theirs_ref = f32[256,768]{1,0:T(8,128)S(1)} collective-permute-done((f32[256,768]{1,0:T(8,128)S(1)}, f32[256,768]{1,0:T(8,128)S(1)}, u32[]{:S(2)}, u32[]{:S(2)}) %collective-permute-start.11) | collective-permute-done | bytes 786464 | tf_op jit(solution)/shard_map/ppermute | solution.py:24
  160.3 1.8 %shard_map.58 = f32[512,768]{1,0:T(8,128)} custom-call(s32[5]{0:T(128)S(1)} %copy-done.4, f32[256,768]{1,0:T(8,128)S(1)} %constant_dynamic-update-slice_fusion.mine_ref, f32[256,768]{1,0:T(8,128)S(1)} %collective-permute-done.11.theirs_ref), custom_call_target="tpu_custom_call" | custom-call | bytes 3145768 | tf_op jit(solution)/shard_map/pallas_call | solution.py:52
  162.1 0.0 collective-permute-done.19.theirs_ref
  162.1 1.7 %shard_map.62 = f32[768,256]{1,0:T(8,128)} custom-call(s32[5]{0:T(128)S(1)} %copy-done.4, f32[128,8,128]{2,1,0:T(8,128)S(1)} %all-to-all-done.2.mine_ref, f32[128,8,128]{2,1,0:T(8,128)S(1)} %collective-permute-done.19.theirs_ref), custom_call_target="tpu_custom_call" | custom-call | bytes 2097192 | tf_op jit(solution)/shard_map/pallas_call | solution.py:52
  (17 shorter events, 0.1 us)
Async XLA Ops:
  8.5 20.9 %copy-start.3 = (f32[8,16,128]{2,1,0:T(8,128)S(1)}, f32[8,16,128]{2,1,0:T(8,128)}, u32[]{:S(2)}) copy-start(f32[8,16,128]{2,1,0:T(8,128)} %get-tuple-element.27.mine_ref) | copy-start | bytes 196612
  8.5 20.9 %copy-start.4 = (s32[5]{0:T(128)S(1)}, s32[5]{0:T(128)}, u32[]{:S(2)}) copy-start(s32[5]{0:T(128)} %stack.23.place_ref) | copy-start | bytes 64
  8.5 20.9 %all-to-all-start = ((f32[8,16,128]{2,1,0:T(8,128)}), f32[8,16,128]{2,1,0:T(8,128)S(1)}, u32[]{:S(2)}, u32[]{:S(2)}) async-start(f32[8,16,128]{2,1,0:T(8,128)} %get-tuple-element.27.mine_ref), calls=%async_computation | async-start | bytes 131072 | tf_op jit(solution)/shard_map/all_to_all | solution.py:294
  29.4 1.6 copy-start.1
  33.1 1.4 copy-start.5
  36.1 22.8 %collective-permute-start = (f32[256,896]{1,0:T(8,128)S(1)}, f32[256,896]{1,0:T(8,128)S(1)}, u32[]{:S(2)}, u32[]{:S(2)}) collective-permute-start(f32[256,896]{1,0:T(8,128)S(1)} %get-tuple-element.32), channel_id=1, source_target_pairs={{0,8},{8,0},{1,9},{9,1},{16,24},{24,16},{17,25},{25,17},{32,40},{4... | collective-permute-start | bytes 2752520 | tf_op jit(solution)/shard_map/ppermute | solution.py:24
  38.3 19.9 %collective-permute-start.15 = (f32[96,1024]{1,0:T(8,128)S(1)}, f32[96,1024]{1,0:T(8,128)S(1)}, u32[]{:S(2)}, u32[]{:S(2)}) collective-permute-start(f32[96,1024]{1,0:T(8,128)S(1)} %get-tuple-element.47), channel_id=1, source_target_pairs={{0,2},{8,10},{1,3},{9,11},{16,18},{24,26},{17,19},{25,27},{32,34},... | collective-permute-start | bytes 1179656 | tf_op jit(solution)/shard_map/ppermute | solution.py:24
  38.6 19.6 %collective-permute-start.16 = (f32[96,1024]{1,0:T(8,128)S(1)}, f32[96,1024]{1,0:T(8,128)S(1)}, u32[]{:S(2)}, u32[]{:S(2)}) collective-permute-start(f32[96,1024]{1,0:T(8,128)S(1)} %get-tuple-element.48), channel_id=1, source_target_pairs={{0,6},{8,14},{1,7},{9,15},{16,22},{24,30},{17,23},{25,31},{32,38},... | collective-permute-start | bytes 1179656 | tf_op jit(solution)/shard_map/ppermute | solution.py:24
  41.0 17.3 %collective-permute-start.17 = (f32[96,1024]{1,0:T(8,128)S(1)}, f32[96,1024]{1,0:T(8,128)S(1)}, u32[]{:S(2)}, u32[]{:S(2)}) collective-permute-start(f32[96,1024]{1,0:T(8,128)S(1)} %get-tuple-element.49), channel_id=1, source_target_pairs={{0,4},{8,12},{1,5},{9,13},{16,20},{24,28},{17,21},{25,29},{32,36},... | collective-permute-start | bytes 1179656 | tf_op jit(solution)/shard_map/ppermute | solution.py:24
  41.0 26.5 %collective-permute-start.12 = (f32[96,1024]{1,0:T(8,128)S(1)}, f32[96,1024]{1,0:T(8,128)S(1)}, u32[]{:S(2)}, u32[]{:S(2)}) collective-permute-start(f32[96,1024]{1,0:T(8,128)S(1)} %get-tuple-element.43), channel_id=1, source_target_pairs={{0,2},{8,10},{1,3},{9,11},{16,18},{24,26},{17,19},{25,27},{32,34},... | collective-permute-start | bytes 1179656 | tf_op jit(solution)/shard_map/ppermute | solution.py:24
  58.2 9.3 %collective-permute-start.13 = (f32[96,1024]{1,0:T(8,128)S(1)}, f32[96,1024]{1,0:T(8,128)S(1)}, u32[]{:S(2)}, u32[]{:S(2)}) collective-permute-start(f32[96,1024]{1,0:T(8,128)S(1)} %get-tuple-element.44), channel_id=1, source_target_pairs={{0,6},{8,14},{1,7},{9,15},{16,22},{24,30},{17,23},{25,31},{32,38},... | collective-permute-start | bytes 1179656 | tf_op jit(solution)/shard_map/ppermute | solution.py:24
  58.2 16.7 %collective-permute-start.14 = (f32[96,1024]{1,0:T(8,128)S(1)}, f32[96,1024]{1,0:T(8,128)S(1)}, u32[]{:S(2)}, u32[]{:S(2)}) collective-permute-start(f32[96,1024]{1,0:T(8,128)S(1)} %get-tuple-element.45), channel_id=1, source_target_pairs={{0,4},{8,12},{1,5},{9,13},{16,20},{24,28},{17,21},{25,29},{32,36},... | collective-permute-start | bytes 1179656 | tf_op jit(solution)/shard_map/ppermute | solution.py:24
  58.3 16.7 %copy-start.2 = (f32[96,8,256]{2,1,0:T(8,128)S(1)}, f32[96,8,256]{2,1,0:T(8,128)}, u32[]{:S(2)}) copy-start(f32[96,8,256]{2,1,0:T(8,128)} %all_books_ref.1) | copy-start | bytes 2359300
  58.4 16.6 %collective-permute-start.18 = (f32[96,1024]{1,0:T(8,128)S(1)}, f32[96,1024]{1,0:T(8,128)S(1)}, u32[]{:S(2)}, u32[]{:S(2)}) collective-permute-start(f32[96,1024]{1,0:T(8,128)S(1)} %shard_map.59), channel_id=1, source_target_pairs={{0,1},{8,9},{1,0},{9,8},{16,17},{24,25},{17,16},{25,24},{32,33},{4... | collective-permute-start | bytes 1179656 | tf_op jit(solution)/shard_map/ppermute | solution.py:24
  59.0 38.1 %collective-permute-start.1 = (f32[128,896]{1,0:T(8,128)S(1)}, f32[128,896]{1,0:T(8,128)S(1)}, u32[]{:S(2)}, u32[]{:S(2)}) collective-permute-start(f32[128,896]{1,0:T(8,128)S(1)} %get-tuple-element.34), channel_id=1, source_target_pairs={{0,128},{8,136},{1,129},{9,137},{16,144},{24,152},{17,145},{25,153... | collective-permute-start | bytes 1376264 | tf_op jit(solution)/shard_map/ppermute | solution.py:24
  84.4 31.6 %all-to-all-start.1 = ((f32[32,8,256]{2,1,0:T(8,128)}), f32[32,8,256]{2,1,0:T(8,128)S(1)}, u32[]{:S(2)}, u32[]{:S(2)}) async-start(f32[32,8,256]{2,1,0:T(8,128)} %shard_map.60), calls=%async_computation.1 | async-start | bytes 524288 | tf_op jit(solution)/shard_map/all_to_all | solution.py:337
  97.2 9.7 %collective-permute-start.2 = (f32[64,896]{1,0:T(8,128)S(1)}, f32[64,896]{1,0:T(8,128)S(1)}, u32[]{:S(2)}, u32[]{:S(2)}) collective-permute-start(f32[64,896]{1,0:T(8,128)S(1)} %get-tuple-element.36), channel_id=1, source_target_pairs={{0,64},{8,72},{1,65},{9,73},{16,80},{24,88},{17,81},{25,89},{32,96... | collective-permute-start | bytes 688136 | tf_op jit(solution)/shard_map/ppermute | solution.py:24
  106.9 23.1 %copy-start = (bf16[512,768]{1,0:T(8,128)(2,1)S(1)}, bf16[512,768]{1,0:T(8,128)(2,1)}, u32[]{:S(2)}) copy-start(bf16[512,768]{1,0:T(8,128)(2,1)} %get-tuple-element.28.old_ref) | copy-start | bytes 2359300
  107.0 7.1 %collective-permute-start.3 = (f32[32,896]{1,0:T(8,128)S(1)}, f32[32,896]{1,0:T(8,128)S(1)}, u32[]{:S(2)}, u32[]{:S(2)}) collective-permute-start(f32[32,896]{1,0:T(8,128)S(1)} %get-tuple-element.38), channel_id=1, source_target_pairs={{0,32},{8,40},{1,33},{9,41},{16,48},{24,56},{17,49},{25,57},{32,0}... | collective-permute-start | bytes 344072 | tf_op jit(solution)/shard_map/ppermute | solution.py:24
  114.1 16.0 %collective-permute-start.4 = (f32[16,896]{1,0:T(8,128)S(1)}, f32[16,896]{1,0:T(8,128)S(1)}, u32[]{:S(2)}, u32[]{:S(2)}) collective-permute-start(f32[16,896]{1,0:T(8,128)S(1)} %get-tuple-element.40), channel_id=1, source_target_pairs={{0,16},{8,24},{1,17},{9,25},{16,0},{24,8},{17,1},{25,9},{32,48},{4... | collective-permute-start | bytes 172040 | tf_op jit(solution)/shard_map/ppermute | solution.py:24
  117.6 40.8 %all-to-all-start.2 = ((f32[128,8,128]{2,1,0:T(8,128)}), f32[128,8,128]{2,1,0:T(8,128)S(1)}, u32[]{:S(2)}, u32[]{:S(2)}) async-start(f32[128,8,128]{2,1,0:T(8,128)} %shard_map.61), calls=%async_computation.2 | async-start | bytes 1048576 | tf_op jit(solution)/shard_map/all_to_all | solution.py:355
  130.1 10.8 %collective-permute-start.7 = (f32[16,768]{1,0:T(8,128)S(1)}, f32[16,768]{1,0:T(8,128)S(1)}, u32[]{:S(2)}, u32[]{:S(2)}) collective-permute-start(f32[16,768]{1,0:T(8,128)S(1)} %shard_map.57), channel_id=1, source_target_pairs={{0,48},{8,56},{1,49},{9,57},{16,32},{24,40},{17,33},{25,41},{32,16... | collective-permute-start | bytes 147464 | tf_op jit(solution)/shard_map/ppermute | solution.py:24
  132.5 12.2 %collective-permute-start.6 = (f32[16,768]{1,0:T(8,128)S(1)}, f32[16,768]{1,0:T(8,128)S(1)}, u32[]{:S(2)}, u32[]{:S(2)}) collective-permute-start(f32[16,768]{1,0:T(8,128)S(1)} %shard_map.57), channel_id=1, source_target_pairs={{0,32},{8,40},{1,33},{9,41},{16,48},{24,56},{17,49},{25,57},{32,0}... | collective-permute-start | bytes 147464 | tf_op jit(solution)/shard_map/ppermute | solution.py:24
  132.6 12.2 %collective-permute-start.5 = (f32[16,768]{1,0:T(8,128)S(1)}, f32[16,768]{1,0:T(8,128)S(1)}, u32[]{:S(2)}, u32[]{:S(2)}) collective-permute-start(f32[16,768]{1,0:T(8,128)S(1)} %shard_map.57), channel_id=1, source_target_pairs={{0,16},{8,24},{1,17},{9,25},{16,0},{24,8},{17,1},{25,9},{32,48},{4... | collective-permute-start | bytes 147464 | tf_op jit(solution)/shard_map/ppermute | solution.py:24
  144.7 9.1 %collective-permute-start.10 = (f32[64,768]{1,0:T(8,128)S(1)}, f32[64,768]{1,0:T(8,128)S(1)}, u32[]{:S(2)}, u32[]{:S(2)}) collective-permute-start(f32[64,768]{1,0:T(8,128)S(1)} %pad_maximum_fusion), channel_id=1, source_target_pairs={{0,192},{8,200},{1,193},{9,201},{16,208},{24,216},{17,209},{25,217... | collective-permute-start | bytes 589832 | tf_op jit(solution)/shard_map/ppermute | solution.py:24
  147.3 6.6 %collective-permute-start.9 = (f32[64,768]{1,0:T(8,128)S(1)}, f32[64,768]{1,0:T(8,128)S(1)}, u32[]{:S(2)}, u32[]{:S(2)}) collective-permute-start(f32[64,768]{1,0:T(8,128)S(1)} %pad_maximum_fusion), channel_id=1, source_target_pairs={{0,128},{8,136},{1,129},{9,137},{16,144},{24,152},{17,145},{25,153... | collective-permute-start | bytes 589832 | tf_op jit(solution)/shard_map/ppermute | solution.py:24
  148.1 5.7 %collective-permute-start.8 = (f32[64,768]{1,0:T(8,128)S(1)}, f32[64,768]{1,0:T(8,128)S(1)}, u32[]{:S(2)}, u32[]{:S(2)}) collective-permute-start(f32[64,768]{1,0:T(8,128)S(1)} %pad_maximum_fusion), channel_id=1, source_target_pairs={{0,64},{8,72},{1,65},{9,73},{16,80},{24,88},{17,81},{25,89},{32,96... | collective-permute-start | bytes 589832 | tf_op jit(solution)/shard_map/ppermute | solution.py:24
  153.9 6.4 %collective-permute-start.11 = (f32[256,768]{1,0:T(8,128)S(1)}, f32[256,768]{1,0:T(8,128)S(1)}, u32[]{:S(2)}, u32[]{:S(2)}) collective-permute-start(f32[256,768]{1,0:T(8,128)S(1)} %constant_dynamic-update-slice_fusion.mine_ref), channel_id=1, source_target_pairs={{0,8},{8,0},{1,9},{9,1},{16,24},{24,16},{17,25},{25,17},{32,40},{4... | collective-permute-start | bytes 2359304 | tf_op jit(solution)/shard_map/ppermute | solution.py:24
  158.4 3.7 %collective-permute-start.19 = (f32[128,8,128]{2,1,0:T(8,128)S(1)}, f32[128,8,128]{2,1,0:T(8,128)S(1)}, u32[]{:S(2)}, u32[]{:S(2)}) collective-permute-start(f32[128,8,128]{2,1,0:T(8,128)S(1)} %all-to-all-done.2.mine_ref), channel_id=1, source_target_pairs={{0,8},{8,0},{1,9},{9,1},{16,24},{24,16},{17,25},{25,17},{32,40},{4... | collective-permute-start | bytes 1572872 | tf_op jit(solution)/shard_map/ppermute | solution.py:24

commit v3 on v2

--- a/solution.py
+++ b/solution.py
@@ -77,30 +77,21 @@
     return spots
 
 
-def logits_kernel(place_ref, emb_ref, cent_ref, p_ref, stat_ref, held_ref, emb_buf, sems):
+def logits_kernel(place_ref, emb_ref, cent_ref, p_ref, stat_ref, cent_t_ref, old_ref, held_ref):
     rows, width = emb_ref.shape
     step = 256
     spots = relative_blocks(place_ref)
     size = cent_ref.shape[0] // len(spots)
-    copies = []
     for i, spot in enumerate(spots):
-        source = cent_ref.at[pl.ds(pl.multiple_of(spot * size, 16), size), :]
-        copies.append(pltpu.make_async_copy(source, held_ref.at[i * size : (i + 1) * size, :], sems.at[i]))
-    for i in range(rows // step):
-        at = slice(i * step, (i + 1) * step)
-        copies.append(pltpu.make_async_copy(emb_ref.at[at, :], emb_buf.at[at, :], sems.at[len(spots) + i]))
-    for copy in copies:
-        copy.start()
-    for copy in copies[: len(spots)]:
-        copy.wait()
+        held_ref[i * size : (i + 1) * size, :] = cent_ref[pl.ds(pl.multiple_of(spot * size, 16), size), :]
     cent = held_ref[...]
+    cent_t_ref[...] = cent.T
+    old_ref[...] = cent[:size, :].astype(F32)
     cent_f = cent.astype(F32)
     half_sq = 0.5 * jnp.sum(cent_f * cent_f, axis=1, keepdims=True)
     tops, sums = [], []
-    for i in range(rows // step):
-        start = i * step
-        copies[len(spots) + i].wait()
-        cross = dot(cent, emb_buf[start : start + step, :], 1, 1)
+    for start in range(0, rows, step):
+        cross = dot(cent, emb_ref[start : start + step, :], 1, 1)
         logits = (cross - half_sq) * (3.0 / math.sqrt(width))
         top = jnp.max(logits, axis=0, keepdims=True)
         p = jnp.exp(logits - top)
@@ -158,8 +149,7 @@
 def centroid_kernel(mine_ref, got_ref, old_ref, out_ref):
     rows, width = out_ref.shape
     total = mine_ref[...] + got_ref[...]
-    old = old_ref[:rows, :].astype(F32)
-    out_ref[...] = (total[:, :width] + old) / (total[:, width : width + 1] + 1.0)
+    out_ref[...] = (total[:, :width] + old_ref[...]) / (total[:, width : width + 1] + 1.0)
 
 
 def add_kernel(a_ref, b_ref, c_ref, d_ref, out_ref):
@@ -277,25 +267,24 @@
     cents = NY * NZH
     share = width // cents
 
-    p, stat, ordered = call(
+    p, stat, cent_t, old = call(
         logits_kernel,
         (
             shape((held, rows_here)),
             shape((cents, 2 * rows_here // 128, 128)),
-            shape((held, width), BF16),
+            shape((width, held), BF16),
+            shape((held // (NC * NX * NZL), width)),
         ),
         (place, embeddings, centroids),
         smem=1,
-        hbm_in=2,
-        scratch=(pltpu.VMEM((rows_here, width), BF16), pltpu.SemaphoreType.DMA((64,))),
-        limit=60,
+        scratch=(pltpu.VMEM((held, width), BF16),),
         flops=2 * rows_here * held * width,
     )
     stats = lax.all_to_all(stat, "cent", 0, 0, tiled=True)
     outs = call(
         weights_kernel,
         (shape((held, rows_here), BF16), shape((held, 128))) + (shape((share, rows_here)),) * 8,
-        (place, p, stat, stats, ordered.T),
+        (place, p, stat, stats, cent_t),
         smem=1,
         flops=2 * rows_here * held * width,
     )
@@ -313,14 +302,12 @@
         scratch=(pltpu.VMEM((width, rows_here), BF16),),
         flops=2 * rows_here * held * width,
     )
-    for move in (other_core, along_x(2), along_x(1), along_zl(2)):
+    for step, move in enumerate((other_core, along_x(2), along_x(1), along_zl(2))):
         half = keep.shape[0] // 2
-        keep, send = call(
-            halve_kernel, (shape((half, width + 128)),) * 2, (keep, hop(send, move)), limit=4
-        )
-    new = call(
-        centroid_kernel, shape((half, width)), (keep, hop(send, along_zl(1)), ordered), limit=4
-    )
+        got = hop(send, move)
+        keep, send = call(halve_kernel, (shape((half, width + 128)),) * 2, (keep, got), limit=4)
+        if step == 2:
+            send, peer = lax.optimization_barrier((send, peer))
     peers = NX * NZL
 
     per = subspaces // cents
@@ -332,6 +319,10 @@
         hbm_in=1,
         scratch=(pltpu.VMEM((per, depth, codes), F32), pltpu.SemaphoreType.DMA),
         flops=64 * rows_here * per * codes * 64,
+    )
+    sums, keep = lax.optimization_barrier((sums, keep))
+    new = call(
+        centroid_kernel, shape((half, width)), (keep, hop(send, along_zl(1)), old), limit=4
     )
     new_z = jnp.concatenate([new] + [hop(new, along_zl(k)) for k in (1, 2, 3)], axis=0)
     all_parts = lax.all_to_all(sums, "rows", 0, 0, tiled=True)
@@ -348,6 +339,7 @@
         scratch=(pltpu.VMEM((share, codes), F32), pltpu.SemaphoreType.DMA),
     )
     new_x = jnp.concatenate([new_z] + [hop(new_z, along_x(k)) for k in (1, 2, 3)], axis=0)
+    tile, new_z = lax.optimization_barrier((tile, new_z))
     new_other = hop(new_x, other_core)
     new_centroids = call(
         centroids_kernel, shape((held, width)), (place, new_x, new_other), smem=1

time: 164 us -> 144 us (0.88)
  waiting for transfers between devices: 68.7 us -> 46.1 us
  blocking collectives: 0 us -> 20.6 us
  starting transfers between devices: 63.4 us -> 52.7 us
  Pallas kernels: 25.6 us -> 20.6 us
  local copies, waits for them, and re-layouts: 5.18 us -> 2.7 us
    all_to_all x0 -> x1, blocking collectives: none -> 20.6 us  [body(): stats = lax.all_to_all(stat, 'cent', 0, 0, tiled=True)]
    ppermute x20, waiting for transfers between devices: 61 us -> 46 us  [hop(): return lax.ppermute(value, BOTH, pairs)]
    all_to_all x1 -> x0, starting transfers between devices: 11.8 us -> none  [body(): stats = lax.all_to_all(stat, 'cent', 0, 0, tiled=True)]
    ppermute x20, starting transfers between devices: 26.5 us -> 35.3 us  [hop(): return lax.ppermute(value, BOTH, pairs)]
    all_to_all x1 -> x0, waiting for transfers between devices: 7.69 us -> none  [body(): stats = lax.all_to_all(stat, 'cent', 0, 0, tiled=True)]
    pallas_call x13, Pallas kernels: 25.6 us -> 20.6 us  [call(): pl.pallas_call(kernel, out_shape=out, in_specs=specs, out_specs=jax.tree....]
    all_to_all x1, starting transfers between devices: 12.7 us -> 7.81 us  [body(): all_parts = lax.all_to_all(sums, 'rows', 0, 0, tiled=True)]
    all_to_all x1, starting transfers between devices: 12.4 us -> 9.65 us  [body(): lax.all_to_all(tile, BOTH, 0, 0, tiled=True, axis_index_groups=same_core)]
  transfers between devices with their start and end apart: 23 -> 22, of which waited for: 10 -> 7; matrix products, arithmetic and copies ran while one was open for 1% -> 0% of each run, Pallas kernels for 8% -> 8%
where the time goes in v3:
time: 144 us
  starting transfers between devices  52.7 us (37%)
  waiting for transfers between devices  46.1 us (32%)
  Pallas kernels  20.6 us (14%)
  blocking collectives  20.6 us (14%)
  local copies, waits for them, and re-layouts  2.7 us (2%)
    ppermute x20, waiting for transfers between devices, hop(): return lax.ppermute(value, BOTH, pairs)  46 us
    ppermute x20, starting transfers between devices, hop(): return lax.ppermute(value, BOTH, pairs)  35.3 us
    pallas_call x13, Pallas kernels, call(): pl.pallas_call(kernel, out_shape=out, in_specs=specs, out_specs=jax.tree....  20.6 us
    all_to_all x1, blocking collectives, body(): stats = lax.all_to_all(stat, 'cent', 0, 0, tiled=True)  20.6 us
    all_to_all x1, starting transfers between devices, body(): lax.all_to_all(tile, BOTH, 0, 0, tiled=True, axis_index_groups=same_core)  9.65 us
    all_to_all x1, starting transfers between devices, body(): all_parts = lax.all_to_all(sums, 'rows', 0, 0, tiled=True)  7.81 us
  transfers between devices with their start and end apart: 22, of which 7 were waited for; matrix products, arithmetic and copies ran while one was open for 0% of the time, Pallas kernels for 8%

profile of v3, /device:TPU:1, one launch (start us, length us, event | category | flops | bytes accessed | tf_op | source)
XLA Modules:
  0.0 143.6 jit_solution(18257919674005029448)
XLA Ops:
  0.7 0.1 stack.23.place_ref
  0.8 0.0 copy-start.1
  0.8 1.4 copy-done.1
  2.2 0.0 copy-start.2
  2.2 1.1 copy-done.2
  3.3 2.1 %shard_map.50 = (f32[512,1024]{1,0:T(8,128)S(1)}, f32[8,16,128]{2,1,0:T(8,128)S(1)}, bf16[768,512]{1,0:T(8,128)(2,1)S(1)}, f32[16,768]{1,0:T(8,128)S(1)}) custom-call(s32[5]{0:T(128)S(1)} %stack.23.place_ref, bf16[1024,768]{1,0:T(8,128)(2,1)S(1)} %copy-done.1, bf16[512,768]{1,0:T(8,128)(2,1)S(1)} %copy-done.2), custom_call_target="tpu_custom_call" | custom-call | flops 805306368 | bytes 4718632 | tf_op jit(solution)/shard_map/pallas_call | solution.py:52
  5.4 20.6 %all_to_all.15.stat_ref = f32[8,16,128]{2,1,0:T(8,128)S(1)} all-to-all(f32[8,16,128]{2,1,0:T(8,128)S(1)} %get-tuple-element.33.mine_ref), channel_id=1, replica_groups=mesh['rows'=32,'cent'=8] {'cent'}, dimensions={0} | all-to-all | bytes 131072 | tf_op jit(solution)/shard_map/all_to_all | solution.py:283
  26.0 2.2 %shard_map.51 = (bf16[512,1024]{1,0:T(8,128)(2,1)S(1)}, f32[512,128]{1,0:T(8,128)S(1)}, f32[96,1024]{1,0:T(8,128)S(1)}, f32[96,1024]{1,0:T(8,128)S(1)}, f32[96,1...) custom-call(s32[5]{0:T(128)S(1)} %stack.23.place_ref, ...), custom_call_target="tpu_custom_call" | custom-call | flops 805306368 | bytes 6029352 | tf_op jit(solution)/shard_map/pallas_call | solution.py:52
  28.1 1.6 %shard_map.52 = (f32[256,896]{1,0:T(8,128)S(1)}, f32[256,896]{1,0:T(8,128)S(1)}, f32[96,1024]{1,0:T(8,128)S(1)}) custom-call(s32[5]{0:T(128)S(1)} %stack.23.place_ref, bf16[512,1024]{1,0:T(8,128)(2,1)S(1)} %get-tuple-element.35.wb_ref, f32[512,128]{1,0:T(8,128)S(1)} %get-tuple-element.36.count_ref, bf16[1024,768]{1,0:T(8,128)(2,1)S(1)} %copy-done.1), custom_call_target="tpu_custom_call" | custom-call | flops 805306368 | bytes 5767208 | tf_op jit(solution)/shard_map/pallas_call | solution.py:52
  29.7 2.2 %collective-permute-start.3 = (f32[256,896]{1,0:T(8,128)S(1)}, f32[256,896]{1,0:T(8,128)S(1)}, u32[]{:S(2)}, u32[]{:S(2)}) collective-permute-start(f32[256,896]{1,0:T(8,128)S(1)} %get-tuple-element.43), channel_id=1, source_target_pairs={{0,8},{8,0},{1,9},{9,1},{16,24},{24,16},{17,25},{25,17},{32,40},{4... | collective-permute-start | bytes 2752520 | tf_op jit(solution)/shard_map/ppermute | solution.py:24
  31.9 0.3 collective-permute-start.6
  32.2 2.4 %collective-permute-start.7 = (f32[96,1024]{1,0:T(8,128)S(1)}, f32[96,1024]{1,0:T(8,128)S(1)}, u32[]{:S(2)}, u32[]{:S(2)}) collective-permute-start(f32[96,1024]{1,0:T(8,128)S(1)} %get-tuple-element.51), channel_id=1, source_target_pairs={{0,6},{8,14},{1,7},{9,15},{16,22},{24,30},{17,23},{25,31},{32,38},... | collective-permute-start | bytes 1179656 | tf_op jit(solution)/shard_map/ppermute | solution.py:24
  34.6 0.0 collective-permute-start.8
  34.6 0.0 collective-permute-done.3.got_ref
  34.6 0.1 shard_map.53
  34.7 2.8 %collective-permute-start.4 = (f32[128,896]{1,0:T(8,128)S(1)}, f32[128,896]{1,0:T(8,128)S(1)}, u32[]{:S(2)}, u32[]{:S(2)}) collective-permute-start(f32[128,896]{1,0:T(8,128)S(1)} %get-tuple-element.45), channel_id=1, source_target_pairs={{0,128},{8,136},{1,129},{9,137},{16,144},{24,152},{17,145},{25,153... | collective-permute-start | bytes 1376264 | tf_op jit(solution)/shard_map/ppermute | solution.py:24
  37.6 14.7 %collective-permute-done.6.b_ref = f32[96,1024]{1,0:T(8,128)S(1)} collective-permute-done((f32[96,1024]{1,0:T(8,128)S(1)}, f32[96,1024]{1,0:T(8,128)S(1)}, u32[]{:S(2)}, u32[]{:S(2)}) %collective-permute-start.6) | collective-permute-done | bytes 393248 | tf_op jit(solution)/shard_map/ppermute | solution.py:24
  52.2 0.0 collective-permute-done.7.c_ref
  52.3 0.0 collective-permute-done.8.d_ref
  52.3 0.0 copy-start
  52.3 0.1 shard_map.56
  52.3 0.5 collective-permute-start.9
  52.9 0.6 collective-permute-start
  53.5 2.1 %collective-permute-start.1 = (f32[96,1024]{1,0:T(8,128)S(1)}, f32[96,1024]{1,0:T(8,128)S(1)}, u32[]{:S(2)}, u32[]{:S(2)}) collective-permute-start(f32[96,1024]{1,0:T(8,128)S(1)} %get-tuple-element.40), channel_id=1, source_target_pairs={{0,6},{8,14},{1,7},{9,15},{16,22},{24,30},{17,23},{25,31},{32,38},... | collective-permute-start | bytes 1179656 | tf_op jit(solution)/shard_map/ppermute | solution.py:24
  55.6 0.9 collective-permute-start.2
  56.4 0.0 collective-permute-done.4.got_ref
  56.5 1.3 collective-permute-start.5
  57.8 4.0 %collective-permute-done.5.got_ref = f32[64,896]{1,0:T(8,128)S(1)} collective-permute-done((f32[64,896]{1,0:T(8,128)S(1)}, f32[64,896]{1,0:T(8,128)S(1)}, u32[]{:S(2)}, u32[]{:S(2)}) %collective-permute-start.5) | collective-permute-done | bytes 229408 | tf_op jit(solution)/shard_map/ppermute | solution.py:24
  61.8 6.2 %collective-permute-done.9.e_ref = f32[96,1024]{1,0:T(8,128)S(1)} collective-permute-done((f32[96,1024]{1,0:T(8,128)S(1)}, f32[96,1024]{1,0:T(8,128)S(1)}, u32[]{:S(2)}, u32[]{:S(2)}) %collective-permute-start.9) | collective-permute-done | bytes 393248 | tf_op jit(solution)/shard_map/ppermute | solution.py:24
  68.0 7.8 %collective-permute-start.10 = (f32[32,896]{1,0:T(8,128)S(1)}, f32[32,896]{1,0:T(8,128)S(1)}, u32[]{:S(2)}, u32[]{:S(2)}) collective-permute-start(f32[32,896]{1,0:T(8,128)S(1)} %get-tuple-element.55), channel_id=1, source_target_pairs={{0,32},{8,40},{1,33},{9,41},{16,48},{24,56},{17,49},{25,57},{32,0}... | collective-permute-start | bytes 344072 | tf_op jit(solution)/shard_map/ppermute | solution.py:24
  75.8 0.0 collective-permute-done.b_ref
  75.8 0.0 collective-permute-done.1.c_ref
  75.8 0.0 collective-permute-done.2.d_ref
  75.8 0.0 copy-done
  75.8 9.4 %shard_map.57 = f32[32,8,256]{2,1,0:T(8,128)} custom-call(s32[5]{0:T(128)S(1)} %stack.23.place_ref, f32[96,8,256]{2,1,0:T(8,128)S(1)} %copy-done, f32[96,1024]{1,0:T(8,128)S(1)} %get-tuple-element.37.emb_t_ref, f32[96,1024]{1,0:T(8,128)S(1)} %get-tuple-element.38.a_ref, f32[96,1024]{1,0:T(8,128)S(1)} %collective-permute-done.b_ref, ...), custom_call_target="tpu_custom_call" | custom-call | flops 12884901888 | bytes 6291496 | tf_op jit(solution)/shard_map/pallas_call | solution.py:52
  85.2 0.0 collective-permute-done.10.got_ref
  85.2 7.8 %all-to-all-start.1 = ((f32[32,8,256]{2,1,0:T(8,128)}), f32[32,8,256]{2,1,0:T(8,128)S(1)}, u32[]{:S(2)}, u32[]{:S(2)}) async-start(f32[32,8,256]{2,1,0:T(8,128)} %shard_map.57), calls=%async_computation.1 | async-start | bytes 524288 | tf_op jit(solution)/shard_map/all_to_all | solution.py:328
  93.1 1.5 %collective-permute-start.11 = (f32[16,896]{1,0:T(8,128)S(1)}, f32[16,896]{1,0:T(8,128)S(1)}, u32[]{:S(2)}, u32[]{:S(2)}) collective-permute-start(f32[16,896]{1,0:T(8,128)S(1)} %get-tuple-element.58), channel_id=1, source_target_pairs={{0,16},{8,24},{1,17},{9,25},{16,0},{24,8},{17,1},{25,9},{32,48},{4... | collective-permute-start | bytes 172040 | tf_op jit(solution)/shard_map/ppermute | solution.py:24
  94.5 4.7 %collective-permute-done.11.got_ref = f32[16,896]{1,0:T(8,128)S(1)} collective-permute-done((f32[16,896]{1,0:T(8,128)S(1)}, f32[16,896]{1,0:T(8,128)S(1)}, u32[]{:S(2)}, u32[]{:S(2)}) %collective-permute-start.11) | collective-permute-done | bytes 57376 | tf_op jit(solution)/shard_map/ppermute | solution.py:24
  99.3 0.1 shard_map.59
  99.4 3.5 %collective-permute-start.14 = (f32[16,768]{1,0:T(8,128)S(1)}, f32[16,768]{1,0:T(8,128)S(1)}, u32[]{:S(2)}, u32[]{:S(2)}) collective-permute-start(f32[16,768]{1,0:T(8,128)S(1)} %shard_map.59), channel_id=1, source_target_pairs={{0,48},{8,56},{1,49},{9,57},{16,32},{24,40},{17,33},{25,41},{32,16... | collective-permute-start | bytes 147464 | tf_op jit(solution)/shard_map/ppermute | solution.py:24
  102.9 0.2 collective-permute-start.13
  103.1 0.2 collective-permute-start.12
  103.3 1.1 collective-permute-done.14
  104.4 2.9 %collective-permute-done.13 = f32[16,768]{1,0:T(8,128)S(1)} collective-permute-done((f32[16,768]{1,0:T(8,128)S(1)}, f32[16,768]{1,0:T(8,128)S(1)}, u32[]{:S(2)}, u32[]{:S(2)}) %collective-permute-start.13) | collective-permute-done | bytes 49184 | tf_op jit(solution)/shard_map/ppermute | solution.py:24
  107.3 0.0 collective-permute-done.12
  107.3 0.0 all-to-all-done.1.parts_ref
  107.3 1.6 %shard_map.61 = f32[128,8,128]{2,1,0:T(8,128)} custom-call(s32[5]{0:T(128)S(1)} %stack.23.place_ref, f32[768,256]{1,0:T(8,128)S(1)} %bitcast.7, f32[32,8,256]{2,1,0:T(8,128)S(1)} %all-to-all-done.1.parts_ref), custom_call_target="tpu_custom_call" | custom-call | bytes 2097192 | tf_op jit(solution)/shard_map/pallas_call | solution.py:52
  108.9 9.7 %all-to-all-start.2 = ((f32[128,8,128]{2,1,0:T(8,128)}), f32[128,8,128]{2,1,0:T(8,128)S(1)}, u32[]{:S(2)}, u32[]{:S(2)}) async-start(f32[128,8,128]{2,1,0:T(8,128)} %shard_map.61), calls=%async_computation.2 | async-start | bytes 1048576 | tf_op jit(solution)/shard_map/all_to_all | solution.py:347
  118.5 1.9 %collective-permute-start.17 = (f32[64,768]{1,0:T(8,128)S(1)}, f32[64,768]{1,0:T(8,128)S(1)}, u32[]{:S(2)}, u32[]{:S(2)}) collective-permute-start(f32[64,768]{1,0:T(8,128)S(1)} %pad_maximum_fusion), channel_id=1, source_target_pairs={{0,192},{8,200},{1,193},{9,201},{16,208},{24,216},{17,209},{25,217... | collective-permute-start | bytes 589832 | tf_op jit(solution)/shard_map/ppermute | solution.py:24
  120.4 0.6 collective-permute-start.16
  121.0 0.9 collective-permute-start.15
  121.9 12.4 %collective-permute-done.15 = f32[64,768]{1,0:T(8,128)S(1)} collective-permute-done((f32[64,768]{1,0:T(8,128)S(1)}, f32[64,768]{1,0:T(8,128)S(1)}, u32[]{:S(2)}, u32[]{:S(2)}) %collective-permute-start.15) | collective-permute-done | bytes 196640 | tf_op jit(solution)/shard_map/ppermute | solution.py:24
  134.3 0.0 collective-permute-done.16
  134.3 0.0 collective-permute-done.17
  134.4 2.2 %collective-permute-start.18 = (f32[256,768]{1,0:T(8,128)S(1)}, f32[256,768]{1,0:T(8,128)S(1)}, u32[]{:S(2)}, u32[]{:S(2)}) collective-permute-start(f32[256,768]{1,0:T(8,128)S(1)} %constant_dynamic-update-slice_fusion.mine_ref), channel_id=1, source_target_pairs={{0,8},{8,0},{1,9},{9,1},{16,24},{24,16},{17,25},{25,17},{32,40},{4... | collective-permute-start | bytes 2359304 | tf_op jit(solution)/shard_map/ppermute | solution.py:24
  136.6 0.0 all-to-all-done.2.mine_ref
  136.6 3.5 %collective-permute-start.19 = (f32[128,8,128]{2,1,0:T(8,128)S(1)}, f32[128,8,128]{2,1,0:T(8,128)S(1)}, u32[]{:S(2)}, u32[]{:S(2)}) collective-permute-start(f32[128,8,128]{2,1,0:T(8,128)S(1)} %all-to-all-done.2.mine_ref), channel_id=1, source_target_pairs={{0,8},{8,0},{1,9},{9,1},{16,24},{24,16},{17,25},{25,17},{32,40},{4... | collective-permute-start | bytes 1572872 | tf_op jit(solution)/shard_map/ppermute | solution.py:24
  140.1 0.0 collective-permute-done.18.theirs_ref
  140.1 1.8 %shard_map.60 = f32[512,768]{1,0:T(8,128)} custom-call(s32[5]{0:T(128)S(1)} %stack.23.place_ref, f32[256,768]{1,0:T(8,128)S(1)} %constant_dynamic-update-slice_fusion.mine_ref, f32[256,768]{1,0:T(8,128)S(1)} %collective-permute-done.18.theirs_ref), custom_call_target="tpu_custom_call" | custom-call | bytes 3145768 | tf_op jit(solution)/shard_map/pallas_call | solution.py:52
  141.9 0.0 collective-permute-done.19.theirs_ref
  141.9 1.7 %shard_map.62 = f32[768,256]{1,0:T(8,128)} custom-call(s32[5]{0:T(128)S(1)} %stack.23.place_ref, f32[128,8,128]{2,1,0:T(8,128)S(1)} %all-to-all-done.2.mine_ref, f32[128,8,128]{2,1,0:T(8,128)S(1)} %collective-permute-done.19.theirs_ref), custom_call_target="tpu_custom_call" | custom-call | bytes 2097192 | tf_op jit(solution)/shard_map/pallas_call | solution.py:52
  (11 shorter events, 0.2 us)
Async XLA Ops:
  0.8 1.4 copy-start.1
  2.2 1.1 copy-start.2
  29.7 4.9 %collective-permute-start.3 = (f32[256,896]{1,0:T(8,128)S(1)}, f32[256,896]{1,0:T(8,128)S(1)}, u32[]{:S(2)}, u32[]{:S(2)}) collective-permute-start(f32[256,896]{1,0:T(8,128)S(1)} %get-tuple-element.43), channel_id=1, source_target_pairs={{0,8},{8,0},{1,9},{9,1},{16,24},{24,16},{17,25},{25,17},{32,40},{4... | collective-permute-start | bytes 2752520 | tf_op jit(solution)/shard_map/ppermute | solution.py:24
  31.9 20.3 %collective-permute-start.6 = (f32[96,1024]{1,0:T(8,128)S(1)}, f32[96,1024]{1,0:T(8,128)S(1)}, u32[]{:S(2)}, u32[]{:S(2)}) collective-permute-start(f32[96,1024]{1,0:T(8,128)S(1)} %get-tuple-element.50), channel_id=1, source_target_pairs={{0,2},{8,10},{1,3},{9,11},{16,18},{24,26},{17,19},{25,27},{32,34},... | collective-permute-start | bytes 1179656 | tf_op jit(solution)/shard_map/ppermute | solution.py:24
  32.2 20.0 %collective-permute-start.7 = (f32[96,1024]{1,0:T(8,128)S(1)}, f32[96,1024]{1,0:T(8,128)S(1)}, u32[]{:S(2)}, u32[]{:S(2)}) collective-permute-start(f32[96,1024]{1,0:T(8,128)S(1)} %get-tuple-element.51), channel_id=1, source_target_pairs={{0,6},{8,14},{1,7},{9,15},{16,22},{24,30},{17,23},{25,31},{32,38},... | collective-permute-start | bytes 1179656 | tf_op jit(solution)/shard_map/ppermute | solution.py:24
  34.6 17.6 %collective-permute-start.8 = (f32[96,1024]{1,0:T(8,128)S(1)}, f32[96,1024]{1,0:T(8,128)S(1)}, u32[]{:S(2)}, u32[]{:S(2)}) collective-permute-start(f32[96,1024]{1,0:T(8,128)S(1)} %get-tuple-element.52), channel_id=1, source_target_pairs={{0,4},{8,12},{1,5},{9,13},{16,20},{24,28},{17,21},{25,29},{32,36},... | collective-permute-start | bytes 1179656 | tf_op jit(solution)/shard_map/ppermute | solution.py:24
  34.7 21.7 %collective-permute-start.4 = (f32[128,896]{1,0:T(8,128)S(1)}, f32[128,896]{1,0:T(8,128)S(1)}, u32[]{:S(2)}, u32[]{:S(2)}) collective-permute-start(f32[128,896]{1,0:T(8,128)S(1)} %get-tuple-element.45), channel_id=1, source_target_pairs={{0,128},{8,136},{1,129},{9,137},{16,144},{24,152},{17,145},{25,153... | collective-permute-start | bytes 1376264 | tf_op jit(solution)/shard_map/ppermute | solution.py:24
  52.3 23.5 %copy-start = (f32[96,8,256]{2,1,0:T(8,128)S(1)}, f32[96,8,256]{2,1,0:T(8,128)}, u32[]{:S(2)}) copy-start(f32[96,8,256]{2,1,0:T(8,128)} %all_books_ref.1) | copy-start | bytes 2359300
  52.3 15.7 %collective-permute-start.9 = (f32[96,1024]{1,0:T(8,128)S(1)}, f32[96,1024]{1,0:T(8,128)S(1)}, u32[]{:S(2)}, u32[]{:S(2)}) collective-permute-start(f32[96,1024]{1,0:T(8,128)S(1)} %shard_map.56), channel_id=1, source_target_pairs={{0,1},{8,9},{1,0},{9,8},{16,17},{24,25},{17,16},{25,24},{32,33},{4... | collective-permute-start | bytes 1179656 | tf_op jit(solution)/shard_map/ppermute | solution.py:24
  52.9 22.9 %collective-permute-start = (f32[96,1024]{1,0:T(8,128)S(1)}, f32[96,1024]{1,0:T(8,128)S(1)}, u32[]{:S(2)}, u32[]{:S(2)}) collective-permute-start(f32[96,1024]{1,0:T(8,128)S(1)} %get-tuple-element.39), channel_id=1, source_target_pairs={{0,2},{8,10},{1,3},{9,11},{16,18},{24,26},{17,19},{25,27},{32,34},... | collective-permute-start | bytes 1179656 | tf_op jit(solution)/shard_map/ppermute | solution.py:24
  53.5 22.3 %collective-permute-start.1 = (f32[96,1024]{1,0:T(8,128)S(1)}, f32[96,1024]{1,0:T(8,128)S(1)}, u32[]{:S(2)}, u32[]{:S(2)}) collective-permute-start(f32[96,1024]{1,0:T(8,128)S(1)} %get-tuple-element.40), channel_id=1, source_target_pairs={{0,6},{8,14},{1,7},{9,15},{16,22},{24,30},{17,23},{25,31},{32,38},... | collective-permute-start | bytes 1179656 | tf_op jit(solution)/shard_map/ppermute | solution.py:24
  55.6 20.2 %collective-permute-start.2 = (f32[96,1024]{1,0:T(8,128)S(1)}, f32[96,1024]{1,0:T(8,128)S(1)}, u32[]{:S(2)}, u32[]{:S(2)}) collective-permute-start(f32[96,1024]{1,0:T(8,128)S(1)} %get-tuple-element.41), channel_id=1, source_target_pairs={{0,4},{8,12},{1,5},{9,13},{16,20},{24,28},{17,21},{25,29},{32,36},... | collective-permute-start | bytes 1179656 | tf_op jit(solution)/shard_map/ppermute | solution.py:24
  56.5 5.3 %collective-permute-start.5 = (f32[64,896]{1,0:T(8,128)S(1)}, f32[64,896]{1,0:T(8,128)S(1)}, u32[]{:S(2)}, u32[]{:S(2)}) collective-permute-start(f32[64,896]{1,0:T(8,128)S(1)} %get-tuple-element.47), channel_id=1, source_target_pairs={{0,64},{8,72},{1,65},{9,73},{16,80},{24,88},{17,81},{25,89},{32,96... | collective-permute-start | bytes 688136 | tf_op jit(solution)/shard_map/ppermute | solution.py:24
  68.0 17.2 %collective-permute-start.10 = (f32[32,896]{1,0:T(8,128)S(1)}, f32[32,896]{1,0:T(8,128)S(1)}, u32[]{:S(2)}, u32[]{:S(2)}) collective-permute-start(f32[32,896]{1,0:T(8,128)S(1)} %get-tuple-element.55), channel_id=1, source_target_pairs={{0,32},{8,40},{1,33},{9,41},{16,48},{24,56},{17,49},{25,57},{32,0}... | collective-permute-start | bytes 344072 | tf_op jit(solution)/shard_map/ppermute | solution.py:24
  85.2 22.0 %all-to-all-start.1 = ((f32[32,8,256]{2,1,0:T(8,128)}), f32[32,8,256]{2,1,0:T(8,128)S(1)}, u32[]{:S(2)}, u32[]{:S(2)}) async-start(f32[32,8,256]{2,1,0:T(8,128)} %shard_map.57), calls=%async_computation.1 | async-start | bytes 524288 | tf_op jit(solution)/shard_map/all_to_all | solution.py:328
  93.1 6.2 %collective-permute-start.11 = (f32[16,896]{1,0:T(8,128)S(1)}, f32[16,896]{1,0:T(8,128)S(1)}, u32[]{:S(2)}, u32[]{:S(2)}) collective-permute-start(f32[16,896]{1,0:T(8,128)S(1)} %get-tuple-element.58), channel_id=1, source_target_pairs={{0,16},{8,24},{1,17},{9,25},{16,0},{24,8},{17,1},{25,9},{32,48},{4... | collective-permute-start | bytes 172040 | tf_op jit(solution)/shard_map/ppermute | solution.py:24
  99.4 5.0 %collective-permute-start.14 = (f32[16,768]{1,0:T(8,128)S(1)}, f32[16,768]{1,0:T(8,128)S(1)}, u32[]{:S(2)}, u32[]{:S(2)}) collective-permute-start(f32[16,768]{1,0:T(8,128)S(1)} %shard_map.59), channel_id=1, source_target_pairs={{0,48},{8,56},{1,49},{9,57},{16,32},{24,40},{17,33},{25,41},{32,16... | collective-permute-start | bytes 147464 | tf_op jit(solution)/shard_map/ppermute | solution.py:24
  102.9 4.4 %collective-permute-start.13 = (f32[16,768]{1,0:T(8,128)S(1)}, f32[16,768]{1,0:T(8,128)S(1)}, u32[]{:S(2)}, u32[]{:S(2)}) collective-permute-start(f32[16,768]{1,0:T(8,128)S(1)} %shard_map.59), channel_id=1, source_target_pairs={{0,32},{8,40},{1,33},{9,41},{16,48},{24,56},{17,49},{25,57},{32,0}... | collective-permute-start | bytes 147464 | tf_op jit(solution)/shard_map/ppermute | solution.py:24
  103.1 4.2 %collective-permute-start.12 = (f32[16,768]{1,0:T(8,128)S(1)}, f32[16,768]{1,0:T(8,128)S(1)}, u32[]{:S(2)}, u32[]{:S(2)}) collective-permute-start(f32[16,768]{1,0:T(8,128)S(1)} %shard_map.59), channel_id=1, source_target_pairs={{0,16},{8,24},{1,17},{9,25},{16,0},{24,8},{17,1},{25,9},{32,48},{4... | collective-permute-start | bytes 147464 | tf_op jit(solution)/shard_map/ppermute | solution.py:24
  108.9 27.7 %all-to-all-start.2 = ((f32[128,8,128]{2,1,0:T(8,128)}), f32[128,8,128]{2,1,0:T(8,128)S(1)}, u32[]{:S(2)}, u32[]{:S(2)}) async-start(f32[128,8,128]{2,1,0:T(8,128)} %shard_map.61), calls=%async_computation.2 | async-start | bytes 1048576 | tf_op jit(solution)/shard_map/all_to_all | solution.py:347
  118.5 15.8 %collective-permute-start.17 = (f32[64,768]{1,0:T(8,128)S(1)}, f32[64,768]{1,0:T(8,128)S(1)}, u32[]{:S(2)}, u32[]{:S(2)}) collective-permute-start(f32[64,768]{1,0:T(8,128)S(1)} %pad_maximum_fusion), channel_id=1, source_target_pairs={{0,192},{8,200},{1,193},{9,201},{16,208},{24,216},{17,209},{25,217... | collective-permute-start | bytes 589832 | tf_op jit(solution)/shard_map/ppermute | solution.py:24
  120.4 13.9 %collective-permute-start.16 = (f32[64,768]{1,0:T(8,128)S(1)}, f32[64,768]{1,0:T(8,128)S(1)}, u32[]{:S(2)}, u32[]{:S(2)}) collective-permute-start(f32[64,768]{1,0:T(8,128)S(1)} %pad_maximum_fusion), channel_id=1, source_target_pairs={{0,128},{8,136},{1,129},{9,137},{16,144},{24,152},{17,145},{25,153... | collective-permute-start | bytes 589832 | tf_op jit(solution)/shard_map/ppermute | solution.py:24
  121.0 13.3 %collective-permute-start.15 = (f32[64,768]{1,0:T(8,128)S(1)}, f32[64,768]{1,0:T(8,128)S(1)}, u32[]{:S(2)}, u32[]{:S(2)}) collective-permute-start(f32[64,768]{1,0:T(8,128)S(1)} %pad_maximum_fusion), channel_id=1, source_target_pairs={{0,64},{8,72},{1,65},{9,73},{16,80},{24,88},{17,81},{25,89},{32,96... | collective-permute-start | bytes 589832 | tf_op jit(solution)/shard_map/ppermute | solution.py:24
  134.4 5.7 %collective-permute-start.18 = (f32[256,768]{1,0:T(8,128)S(1)}, f32[256,768]{1,0:T(8,128)S(1)}, u32[]{:S(2)}, u32[]{:S(2)}) collective-permute-start(f32[256,768]{1,0:T(8,128)S(1)} %constant_dynamic-update-slice_fusion.mine_ref), channel_id=1, source_target_pairs={{0,8},{8,0},{1,9},{9,1},{16,24},{24,16},{17,25},{25,17},{32,40},{4... | collective-permute-start | bytes 2359304 | tf_op jit(solution)/shard_map/ppermute | solution.py:24
  136.6 5.3 %collective-permute-start.19 = (f32[128,8,128]{2,1,0:T(8,128)S(1)}, f32[128,8,128]{2,1,0:T(8,128)S(1)}, u32[]{:S(2)}, u32[]{:S(2)}) collective-permute-start(f32[128,8,128]{2,1,0:T(8,128)S(1)} %all-to-all-done.2.mine_ref), channel_id=1, source_target_pairs={{0,8},{8,0},{1,9},{9,1},{16,24},{24,16},{17,25},{25,17},{32,40},{4... | collective-permute-start | bytes 1572872 | tf_op jit(solution)/shard_map/ppermute | solution.py:24

commit v4 on v3

--- a/solution.py
+++ b/solution.py
@@ -1,3 +1,4 @@
+import functools
 import itertools
 import math
 
@@ -164,16 +165,21 @@
 
 
 def codebook_kernel(
-    place_ref, all_books_ref, emb_t_ref, a_ref, b_ref, c_ref, d_ref, e_ref, out_ref, books_ref, sem
+    side, place_ref, all_books_ref, emb_t_ref, a_ref, b_ref, c_ref, d_ref, e_ref, *refs
 ):
+    out_ref, books_ref, sem = refs[-3:]
     subspaces, depth, codes = books_ref.shape
     first = (place_ref[1] * NZH + place_ref[3]) * subspaces
+    if side:
+        for xz in range(NX * NZL):
+            out_ref[xz * NC] = refs[0][xz * NC]
     copy = pltpu.make_async_copy(all_books_ref.at[pl.ds(first, subspaces)], books_ref, sem)
     copy.start()
     copy.wait()
     rows = emb_t_ref.shape[1]
     ones = jnp.where(lax.broadcasted_iota(jnp.int32, (2 * depth, rows), 0) < 3, 1.0, 0.0)
-    for m in range(subspaces):
+    half = subspaces // 2
+    for m in range(side * half, (side + 1) * half):
         at = slice(m * depth, (m + 1) * depth)
         recon = a_ref[at, :] + b_ref[at, :] + c_ref[at, :] + d_ref[at, :] + e_ref[at, :]
         r = emb_t_ref[at, :] - recon
@@ -302,27 +308,35 @@
         scratch=(pltpu.VMEM((width, rows_here), BF16),),
         flops=2 * rows_here * held * width,
     )
-    for step, move in enumerate((other_core, along_x(2), along_x(1), along_zl(2))):
+    for move in (other_core, along_x(2), along_x(1)):
         half = keep.shape[0] // 2
         got = hop(send, move)
         keep, send = call(halve_kernel, (shape((half, width + 128)),) * 2, (keep, got), limit=4)
-        if step == 2:
-            send, peer = lax.optimization_barrier((send, peer))
     peers = NX * NZL
-
     per = subspaces // cents
-    sums = call(
-        codebook_kernel,
-        shape((NX * NZL * NC, 8, codes)),
-        (place, codebooks, emb_t, mine[0], *got_mine, peer),
-        smem=1,
-        hbm_in=1,
-        scratch=(pltpu.VMEM((per, depth, codes), F32), pltpu.SemaphoreType.DMA),
-        flops=64 * rows_here * per * codes * 64,
-    )
-    sums, keep = lax.optimization_barrier((sums, keep))
+
+    def codebook_half(side, *more):
+        return call(
+            functools.partial(codebook_kernel, side),
+            shape((NX * NZL * NC, 8, codes)),
+            (place, codebooks, emb_t, mine[0], *got_mine, peer, *more),
+            smem=1,
+            hbm_in=1,
+            scratch=(pltpu.VMEM((per, depth, codes), F32), pltpu.SemaphoreType.DMA),
+            flops=64 * rows_here * per * codes * 64,
+        )
+
+    send, peer = lax.optimization_barrier((send, peer))
+    got = hop(send, along_zl(2))
+    first_sums = codebook_half(0)
+    first_sums, got = lax.optimization_barrier((first_sums, got))
+    half = keep.shape[0] // 2
+    keep, send = call(halve_kernel, (shape((half, width + 128)),) * 2, (keep, got), limit=4)
+    got = hop(send, along_zl(1))
+    sums = codebook_half(1, first_sums)
+    sums, got = lax.optimization_barrier((sums, got))
     new = call(
-        centroid_kernel, shape((half, width)), (keep, hop(send, along_zl(1)), old), limit=4
+        centroid_kernel, shape((half, width)), (keep, got, old), limit=4
     )
     new_z = jnp.concatenate([new] + [hop(new, along_zl(k)) for k in (1, 2, 3)], axis=0)
     all_parts = lax.all_to_all(sums, "rows", 0, 0, tiled=True)
@@ -339,7 +353,6 @@
         scratch=(pltpu.VMEM((share, codes), F32), pltpu.SemaphoreType.DMA),
     )
     new_x = jnp.concatenate([new_z] + [hop(new_z, along_x(k)) for k in (1, 2, 3)], axis=0)
-    tile, new_z = lax.optimization_barrier((tile, new_z))
     new_other = hop(new_x, other_core)
     new_centroids = call(
         centroids_kernel, shape((held, width)), (place, new_x, new_other), smem=1

time: 144 us -> 143 us (level)
  starting transfers between devices: 52.7 us -> 44.9 us
  waiting for transfers between devices: 46.1 us -> 51.7 us
    all_to_all x1, waiting for transfers between devices: 0.01 us -> 10.1 us  [body(): all_parts = lax.all_to_all(sums, 'rows', 0, 0, tiled=True)]
    ppermute x20, waiting for transfers between devices: 46 us -> 38.6 us  [hop(): return lax.ppermute(value, BOTH, pairs)]
    ppermute x20, starting transfers between devices: 35.3 us -> 28.2 us  [hop(): return lax.ppermute(value, BOTH, pairs)]
    all_to_all x1, waiting for transfers between devices: 0.01 us -> 3.05 us  [body(): lax.all_to_all(tile, BOTH, 0, 0, tiled=True, axis_index_groups=same_core)]
    pallas_call x13 -> x14, Pallas kernels: 20.6 us -> 21.5 us  [call(): pl.pallas_call(kernel, out_shape=out, in_specs=specs, out_specs=jax.tree....]
  transfers between devices with their start and end apart: 22 -> 22, of which waited for: 7 -> 7; matrix products, arithmetic and copies ran while one was open for 0% -> 0% of each run, Pallas kernels for 8% -> 10%
where the time goes in v4:
time: 143 us; the launch traced here: 142 us
  waiting for transfers between devices  51.7 us (36%)
  starting transfers between devices  44.9 us (31%)
  Pallas kernels  21.5 us (15%)
  blocking collectives  20.6 us (14%)
  local copies, waits for them, and re-layouts  2.7 us (2%)
    ppermute x20, waiting for transfers between devices, hop(): return lax.ppermute(value, BOTH, pairs)  38.6 us
    ppermute x20, starting transfers between devices, hop(): return lax.ppermute(value, BOTH, pairs)  28.2 us
    pallas_call x14, Pallas kernels, call(): pl.pallas_call(kernel, out_shape=out, in_specs=specs, out_specs=jax.tree....  21.5 us
    all_to_all x1, blocking collectives, body(): stats = lax.all_to_all(stat, 'cent', 0, 0, tiled=True)  20.6 us
    all_to_all x1, waiting for transfers between devices, body(): all_parts = lax.all_to_all(sums, 'rows', 0, 0, tiled=True)  10.1 us
    all_to_all x1, starting transfers between devices, body(): all_parts = lax.all_to_all(sums, 'rows', 0, 0, tiled=True)  8.47 us
    all_to_all x1, starting transfers between devices, body(): lax.all_to_all(tile, BOTH, 0, 0, tiled=True, axis_index_groups=same_core)  8.28 us
    all_to_all x1, waiting for transfers between devices, body(): lax.all_to_all(tile, BOTH, 0, 0, tiled=True, axis_index_groups=same_core)  3.05 us
  transfers between devices with their start and end apart: 22, of which 7 were waited for; matrix products, arithmetic and copies ran while one was open for 0% of the time, Pallas kernels for 10%

profile of v4, /device:TPU:1, one launch (start us, length us, event | category | flops | bytes accessed | tf_op | source)
XLA Modules:
  0.0 142.3 jit_solution(11131625861321011404)
XLA Ops:
  0.7 0.1 stack.23.place_ref
  0.8 0.0 copy-start.1
  0.8 1.4 copy-done.1
  2.2 0.0 copy-start.2
  2.2 1.1 copy-done.2
  3.3 2.1 %shard_map.50 = (f32[512,1024]{1,0:T(8,128)S(1)}, f32[8,16,128]{2,1,0:T(8,128)S(1)}, bf16[768,512]{1,0:T(8,128)(2,1)S(1)}, f32[16,768]{1,0:T(8,128)S(1)}) custom-call(s32[5]{0:T(128)S(1)} %stack.23.place_ref, bf16[1024,768]{1,0:T(8,128)(2,1)S(1)} %copy-done.1, bf16[512,768]{1,0:T(8,128)(2,1)S(1)} %copy-done.2), custom_call_target="tpu_custom_call" | custom-call | flops 805306368 | bytes 4718632 | tf_op jit(solution)/shard_map/pallas_call | solution.py:53
  5.4 20.6 %all_to_all.15.stat_ref = f32[8,16,128]{2,1,0:T(8,128)S(1)} all-to-all(f32[8,16,128]{2,1,0:T(8,128)S(1)} %get-tuple-element.34.mine_ref), channel_id=1, replica_groups=mesh['rows'=32,'cent'=8] {'cent'}, dimensions={0} | all-to-all | bytes 131072 | tf_op jit(solution)/shard_map/all_to_all | solution.py:289
  26.0 2.2 %shard_map.51 = (bf16[512,1024]{1,0:T(8,128)(2,1)S(1)}, f32[512,128]{1,0:T(8,128)S(1)}, f32[96,1024]{1,0:T(8,128)S(1)}, f32[96,1024]{1,0:T(8,128)S(1)}, f32[96,1...) custom-call(s32[5]{0:T(128)S(1)} %stack.23.place_ref, ...), custom_call_target="tpu_custom_call" | custom-call | flops 805306368 | bytes 6029352 | tf_op jit(solution)/shard_map/pallas_call | solution.py:53
  28.1 1.6 %shard_map.52 = (f32[256,896]{1,0:T(8,128)S(1)}, f32[256,896]{1,0:T(8,128)S(1)}, f32[96,1024]{1,0:T(8,128)S(1)}) custom-call(s32[5]{0:T(128)S(1)} %stack.23.place_ref, bf16[512,1024]{1,0:T(8,128)(2,1)S(1)} %get-tuple-element.36.wb_ref, f32[512,128]{1,0:T(8,128)S(1)} %get-tuple-element.37.count_ref, bf16[1024,768]{1,0:T(8,128)(2,1)S(1)} %copy-done.1), custom_call_target="tpu_custom_call" | custom-call | flops 805306368 | bytes 5767208 | tf_op jit(solution)/shard_map/pallas_call | solution.py:53
  29.7 2.2 %collective-permute-start = (f32[256,896]{1,0:T(8,128)S(1)}, f32[256,896]{1,0:T(8,128)S(1)}, u32[]{:S(2)}, u32[]{:S(2)}) collective-permute-start(f32[256,896]{1,0:T(8,128)S(1)} %get-tuple-element.39), channel_id=1, source_target_pairs={{0,8},{8,0},{1,9},{9,1},{16,24},{24,16},{17,25},{25,17},{32,40},{4... | collective-permute-start | bytes 2752520 | tf_op jit(solution)/shard_map/ppermute | solution.py:25
  31.9 0.3 collective-permute-start.6
  32.2 2.4 %collective-permute-start.7 = (f32[96,1024]{1,0:T(8,128)S(1)}, f32[96,1024]{1,0:T(8,128)S(1)}, u32[]{:S(2)}, u32[]{:S(2)}) collective-permute-start(f32[96,1024]{1,0:T(8,128)S(1)} %get-tuple-element.53), channel_id=1, source_target_pairs={{0,6},{8,14},{1,7},{9,15},{16,22},{24,30},{17,23},{25,31},{32,38},... | collective-permute-start | bytes 1179656 | tf_op jit(solution)/shard_map/ppermute | solution.py:25
  34.6 0.0 collective-permute-start.8
  34.6 0.0 collective-permute-done.got_ref
  34.6 0.1 shard_map.53
  34.7 2.8 %collective-permute-start.1 = (f32[128,896]{1,0:T(8,128)S(1)}, f32[128,896]{1,0:T(8,128)S(1)}, u32[]{:S(2)}, u32[]{:S(2)}) collective-permute-start(f32[128,896]{1,0:T(8,128)S(1)} %get-tuple-element.41), channel_id=1, source_target_pairs={{0,128},{8,136},{1,129},{9,137},{16,144},{24,152},{17,145},{25,153... | collective-permute-start | bytes 1376264 | tf_op jit(solution)/shard_map/ppermute | solution.py:25
  37.6 14.7 %collective-permute-done.6.b_ref = f32[96,1024]{1,0:T(8,128)S(1)} collective-permute-done((f32[96,1024]{1,0:T(8,128)S(1)}, f32[96,1024]{1,0:T(8,128)S(1)}, u32[]{:S(2)}, u32[]{:S(2)}) %collective-permute-start.6) | collective-permute-done | bytes 393248 | tf_op jit(solution)/shard_map/ppermute | solution.py:25
  52.2 0.0 collective-permute-done.7.c_ref
  52.2 0.0 collective-permute-done.8.d_ref
  52.2 0.0 copy-start
  52.2 0.1 shard_map.56
  52.3 0.6 collective-permute-start.9
  52.9 0.6 collective-permute-start.3
  53.5 2.1 %collective-permute-start.4 = (f32[96,1024]{1,0:T(8,128)S(1)}, f32[96,1024]{1,0:T(8,128)S(1)}, u32[]{:S(2)}, u32[]{:S(2)}) collective-permute-start(f32[96,1024]{1,0:T(8,128)S(1)} %get-tuple-element.48), channel_id=1, source_target_pairs={{0,6},{8,14},{1,7},{9,15},{16,22},{24,30},{17,23},{25,31},{32,38},... | collective-permute-start | bytes 1179656 | tf_op jit(solution)/shard_map/ppermute | solution.py:25
  55.6 0.9 collective-permute-start.5
  56.4 0.0 collective-permute-done.1.got_ref
  56.5 1.3 collective-permute-start.2
  57.8 4.0 %collective-permute-done.2.got_ref = f32[64,896]{1,0:T(8,128)S(1)} collective-permute-done((f32[64,896]{1,0:T(8,128)S(1)}, f32[64,896]{1,0:T(8,128)S(1)}, u32[]{:S(2)}, u32[]{:S(2)}) %collective-permute-start.2) | collective-permute-done | bytes 229408 | tf_op jit(solution)/shard_map/ppermute | solution.py:25
  61.8 6.2 %collective-permute-done.9.e_ref = f32[96,1024]{1,0:T(8,128)S(1)} collective-permute-done((f32[96,1024]{1,0:T(8,128)S(1)}, f32[96,1024]{1,0:T(8,128)S(1)}, u32[]{:S(2)}, u32[]{:S(2)}) %collective-permute-start.9) | collective-permute-done | bytes 393248 | tf_op jit(solution)/shard_map/ppermute | solution.py:25
  68.0 7.8 %collective-permute-start.10 = (f32[32,896]{1,0:T(8,128)S(1)}, f32[32,896]{1,0:T(8,128)S(1)}, u32[]{:S(2)}, u32[]{:S(2)}) collective-permute-start(f32[32,896]{1,0:T(8,128)S(1)} %get-tuple-element.56), channel_id=1, source_target_pairs={{0,32},{8,40},{1,33},{9,41},{16,48},{24,56},{17,49},{25,57},{32,0}... | collective-permute-start | bytes 344072 | tf_op jit(solution)/shard_map/ppermute | solution.py:25
  75.8 0.0 collective-permute-done.3.b_ref
  75.8 0.0 collective-permute-done.4.c_ref
  75.8 0.0 collective-permute-done.5.d_ref
  75.8 0.0 copy-done
  75.8 4.8 %shard_map.57.refs_0_ = f32[32,8,256]{2,1,0:T(8,128)S(1)} custom-call(s32[5]{0:T(128)S(1)} %stack.23.place_ref, f32[96,8,256]{2,1,0:T(8,128)S(1)} %copy-done, f32[96,1024]{1,0:T(8,128)S(1)} %get-tuple-element.45.emb_t_ref, f32[96,1024]{1,0:T(8,128)S(1)} %get-tuple-element.46.a_ref, f32[96,1024]{1,0:T(8,128)S(1)} %collective-permute-done.3.b_ref, ...), custom_call_target="tpu_custom_call" | custom-call | flops 12884901888 | bytes 6291496 | tf_op jit(solution)/shard_map/pallas_call | solution.py:53
  80.6 0.0 collective-permute-done.10.got_ref
  80.6 0.1 collective-permute-start.11
  80.7 5.5 %shard_map.59 = f32[32,8,256]{2,1,0:T(8,128)} custom-call(s32[5]{0:T(128)S(1)} %stack.23.place_ref, f32[96,8,256]{2,1,0:T(8,128)S(1)} %copy-done, f32[96,1024]{1,0:T(8,128)S(1)} %get-tuple-element.45.emb_t_ref, f32[96,1024]{1,0:T(8,128)S(1)} %get-tuple-element.46.a_ref, f32[96,1024]{1,0:T(8,128)S(1)} %collective-permute-done.3.b_ref, ...), custom_call_target="tpu_custom_call" | custom-call | flops 12884901888 | bytes 6815784 | tf_op jit(solution)/shard_map/pallas_call | solution.py:53
  86.2 0.0 collective-permute-done.11.got_ref
  86.2 8.5 %all-to-all-start.1 = ((f32[32,8,256]{2,1,0:T(8,128)}), f32[32,8,256]{2,1,0:T(8,128)S(1)}, u32[]{:S(2)}, u32[]{:S(2)}) async-start(f32[32,8,256]{2,1,0:T(8,128)} %shard_map.59), calls=%async_computation.1 | async-start | bytes 524288 | tf_op jit(solution)/shard_map/all_to_all | solution.py:342
  94.7 0.1 shard_map.60
  94.8 3.2 %collective-permute-start.14 = (f32[16,768]{1,0:T(8,128)S(1)}, f32[16,768]{1,0:T(8,128)S(1)}, u32[]{:S(2)}, u32[]{:S(2)}) collective-permute-start(f32[16,768]{1,0:T(8,128)S(1)} %shard_map.60), channel_id=1, source_target_pairs={{0,48},{8,56},{1,49},{9,57},{16,32},{24,40},{17,33},{25,41},{32,16... | collective-permute-start | bytes 147464 | tf_op jit(solution)/shard_map/ppermute | solution.py:25
  98.0 0.0 collective-permute-start.13
  98.0 0.4 collective-permute-start.12
  98.4 10.1 %all-to-all-done.1.parts_ref = f32[32,8,256]{2,1,0:T(8,128)S(1)} async-done(((f32[32,8,256]{2,1,0:T(8,128)}), f32[32,8,256]{2,1,0:T(8,128)S(1)}, u32[]{:S(2)}, u32[]{:S(2)}) %all-to-all-start.1) | async-done | bytes 262176 | tf_op jit(solution)/shard_map/all_to_all | solution.py:342
  108.5 1.6 %shard_map.62 = f32[128,8,128]{2,1,0:T(8,128)} custom-call(s32[5]{0:T(128)S(1)} %stack.23.place_ref, f32[768,256]{1,0:T(8,128)S(1)} %bitcast.7, f32[32,8,256]{2,1,0:T(8,128)S(1)} %all-to-all-done.1.parts_ref), custom_call_target="tpu_custom_call" | custom-call | bytes 2097192 | tf_op jit(solution)/shard_map/pallas_call | solution.py:53
  110.0 8.3 %all-to-all-start.2 = ((f32[128,8,128]{2,1,0:T(8,128)}), f32[128,8,128]{2,1,0:T(8,128)S(1)}, u32[]{:S(2)}, u32[]{:S(2)}) async-start(f32[128,8,128]{2,1,0:T(8,128)} %shard_map.62), calls=%async_computation.2 | async-start | bytes 1048576 | tf_op jit(solution)/shard_map/all_to_all | solution.py:360
  118.3 0.0 collective-permute-done.14
  118.3 0.0 collective-permute-done.13
  118.4 0.0 collective-permute-done.12
  118.4 1.9 %collective-permute-start.17 = (f32[64,768]{1,0:T(8,128)S(1)}, f32[64,768]{1,0:T(8,128)S(1)}, u32[]{:S(2)}, u32[]{:S(2)}) collective-permute-start(f32[64,768]{1,0:T(8,128)S(1)} %pad_maximum_fusion), channel_id=1, source_target_pairs={{0,192},{8,200},{1,193},{9,201},{16,208},{24,216},{17,209},{25,217... | collective-permute-start | bytes 589832 | tf_op jit(solution)/shard_map/ppermute | solution.py:25
  120.3 0.6 collective-permute-start.16
  120.9 0.9 collective-permute-start.15
  121.8 13.5 %collective-permute-done.15 = f32[64,768]{1,0:T(8,128)S(1)} collective-permute-done((f32[64,768]{1,0:T(8,128)S(1)}, f32[64,768]{1,0:T(8,128)S(1)}, u32[]{:S(2)}, u32[]{:S(2)}) %collective-permute-start.15) | collective-permute-done | bytes 196640 | tf_op jit(solution)/shard_map/ppermute | solution.py:25
  135.3 0.0 collective-permute-done.16
  135.4 0.0 collective-permute-done.17
  135.4 0.3 collective-permute-start.18
  135.7 3.1 %all-to-all-done.2.mine_ref = f32[128,8,128]{2,1,0:T(8,128)S(1)} async-done(((f32[128,8,128]{2,1,0:T(8,128)}), f32[128,8,128]{2,1,0:T(8,128)S(1)}, u32[]{:S(2)}, u32[]{:S(2)}) %all-to-all-start.2) | async-done | bytes 524320 | tf_op jit(solution)/shard_map/all_to_all | solution.py:360
  138.7 0.0 collective-permute-start.19
  138.7 0.0 collective-permute-done.18.theirs_ref
  138.7 1.8 %shard_map.61 = f32[512,768]{1,0:T(8,128)} custom-call(s32[5]{0:T(128)S(1)} %stack.23.place_ref, f32[256,768]{1,0:T(8,128)S(1)} %constant_dynamic-update-slice_fusion.mine_ref, f32[256,768]{1,0:T(8,128)S(1)} %collective-permute-done.18.theirs_ref), custom_call_target="tpu_custom_call" | custom-call | bytes 3145768 | tf_op jit(solution)/shard_map/pallas_call | solution.py:53
  140.5 0.1 collective-permute-done.19.theirs_ref
  140.6 1.7 %shard_map.63 = f32[768,256]{1,0:T(8,128)} custom-call(s32[5]{0:T(128)S(1)} %stack.23.place_ref, f32[128,8,128]{2,1,0:T(8,128)S(1)} %all-to-all-done.2.mine_ref, f32[128,8,128]{2,1,0:T(8,128)S(1)} %collective-permute-done.19.theirs_ref), custom_call_target="tpu_custom_call" | custom-call | bytes 2097192 | tf_op jit(solution)/shard_map/pallas_call | solution.py:53
  (11 shorter events, 0.2 us)
Async XLA Ops:
  0.8 1.4 copy-start.1
  2.2 1.1 copy-start.2
  29.7 4.9 %collective-permute-start = (f32[256,896]{1,0:T(8,128)S(1)}, f32[256,896]{1,0:T(8,128)S(1)}, u32[]{:S(2)}, u32[]{:S(2)}) collective-permute-start(f32[256,896]{1,0:T(8,128)S(1)} %get-tuple-element.39), channel_id=1, source_target_pairs={{0,8},{8,0},{1,9},{9,1},{16,24},{24,16},{17,25},{25,17},{32,40},{4... | collective-permute-start | bytes 2752520 | tf_op jit(solution)/shard_map/ppermute | solution.py:25
  31.9 20.3 %collective-permute-start.6 = (f32[96,1024]{1,0:T(8,128)S(1)}, f32[96,1024]{1,0:T(8,128)S(1)}, u32[]{:S(2)}, u32[]{:S(2)}) collective-permute-start(f32[96,1024]{1,0:T(8,128)S(1)} %get-tuple-element.52), channel_id=1, source_target_pairs={{0,2},{8,10},{1,3},{9,11},{16,18},{24,26},{17,19},{25,27},{32,34},... | collective-permute-start | bytes 1179656 | tf_op jit(solution)/shard_map/ppermute | solution.py:25
  32.2 20.0 %collective-permute-start.7 = (f32[96,1024]{1,0:T(8,128)S(1)}, f32[96,1024]{1,0:T(8,128)S(1)}, u32[]{:S(2)}, u32[]{:S(2)}) collective-permute-start(f32[96,1024]{1,0:T(8,128)S(1)} %get-tuple-element.53), channel_id=1, source_target_pairs={{0,6},{8,14},{1,7},{9,15},{16,22},{24,30},{17,23},{25,31},{32,38},... | collective-permute-start | bytes 1179656 | tf_op jit(solution)/shard_map/ppermute | solution.py:25
  34.6 17.6 %collective-permute-start.8 = (f32[96,1024]{1,0:T(8,128)S(1)}, f32[96,1024]{1,0:T(8,128)S(1)}, u32[]{:S(2)}, u32[]{:S(2)}) collective-permute-start(f32[96,1024]{1,0:T(8,128)S(1)} %get-tuple-element.54), channel_id=1, source_target_pairs={{0,4},{8,12},{1,5},{9,13},{16,20},{24,28},{17,21},{25,29},{32,36},... | collective-permute-start | bytes 1179656 | tf_op jit(solution)/shard_map/ppermute | solution.py:25
  34.7 21.7 %collective-permute-start.1 = (f32[128,896]{1,0:T(8,128)S(1)}, f32[128,896]{1,0:T(8,128)S(1)}, u32[]{:S(2)}, u32[]{:S(2)}) collective-permute-start(f32[128,896]{1,0:T(8,128)S(1)} %get-tuple-element.41), channel_id=1, source_target_pairs={{0,128},{8,136},{1,129},{9,137},{16,144},{24,152},{17,145},{25,153... | collective-permute-start | bytes 1376264 | tf_op jit(solution)/shard_map/ppermute | solution.py:25
  52.2 23.5 %copy-start = (f32[96,8,256]{2,1,0:T(8,128)S(1)}, f32[96,8,256]{2,1,0:T(8,128)}, u32[]{:S(2)}) copy-start(f32[96,8,256]{2,1,0:T(8,128)} %all_books_ref.3) | copy-start | bytes 2359300
  52.3 15.7 %collective-permute-start.9 = (f32[96,1024]{1,0:T(8,128)S(1)}, f32[96,1024]{1,0:T(8,128)S(1)}, u32[]{:S(2)}, u32[]{:S(2)}) collective-permute-start(f32[96,1024]{1,0:T(8,128)S(1)} %shard_map.56), channel_id=1, source_target_pairs={{0,1},{8,9},{1,0},{9,8},{16,17},{24,25},{17,16},{25,24},{32,33},{4... | collective-permute-start | bytes 1179656 | tf_op jit(solution)/shard_map/ppermute | solution.py:25
  52.9 22.9 %collective-permute-start.3 = (f32[96,1024]{1,0:T(8,128)S(1)}, f32[96,1024]{1,0:T(8,128)S(1)}, u32[]{:S(2)}, u32[]{:S(2)}) collective-permute-start(f32[96,1024]{1,0:T(8,128)S(1)} %get-tuple-element.47), channel_id=1, source_target_pairs={{0,2},{8,10},{1,3},{9,11},{16,18},{24,26},{17,19},{25,27},{32,34},... | collective-permute-start | bytes 1179656 | tf_op jit(solution)/shard_map/ppermute | solution.py:25
  53.5 22.3 %collective-permute-start.4 = (f32[96,1024]{1,0:T(8,128)S(1)}, f32[96,1024]{1,0:T(8,128)S(1)}, u32[]{:S(2)}, u32[]{:S(2)}) collective-permute-start(f32[96,1024]{1,0:T(8,128)S(1)} %get-tuple-element.48), channel_id=1, source_target_pairs={{0,6},{8,14},{1,7},{9,15},{16,22},{24,30},{17,23},{25,31},{32,38},... | collective-permute-start | bytes 1179656 | tf_op jit(solution)/shard_map/ppermute | solution.py:25
  55.6 20.2 %collective-permute-start.5 = (f32[96,1024]{1,0:T(8,128)S(1)}, f32[96,1024]{1,0:T(8,128)S(1)}, u32[]{:S(2)}, u32[]{:S(2)}) collective-permute-start(f32[96,1024]{1,0:T(8,128)S(1)} %get-tuple-element.49), channel_id=1, source_target_pairs={{0,4},{8,12},{1,5},{9,13},{16,20},{24,28},{17,21},{25,29},{32,36},... | collective-permute-start | bytes 1179656 | tf_op jit(solution)/shard_map/ppermute | solution.py:25
  56.5 5.3 %collective-permute-start.2 = (f32[64,896]{1,0:T(8,128)S(1)}, f32[64,896]{1,0:T(8,128)S(1)}, u32[]{:S(2)}, u32[]{:S(2)}) collective-permute-start(f32[64,896]{1,0:T(8,128)S(1)} %get-tuple-element.43), channel_id=1, source_target_pairs={{0,64},{8,72},{1,65},{9,73},{16,80},{24,88},{17,81},{25,89},{32,96... | collective-permute-start | bytes 688136 | tf_op jit(solution)/shard_map/ppermute | solution.py:25
  68.0 12.6 %collective-permute-start.10 = (f32[32,896]{1,0:T(8,128)S(1)}, f32[32,896]{1,0:T(8,128)S(1)}, u32[]{:S(2)}, u32[]{:S(2)}) collective-permute-start(f32[32,896]{1,0:T(8,128)S(1)} %get-tuple-element.56), channel_id=1, source_target_pairs={{0,32},{8,40},{1,33},{9,41},{16,48},{24,56},{17,49},{25,57},{32,0}... | collective-permute-start | bytes 344072 | tf_op jit(solution)/shard_map/ppermute | solution.py:25
  80.6 5.6 %collective-permute-start.11 = (f32[16,896]{1,0:T(8,128)S(1)}, f32[16,896]{1,0:T(8,128)S(1)}, u32[]{:S(2)}, u32[]{:S(2)}) collective-permute-start(f32[16,896]{1,0:T(8,128)S(1)} %get-tuple-element.60), channel_id=1, source_target_pairs={{0,16},{8,24},{1,17},{9,25},{16,0},{24,8},{17,1},{25,9},{32,48},{4... | collective-permute-start | bytes 172040 | tf_op jit(solution)/shard_map/ppermute | solution.py:25
  86.2 22.2 %all-to-all-start.1 = ((f32[32,8,256]{2,1,0:T(8,128)}), f32[32,8,256]{2,1,0:T(8,128)S(1)}, u32[]{:S(2)}, u32[]{:S(2)}) async-start(f32[32,8,256]{2,1,0:T(8,128)} %shard_map.59), calls=%async_computation.1 | async-start | bytes 524288 | tf_op jit(solution)/shard_map/all_to_all | solution.py:342
  94.8 23.5 %collective-permute-start.14 = (f32[16,768]{1,0:T(8,128)S(1)}, f32[16,768]{1,0:T(8,128)S(1)}, u32[]{:S(2)}, u32[]{:S(2)}) collective-permute-start(f32[16,768]{1,0:T(8,128)S(1)} %shard_map.60), channel_id=1, source_target_pairs={{0,48},{8,56},{1,49},{9,57},{16,32},{24,40},{17,33},{25,41},{32,16... | collective-permute-start | bytes 147464 | tf_op jit(solution)/shard_map/ppermute | solution.py:25
  98.0 20.3 %collective-permute-start.13 = (f32[16,768]{1,0:T(8,128)S(1)}, f32[16,768]{1,0:T(8,128)S(1)}, u32[]{:S(2)}, u32[]{:S(2)}) collective-permute-start(f32[16,768]{1,0:T(8,128)S(1)} %shard_map.60), channel_id=1, source_target_pairs={{0,32},{8,40},{1,33},{9,41},{16,48},{24,56},{17,49},{25,57},{32,0}... | collective-permute-start | bytes 147464 | tf_op jit(solution)/shard_map/ppermute | solution.py:25
  98.0 20.3 %collective-permute-start.12 = (f32[16,768]{1,0:T(8,128)S(1)}, f32[16,768]{1,0:T(8,128)S(1)}, u32[]{:S(2)}, u32[]{:S(2)}) collective-permute-start(f32[16,768]{1,0:T(8,128)S(1)} %shard_map.60), channel_id=1, source_target_pairs={{0,16},{8,24},{1,17},{9,25},{16,0},{24,8},{17,1},{25,9},{32,48},{4... | collective-permute-start | bytes 147464 | tf_op jit(solution)/shard_map/ppermute | solution.py:25
  110.0 28.7 %all-to-all-start.2 = ((f32[128,8,128]{2,1,0:T(8,128)}), f32[128,8,128]{2,1,0:T(8,128)S(1)}, u32[]{:S(2)}, u32[]{:S(2)}) async-start(f32[128,8,128]{2,1,0:T(8,128)} %shard_map.62), calls=%async_computation.2 | async-start | bytes 1048576 | tf_op jit(solution)/shard_map/all_to_all | solution.py:360
  118.4 17.0 %collective-permute-start.17 = (f32[64,768]{1,0:T(8,128)S(1)}, f32[64,768]{1,0:T(8,128)S(1)}, u32[]{:S(2)}, u32[]{:S(2)}) collective-permute-start(f32[64,768]{1,0:T(8,128)S(1)} %pad_maximum_fusion), channel_id=1, source_target_pairs={{0,192},{8,200},{1,193},{9,201},{16,208},{24,216},{17,209},{25,217... | collective-permute-start | bytes 589832 | tf_op jit(solution)/shard_map/ppermute | solution.py:25
  120.3 15.1 %collective-permute-start.16 = (f32[64,768]{1,0:T(8,128)S(1)}, f32[64,768]{1,0:T(8,128)S(1)}, u32[]{:S(2)}, u32[]{:S(2)}) collective-permute-start(f32[64,768]{1,0:T(8,128)S(1)} %pad_maximum_fusion), channel_id=1, source_target_pairs={{0,128},{8,136},{1,129},{9,137},{16,144},{24,152},{17,145},{25,153... | collective-permute-start | bytes 589832 | tf_op jit(solution)/shard_map/ppermute | solution.py:25
  120.9 14.4 %collective-permute-start.15 = (f32[64,768]{1,0:T(8,128)S(1)}, f32[64,768]{1,0:T(8,128)S(1)}, u32[]{:S(2)}, u32[]{:S(2)}) collective-permute-start(f32[64,768]{1,0:T(8,128)S(1)} %pad_maximum_fusion), channel_id=1, source_target_pairs={{0,64},{8,72},{1,65},{9,73},{16,80},{24,88},{17,81},{25,89},{32,96... | collective-permute-start | bytes 589832 | tf_op jit(solution)/shard_map/ppermute | solution.py:25
  135.4 3.3 %collective-permute-start.18 = (f32[256,768]{1,0:T(8,128)S(1)}, f32[256,768]{1,0:T(8,128)S(1)}, u32[]{:S(2)}, u32[]{:S(2)}) collective-permute-start(f32[256,768]{1,0:T(8,128)S(1)} %constant_dynamic-update-slice_fusion.mine_ref), channel_id=1, source_target_pairs={{0,8},{8,0},{1,9},{9,1},{16,24},{24,16},{17,25},{25,17},{32,40},{4... | collective-permute-start | bytes 2359304 | tf_op jit(solution)/shard_map/ppermute | solution.py:25
  138.7 1.9 %collective-permute-start.19 = (f32[128,8,128]{2,1,0:T(8,128)S(1)}, f32[128,8,128]{2,1,0:T(8,128)S(1)}, u32[]{:S(2)}, u32[]{:S(2)}) collective-permute-start(f32[128,8,128]{2,1,0:T(8,128)S(1)} %all-to-all-done.2.mine_ref), channel_id=1, source_target_pairs={{0,8},{8,0},{1,9},{9,1},{16,24},{24,16},{17,25},{25,17},{32,40},{4... | collective-permute-start | bytes 1572872 | tf_op jit(solution)/shard_map/ppermute | solution.py:25

commit v5 on v3

--- a/solution.py
+++ b/solution.py
@@ -191,14 +191,10 @@
         i0, i1, i2 = pieces(jnp.broadcast_to(inv, (depth, rows)))
         scaled = jnp.concatenate([q0, q1, q2, i0, i1, i2], axis=0).astype(BF16)
         p_hi = p.astype(BF16)
-        p_lo = (p - p_hi.astype(F32)).astype(BF16)
         high = dot(scaled, p_hi, 1, 1)
-        low = dot(scaled, p_lo, 1, 1)
-        mass = high[:depth] + (high[depth : 2 * depth] + (high[2 * depth : 3 * depth] + low[:depth]))
-        mass = mass + low[depth : 2 * depth]
+        mass = high[:depth] + (high[depth : 2 * depth] + high[2 * depth : 3 * depth])
         o = 3 * depth
-        count = high[o : o + 1] + (high[o + depth : o + depth + 1] + low[o : o + 1])
-        count = count + high[o + 2 * depth : o + 2 * depth + 1] + low[o + depth : o + depth + 1]
+        count = high[o : o + 1] + (high[o + depth : o + depth + 1] + high[o + 2 * depth : o + 2 * depth + 1])
         for d in range(depth):
             owner, slot = divmod(m * depth + d, 3)
             core, xz = divmod(owner, NX * NZL)
@@ -339,7 +335,6 @@
         scratch=(pltpu.VMEM((share, codes), F32), pltpu.SemaphoreType.DMA),
     )
     new_x = jnp.concatenate([new_z] + [hop(new_z, along_x(k)) for k in (1, 2, 3)], axis=0)
-    tile, new_z = lax.optimization_barrier((tile, new_z))
     new_other = hop(new_x, other_core)
     new_centroids = call(
         centroids_kernel, shape((held, width)), (place, new_x, new_other), smem=1

time: 144 us -> 138 us (0.958)
  Pallas kernels: 20.6 us -> 17 us
  waiting for transfers between devices: 46.1 us -> 43.5 us
    ppermute x20, waiting for transfers between devices: 46 us -> 42.3 us  [hop(): return lax.ppermute(value, BOTH, pairs)]
    pallas_call x13, Pallas kernels: 20.6 us -> 17 us  [call(): pl.pallas_call(kernel, out_shape=out, in_specs=specs, out_specs=jax.tree....]
  transfers between devices with their start and end apart: 22 -> 22, of which waited for: 7 -> 8; matrix products, arithmetic and copies ran while one was open for 0% -> 0% of each run, Pallas kernels for 8% -> 7%
where the time goes in v5:
time: 138 us
  starting transfers between devices  52.8 us (38%)
  waiting for transfers between devices  43.5 us (32%)
  blocking collectives  20.6 us (15%)
  Pallas kernels  17 us (12%)
  local copies, waits for them, and re-layouts  2.69 us (2%)
    ppermute x20, waiting for transfers between devices, hop(): return lax.ppermute(value, BOTH, pairs)  42.3 us
    ppermute x20, starting transfers between devices, hop(): return lax.ppermute(value, BOTH, pairs)  34.7 us
    all_to_all x1, blocking collectives, body(): stats = lax.all_to_all(stat, 'cent', 0, 0, tiled=True)  20.6 us
    pallas_call x13, Pallas kernels, call(): pl.pallas_call(kernel, out_shape=out, in_specs=specs, out_specs=jax.tree....  17 us
    all_to_all x1, starting transfers between devices, body(): lax.all_to_all(tile, BOTH, 0, 0, tiled=True, axis_index_groups=same_core)  10.3 us
    all_to_all x1, starting transfers between devices, body(): all_parts = lax.all_to_all(sums, 'rows', 0, 0, tiled=True)  7.81 us
  transfers between devices with their start and end apart: 22, of which 8 were waited for; matrix products, arithmetic and copies ran while one was open for 0% of the time, Pallas kernels for 7%

profile of v5, /device:TPU:1, one launch (start us, length us, event | category | flops | bytes accessed | tf_op | source)
XLA Modules:
  0.0 137.5 jit_solution(748554755049488607)
XLA Ops:
  0.7 0.1 stack.23.place_ref
  0.8 0.0 copy-start.1
  0.8 1.4 %copy-done.1 = bf16[1024,768]{1,0:T(8,128)(2,1)S(1)} copy-done((bf16[1024,768]{1,0:T(8,128)(2,1)S(1)}, bf16[1024,768]{1,0:T(8,128)(2,1)}, u32[]{:S(2)}) %copy-start.1) | copy-done | bytes 1572888
  2.2 0.0 copy-start.2
  2.2 1.1 copy-done.2
  3.3 2.1 %shard_map.50 = (f32[512,1024]{1,0:T(8,128)S(1)}, f32[8,16,128]{2,1,0:T(8,128)S(1)}, bf16[768,512]{1,0:T(8,128)(2,1)S(1)}, f32[16,768]{1,0:T(8,128)S(1)}) custom-call(s32[5]{0:T(128)S(1)} %stack.23.place_ref, bf16[1024,768]{1,0:T(8,128)(2,1)S(1)} %copy-done.1, bf16[512,768]{1,0:T(8,128)(2,1)S(1)} %copy-done.2), custom_call_target="tpu_custom_call" | custom-call | flops 805306368 | bytes 4718632 | tf_op jit(solution)/shard_map/pallas_call | solution.py:52
  5.4 20.6 %all_to_all.15.stat_ref = f32[8,16,128]{2,1,0:T(8,128)S(1)} all-to-all(f32[8,16,128]{2,1,0:T(8,128)S(1)} %get-tuple-element.32.mine_ref), channel_id=1, replica_groups=mesh['rows'=32,'cent'=8] {'cent'}, dimensions={0} | all-to-all | bytes 131072 | tf_op jit(solution)/shard_map/all_to_all | solution.py:279
  26.0 2.2 %shard_map.51 = (bf16[512,1024]{1,0:T(8,128)(2,1)S(1)}, f32[512,128]{1,0:T(8,128)S(1)}, f32[96,1024]{1,0:T(8,128)S(1)}, f32[96,1024]{1,0:T(8,128)S(1)}, f32[96,1...) custom-call(s32[5]{0:T(128)S(1)} %stack.23.place_ref, ...), custom_call_target="tpu_custom_call" | custom-call | flops 805306368 | bytes 6029352 | tf_op jit(solution)/shard_map/pallas_call | solution.py:52
  28.1 1.6 %shard_map.52 = (f32[256,896]{1,0:T(8,128)S(1)}, f32[256,896]{1,0:T(8,128)S(1)}, f32[96,1024]{1,0:T(8,128)S(1)}) custom-call(s32[5]{0:T(128)S(1)} %stack.23.place_ref, bf16[512,1024]{1,0:T(8,128)(2,1)S(1)} %get-tuple-element.34.wb_ref, f32[512,128]{1,0:T(8,128)S(1)} %get-tuple-element.35.count_ref, bf16[1024,768]{1,0:T(8,128)(2,1)S(1)} %copy-done.1), custom_call_target="tpu_custom_call" | custom-call | flops 805306368 | bytes 5767208 | tf_op jit(solution)/shard_map/pallas_call | solution.py:52
  29.7 2.2 %collective-permute-start.3 = (f32[256,896]{1,0:T(8,128)S(1)}, f32[256,896]{1,0:T(8,128)S(1)}, u32[]{:S(2)}, u32[]{:S(2)}) collective-permute-start(f32[256,896]{1,0:T(8,128)S(1)} %get-tuple-element.42), channel_id=1, source_target_pairs={{0,8},{8,0},{1,9},{9,1},{16,24},{24,16},{17,25},{25,17},{32,40},{4... | collective-permute-start | bytes 2752520 | tf_op jit(solution)/shard_map/ppermute | solution.py:24
  31.9 0.3 collective-permute-start.6
  32.2 2.4 %collective-permute-start.7 = (f32[96,1024]{1,0:T(8,128)S(1)}, f32[96,1024]{1,0:T(8,128)S(1)}, u32[]{:S(2)}, u32[]{:S(2)}) collective-permute-start(f32[96,1024]{1,0:T(8,128)S(1)} %get-tuple-element.50), channel_id=1, source_target_pairs={{0,6},{8,14},{1,7},{9,15},{16,22},{24,30},{17,23},{25,31},{32,38},... | collective-permute-start | bytes 1179656 | tf_op jit(solution)/shard_map/ppermute | solution.py:24
  34.6 0.0 collective-permute-start.8
  34.6 0.0 collective-permute-done.3.got_ref
  34.6 0.1 shard_map.53
  34.7 2.8 %collective-permute-start.4 = (f32[128,896]{1,0:T(8,128)S(1)}, f32[128,896]{1,0:T(8,128)S(1)}, u32[]{:S(2)}, u32[]{:S(2)}) collective-permute-start(f32[128,896]{1,0:T(8,128)S(1)} %get-tuple-element.44), channel_id=1, source_target_pairs={{0,128},{8,136},{1,129},{9,137},{16,144},{24,152},{17,145},{25,153... | collective-permute-start | bytes 1376264 | tf_op jit(solution)/shard_map/ppermute | solution.py:24
  37.6 14.7 %collective-permute-done.6.b_ref = f32[96,1024]{1,0:T(8,128)S(1)} collective-permute-done((f32[96,1024]{1,0:T(8,128)S(1)}, f32[96,1024]{1,0:T(8,128)S(1)}, u32[]{:S(2)}, u32[]{:S(2)}) %collective-permute-start.6) | collective-permute-done | bytes 393248 | tf_op jit(solution)/shard_map/ppermute | solution.py:24
  52.2 0.0 collective-permute-done.7.c_ref
  52.3 0.0 collective-permute-done.8.d_ref
  52.3 0.0 copy-start
  52.3 0.1 shard_map.56
  52.3 0.5 collective-permute-start.9
  52.9 0.6 collective-permute-start
  53.5 2.1 %collective-permute-start.1 = (f32[96,1024]{1,0:T(8,128)S(1)}, f32[96,1024]{1,0:T(8,128)S(1)}, u32[]{:S(2)}, u32[]{:S(2)}) collective-permute-start(f32[96,1024]{1,0:T(8,128)S(1)} %get-tuple-element.39), channel_id=1, source_target_pairs={{0,6},{8,14},{1,7},{9,15},{16,22},{24,30},{17,23},{25,31},{32,38},... | collective-permute-start | bytes 1179656 | tf_op jit(solution)/shard_map/ppermute | solution.py:24
  55.6 0.9 collective-permute-start.2
  56.4 0.0 collective-permute-done.4.got_ref
  56.5 1.3 collective-permute-start.5
  57.8 4.0 %collective-permute-done.5.got_ref = f32[64,896]{1,0:T(8,128)S(1)} collective-permute-done((f32[64,896]{1,0:T(8,128)S(1)}, f32[64,896]{1,0:T(8,128)S(1)}, u32[]{:S(2)}, u32[]{:S(2)}) %collective-permute-start.5) | collective-permute-done | bytes 229408 | tf_op jit(solution)/shard_map/ppermute | solution.py:24
  61.8 6.2 %collective-permute-done.9.e_ref = f32[96,1024]{1,0:T(8,128)S(1)} collective-permute-done((f32[96,1024]{1,0:T(8,128)S(1)}, f32[96,1024]{1,0:T(8,128)S(1)}, u32[]{:S(2)}, u32[]{:S(2)}) %collective-permute-start.9) | collective-permute-done | bytes 393248 | tf_op jit(solution)/shard_map/ppermute | solution.py:24
  68.0 7.8 %collective-permute-start.10 = (f32[32,896]{1,0:T(8,128)S(1)}, f32[32,896]{1,0:T(8,128)S(1)}, u32[]{:S(2)}, u32[]{:S(2)}) collective-permute-start(f32[32,896]{1,0:T(8,128)S(1)} %get-tuple-element.54), channel_id=1, source_target_pairs={{0,32},{8,40},{1,33},{9,41},{16,48},{24,56},{17,49},{25,57},{32,0}... | collective-permute-start | bytes 344072 | tf_op jit(solution)/shard_map/ppermute | solution.py:24
  75.8 0.0 collective-permute-done.b_ref
  75.8 0.0 collective-permute-done.1.c_ref
  75.8 0.0 collective-permute-done.2.d_ref
  75.8 0.0 copy-done
  75.8 5.8 %shard_map.57 = f32[32,8,256]{2,1,0:T(8,128)} custom-call(s32[5]{0:T(128)S(1)} %stack.23.place_ref, f32[96,8,256]{2,1,0:T(8,128)S(1)} %copy-done, f32[96,1024]{1,0:T(8,128)S(1)} %get-tuple-element.36.emb_t_ref, f32[96,1024]{1,0:T(8,128)S(1)} %get-tuple-element.37.a_ref, f32[96,1024]{1,0:T(8,128)S(1)} %collective-permute-done.b_ref, ...), custom_call_target="tpu_custom_call" | custom-call | flops 12884901888 | bytes 6291496 | tf_op jit(solution)/shard_map/pallas_call | solution.py:52
  81.6 0.0 collective-permute-done.10.got_ref
  81.6 7.8 %all-to-all-start.1 = ((f32[32,8,256]{2,1,0:T(8,128)}), f32[32,8,256]{2,1,0:T(8,128)S(1)}, u32[]{:S(2)}, u32[]{:S(2)}) async-start(f32[32,8,256]{2,1,0:T(8,128)} %shard_map.57), calls=%async_computation.1 | async-start | bytes 524288 | tf_op jit(solution)/shard_map/all_to_all | solution.py:324
  89.4 1.5 %collective-permute-start.11 = (f32[16,896]{1,0:T(8,128)S(1)}, f32[16,896]{1,0:T(8,128)S(1)}, u32[]{:S(2)}, u32[]{:S(2)}) collective-permute-start(f32[16,896]{1,0:T(8,128)S(1)} %get-tuple-element.57), channel_id=1, source_target_pairs={{0,16},{8,24},{1,17},{9,25},{16,0},{24,8},{17,1},{25,9},{32,48},{4... | collective-permute-start | bytes 172040 | tf_op jit(solution)/shard_map/ppermute | solution.py:24
  90.9 4.7 %collective-permute-done.11.got_ref = f32[16,896]{1,0:T(8,128)S(1)} collective-permute-done((f32[16,896]{1,0:T(8,128)S(1)}, f32[16,896]{1,0:T(8,128)S(1)}, u32[]{:S(2)}, u32[]{:S(2)}) %collective-permute-start.11) | collective-permute-done | bytes 57376 | tf_op jit(solution)/shard_map/ppermute | solution.py:24
  95.7 0.1 shard_map.59
  95.7 3.5 %collective-permute-start.14 = (f32[16,768]{1,0:T(8,128)S(1)}, f32[16,768]{1,0:T(8,128)S(1)}, u32[]{:S(2)}, u32[]{:S(2)}) collective-permute-start(f32[16,768]{1,0:T(8,128)S(1)} %shard_map.59), channel_id=1, source_target_pairs={{0,48},{8,56},{1,49},{9,57},{16,32},{24,40},{17,33},{25,41},{32,16... | collective-permute-start | bytes 147464 | tf_op jit(solution)/shard_map/ppermute | solution.py:24
  99.3 0.2 collective-permute-start.13
  99.5 0.2 collective-permute-start.12
  99.7 1.0 all-to-all-done.1.parts_ref
  100.7 1.6 %shard_map.61 = f32[128,8,128]{2,1,0:T(8,128)} custom-call(s32[5]{0:T(128)S(1)} %stack.23.place_ref, f32[768,256]{1,0:T(8,128)S(1)} %bitcast.7, f32[32,8,256]{2,1,0:T(8,128)S(1)} %all-to-all-done.1.parts_ref), custom_call_target="tpu_custom_call" | custom-call | bytes 2097192 | tf_op jit(solution)/shard_map/pallas_call | solution.py:52
  102.2 10.3 %all-to-all-start.2 = ((f32[128,8,128]{2,1,0:T(8,128)}), f32[128,8,128]{2,1,0:T(8,128)S(1)}, u32[]{:S(2)}, u32[]{:S(2)}) async-start(f32[128,8,128]{2,1,0:T(8,128)} %shard_map.61), calls=%async_computation.2 | async-start | bytes 1048576 | tf_op jit(solution)/shard_map/all_to_all | solution.py:342
  112.5 0.0 collective-permute-done.14
  112.5 0.0 collective-permute-done.13
  112.5 0.0 collective-permute-done.12
  112.5 1.9 %collective-permute-start.17 = (f32[64,768]{1,0:T(8,128)S(1)}, f32[64,768]{1,0:T(8,128)S(1)}, u32[]{:S(2)}, u32[]{:S(2)}) collective-permute-start(f32[64,768]{1,0:T(8,128)S(1)} %pad_maximum_fusion), channel_id=1, source_target_pairs={{0,192},{8,200},{1,193},{9,201},{16,208},{24,216},{17,209},{25,217... | collective-permute-start | bytes 589832 | tf_op jit(solution)/shard_map/ppermute | solution.py:24
  114.4 0.6 collective-permute-start.16
  115.0 0.9 collective-permute-start.15
  115.9 12.2 %collective-permute-done.15 = f32[64,768]{1,0:T(8,128)S(1)} collective-permute-done((f32[64,768]{1,0:T(8,128)S(1)}, f32[64,768]{1,0:T(8,128)S(1)}, u32[]{:S(2)}, u32[]{:S(2)}) %collective-permute-start.15) | collective-permute-done | bytes 196640 | tf_op jit(solution)/shard_map/ppermute | solution.py:24
  128.1 0.0 collective-permute-done.16
  128.2 0.5 collective-permute-done.17
  128.6 1.8 %collective-permute-start.18 = (f32[256,768]{1,0:T(8,128)S(1)}, f32[256,768]{1,0:T(8,128)S(1)}, u32[]{:S(2)}, u32[]{:S(2)}) collective-permute-start(f32[256,768]{1,0:T(8,128)S(1)} %constant_dynamic-update-slice_fusion.mine_ref), channel_id=1, source_target_pairs={{0,8},{8,0},{1,9},{9,1},{16,24},{24,16},{17,25},{25,17},{32,40},{4... | collective-permute-start | bytes 2359304 | tf_op jit(solution)/shard_map/ppermute | solution.py:24
  130.4 0.2 all-to-all-done.2.mine_ref
  130.7 3.4 %collective-permute-start.19 = (f32[128,8,128]{2,1,0:T(8,128)S(1)}, f32[128,8,128]{2,1,0:T(8,128)S(1)}, u32[]{:S(2)}, u32[]{:S(2)}) collective-permute-start(f32[128,8,128]{2,1,0:T(8,128)S(1)} %all-to-all-done.2.mine_ref), channel_id=1, source_target_pairs={{0,8},{8,0},{1,9},{9,1},{16,24},{24,16},{17,25},{25,17},{32,40},{4... | collective-permute-start | bytes 1572872 | tf_op jit(solution)/shard_map/ppermute | solution.py:24
  134.1 0.0 collective-permute-done.18.theirs_ref
  134.1 1.8 %shard_map.60 = f32[512,768]{1,0:T(8,128)} custom-call(s32[5]{0:T(128)S(1)} %stack.23.place_ref, f32[256,768]{1,0:T(8,128)S(1)} %constant_dynamic-update-slice_fusion.mine_ref, f32[256,768]{1,0:T(8,128)S(1)} %collective-permute-done.18.theirs_ref), custom_call_target="tpu_custom_call" | custom-call | bytes 3145768 | tf_op jit(solution)/shard_map/pallas_call | solution.py:52
  135.9 0.0 collective-permute-done.19.theirs_ref
  135.9 1.7 %shard_map.62 = f32[768,256]{1,0:T(8,128)} custom-call(s32[5]{0:T(128)S(1)} %stack.23.place_ref, f32[128,8,128]{2,1,0:T(8,128)S(1)} %all-to-all-done.2.mine_ref, f32[128,8,128]{2,1,0:T(8,128)S(1)} %collective-permute-done.19.theirs_ref), custom_call_target="tpu_custom_call" | custom-call | bytes 2097192 | tf_op jit(solution)/shard_map/pallas_call | solution.py:52
  (11 shorter events, 0.2 us)
Async XLA Ops:
  0.8 1.4 %copy-start.1 = (bf16[1024,768]{1,0:T(8,128)(2,1)S(1)}, bf16[1024,768]{1,0:T(8,128)(2,1)}, u32[]{:S(2)}) copy-start(bf16[1024,768]{1,0:T(8,128)(2,1)} %emb_ref.3) | copy-start | bytes 4718596
  2.2 1.1 copy-start.2
  29.7 4.9 %collective-permute-start.3 = (f32[256,896]{1,0:T(8,128)S(1)}, f32[256,896]{1,0:T(8,128)S(1)}, u32[]{:S(2)}, u32[]{:S(2)}) collective-permute-start(f32[256,896]{1,0:T(8,128)S(1)} %get-tuple-element.42), channel_id=1, source_target_pairs={{0,8},{8,0},{1,9},{9,1},{16,24},{24,16},{17,25},{25,17},{32,40},{4... | collective-permute-start | bytes 2752520 | tf_op jit(solution)/shard_map/ppermute | solution.py:24
  31.9 20.3 %collective-permute-start.6 = (f32[96,1024]{1,0:T(8,128)S(1)}, f32[96,1024]{1,0:T(8,128)S(1)}, u32[]{:S(2)}, u32[]{:S(2)}) collective-permute-start(f32[96,1024]{1,0:T(8,128)S(1)} %get-tuple-element.49), channel_id=1, source_target_pairs={{0,2},{8,10},{1,3},{9,11},{16,18},{24,26},{17,19},{25,27},{32,34},... | collective-permute-start | bytes 1179656 | tf_op jit(solution)/shard_map/ppermute | solution.py:24
  32.2 20.0 %collective-permute-start.7 = (f32[96,1024]{1,0:T(8,128)S(1)}, f32[96,1024]{1,0:T(8,128)S(1)}, u32[]{:S(2)}, u32[]{:S(2)}) collective-permute-start(f32[96,1024]{1,0:T(8,128)S(1)} %get-tuple-element.50), channel_id=1, source_target_pairs={{0,6},{8,14},{1,7},{9,15},{16,22},{24,30},{17,23},{25,31},{32,38},... | collective-permute-start | bytes 1179656 | tf_op jit(solution)/shard_map/ppermute | solution.py:24
  34.6 17.6 %collective-permute-start.8 = (f32[96,1024]{1,0:T(8,128)S(1)}, f32[96,1024]{1,0:T(8,128)S(1)}, u32[]{:S(2)}, u32[]{:S(2)}) collective-permute-start(f32[96,1024]{1,0:T(8,128)S(1)} %get-tuple-element.51), channel_id=1, source_target_pairs={{0,4},{8,12},{1,5},{9,13},{16,20},{24,28},{17,21},{25,29},{32,36},... | collective-permute-start | bytes 1179656 | tf_op jit(solution)/shard_map/ppermute | solution.py:24
  34.7 21.7 %collective-permute-start.4 = (f32[128,896]{1,0:T(8,128)S(1)}, f32[128,896]{1,0:T(8,128)S(1)}, u32[]{:S(2)}, u32[]{:S(2)}) collective-permute-start(f32[128,896]{1,0:T(8,128)S(1)} %get-tuple-element.44), channel_id=1, source_target_pairs={{0,128},{8,136},{1,129},{9,137},{16,144},{24,152},{17,145},{25,153... | collective-permute-start | bytes 1376264 | tf_op jit(solution)/shard_map/ppermute | solution.py:24
  52.3 23.5 %copy-start = (f32[96,8,256]{2,1,0:T(8,128)S(1)}, f32[96,8,256]{2,1,0:T(8,128)}, u32[]{:S(2)}) copy-start(f32[96,8,256]{2,1,0:T(8,128)} %all_books_ref.1) | copy-start | bytes 2359300
  52.3 15.7 %collective-permute-start.9 = (f32[96,1024]{1,0:T(8,128)S(1)}, f32[96,1024]{1,0:T(8,128)S(1)}, u32[]{:S(2)}, u32[]{:S(2)}) collective-permute-start(f32[96,1024]{1,0:T(8,128)S(1)} %shard_map.56), channel_id=1, source_target_pairs={{0,1},{8,9},{1,0},{9,8},{16,17},{24,25},{17,16},{25,24},{32,33},{4... | collective-permute-start | bytes 1179656 | tf_op jit(solution)/shard_map/ppermute | solution.py:24
  52.9 22.9 %collective-permute-start = (f32[96,1024]{1,0:T(8,128)S(1)}, f32[96,1024]{1,0:T(8,128)S(1)}, u32[]{:S(2)}, u32[]{:S(2)}) collective-permute-start(f32[96,1024]{1,0:T(8,128)S(1)} %get-tuple-element.38), channel_id=1, source_target_pairs={{0,2},{8,10},{1,3},{9,11},{16,18},{24,26},{17,19},{25,27},{32,34},... | collective-permute-start | bytes 1179656 | tf_op jit(solution)/shard_map/ppermute | solution.py:24
  53.5 22.3 %collective-permute-start.1 = (f32[96,1024]{1,0:T(8,128)S(1)}, f32[96,1024]{1,0:T(8,128)S(1)}, u32[]{:S(2)}, u32[]{:S(2)}) collective-permute-start(f32[96,1024]{1,0:T(8,128)S(1)} %get-tuple-element.39), channel_id=1, source_target_pairs={{0,6},{8,14},{1,7},{9,15},{16,22},{24,30},{17,23},{25,31},{32,38},... | collective-permute-start | bytes 1179656 | tf_op jit(solution)/shard_map/ppermute | solution.py:24
  55.6 20.2 %collective-permute-start.2 = (f32[96,1024]{1,0:T(8,128)S(1)}, f32[96,1024]{1,0:T(8,128)S(1)}, u32[]{:S(2)}, u32[]{:S(2)}) collective-permute-start(f32[96,1024]{1,0:T(8,128)S(1)} %get-tuple-element.40), channel_id=1, source_target_pairs={{0,4},{8,12},{1,5},{9,13},{16,20},{24,28},{17,21},{25,29},{32,36},... | collective-permute-start | bytes 1179656 | tf_op jit(solution)/shard_map/ppermute | solution.py:24
  56.5 5.3 %collective-permute-start.5 = (f32[64,896]{1,0:T(8,128)S(1)}, f32[64,896]{1,0:T(8,128)S(1)}, u32[]{:S(2)}, u32[]{:S(2)}) collective-permute-start(f32[64,896]{1,0:T(8,128)S(1)} %get-tuple-element.46), channel_id=1, source_target_pairs={{0,64},{8,72},{1,65},{9,73},{16,80},{24,88},{17,81},{25,89},{32,96... | collective-permute-start | bytes 688136 | tf_op jit(solution)/shard_map/ppermute | solution.py:24
  68.0 13.6 %collective-permute-start.10 = (f32[32,896]{1,0:T(8,128)S(1)}, f32[32,896]{1,0:T(8,128)S(1)}, u32[]{:S(2)}, u32[]{:S(2)}) collective-permute-start(f32[32,896]{1,0:T(8,128)S(1)} %get-tuple-element.54), channel_id=1, source_target_pairs={{0,32},{8,40},{1,33},{9,41},{16,48},{24,56},{17,49},{25,57},{32,0}... | collective-permute-start | bytes 344072 | tf_op jit(solution)/shard_map/ppermute | solution.py:24
  81.6 19.0 %all-to-all-start.1 = ((f32[32,8,256]{2,1,0:T(8,128)}), f32[32,8,256]{2,1,0:T(8,128)S(1)}, u32[]{:S(2)}, u32[]{:S(2)}) async-start(f32[32,8,256]{2,1,0:T(8,128)} %shard_map.57), calls=%async_computation.1 | async-start | bytes 524288 | tf_op jit(solution)/shard_map/all_to_all | solution.py:324
  89.4 6.2 %collective-permute-start.11 = (f32[16,896]{1,0:T(8,128)S(1)}, f32[16,896]{1,0:T(8,128)S(1)}, u32[]{:S(2)}, u32[]{:S(2)}) collective-permute-start(f32[16,896]{1,0:T(8,128)S(1)} %get-tuple-element.57), channel_id=1, source_target_pairs={{0,16},{8,24},{1,17},{9,25},{16,0},{24,8},{17,1},{25,9},{32,48},{4... | collective-permute-start | bytes 172040 | tf_op jit(solution)/shard_map/ppermute | solution.py:24
  95.7 16.8 %collective-permute-start.14 = (f32[16,768]{1,0:T(8,128)S(1)}, f32[16,768]{1,0:T(8,128)S(1)}, u32[]{:S(2)}, u32[]{:S(2)}) collective-permute-start(f32[16,768]{1,0:T(8,128)S(1)} %shard_map.59), channel_id=1, source_target_pairs={{0,48},{8,56},{1,49},{9,57},{16,32},{24,40},{17,33},{25,41},{32,16... | collective-permute-start | bytes 147464 | tf_op jit(solution)/shard_map/ppermute | solution.py:24
  99.3 13.2 %collective-permute-start.13 = (f32[16,768]{1,0:T(8,128)S(1)}, f32[16,768]{1,0:T(8,128)S(1)}, u32[]{:S(2)}, u32[]{:S(2)}) collective-permute-start(f32[16,768]{1,0:T(8,128)S(1)} %shard_map.59), channel_id=1, source_target_pairs={{0,32},{8,40},{1,33},{9,41},{16,48},{24,56},{17,49},{25,57},{32,0}... | collective-permute-start | bytes 147464 | tf_op jit(solution)/shard_map/ppermute | solution.py:24
  99.5 13.1 %collective-permute-start.12 = (f32[16,768]{1,0:T(8,128)S(1)}, f32[16,768]{1,0:T(8,128)S(1)}, u32[]{:S(2)}, u32[]{:S(2)}) collective-permute-start(f32[16,768]{1,0:T(8,128)S(1)} %shard_map.59), channel_id=1, source_target_pairs={{0,16},{8,24},{1,17},{9,25},{16,0},{24,8},{17,1},{25,9},{32,48},{4... | collective-permute-start | bytes 147464 | tf_op jit(solution)/shard_map/ppermute | solution.py:24
  102.2 28.5 %all-to-all-start.2 = ((f32[128,8,128]{2,1,0:T(8,128)}), f32[128,8,128]{2,1,0:T(8,128)S(1)}, u32[]{:S(2)}, u32[]{:S(2)}) async-start(f32[128,8,128]{2,1,0:T(8,128)} %shard_map.61), calls=%async_computation.2 | async-start | bytes 1048576 | tf_op jit(solution)/shard_map/all_to_all | solution.py:342
  112.5 16.1 %collective-permute-start.17 = (f32[64,768]{1,0:T(8,128)S(1)}, f32[64,768]{1,0:T(8,128)S(1)}, u32[]{:S(2)}, u32[]{:S(2)}) collective-permute-start(f32[64,768]{1,0:T(8,128)S(1)} %pad_maximum_fusion), channel_id=1, source_target_pairs={{0,192},{8,200},{1,193},{9,201},{16,208},{24,216},{17,209},{25,217... | collective-permute-start | bytes 589832 | tf_op jit(solution)/shard_map/ppermute | solution.py:24
  114.4 13.7 %collective-permute-start.16 = (f32[64,768]{1,0:T(8,128)S(1)}, f32[64,768]{1,0:T(8,128)S(1)}, u32[]{:S(2)}, u32[]{:S(2)}) collective-permute-start(f32[64,768]{1,0:T(8,128)S(1)} %pad_maximum_fusion), channel_id=1, source_target_pairs={{0,128},{8,136},{1,129},{9,137},{16,144},{24,152},{17,145},{25,153... | collective-permute-start | bytes 589832 | tf_op jit(solution)/shard_map/ppermute | solution.py:24
  115.0 13.1 %collective-permute-start.15 = (f32[64,768]{1,0:T(8,128)S(1)}, f32[64,768]{1,0:T(8,128)S(1)}, u32[]{:S(2)}, u32[]{:S(2)}) collective-permute-start(f32[64,768]{1,0:T(8,128)S(1)} %pad_maximum_fusion), channel_id=1, source_target_pairs={{0,64},{8,72},{1,65},{9,73},{16,80},{24,88},{17,81},{25,89},{32,96... | collective-permute-start | bytes 589832 | tf_op jit(solution)/shard_map/ppermute | solution.py:24
  128.6 5.4 %collective-permute-start.18 = (f32[256,768]{1,0:T(8,128)S(1)}, f32[256,768]{1,0:T(8,128)S(1)}, u32[]{:S(2)}, u32[]{:S(2)}) collective-permute-start(f32[256,768]{1,0:T(8,128)S(1)} %constant_dynamic-update-slice_fusion.mine_ref), channel_id=1, source_target_pairs={{0,8},{8,0},{1,9},{9,1},{16,24},{24,16},{17,25},{25,17},{32,40},{4... | collective-permute-start | bytes 2359304 | tf_op jit(solution)/shard_map/ppermute | solution.py:24
  130.7 5.2 %collective-permute-start.19 = (f32[128,8,128]{2,1,0:T(8,128)S(1)}, f32[128,8,128]{2,1,0:T(8,128)S(1)}, u32[]{:S(2)}, u32[]{:S(2)}) collective-permute-start(f32[128,8,128]{2,1,0:T(8,128)S(1)} %all-to-all-done.2.mine_ref), channel_id=1, source_target_pairs={{0,8},{8,0},{1,9},{9,1},{16,24},{24,16},{17,25},{25,17},{32,40},{4... | collective-permute-start | bytes 1572872 | tf_op jit(solution)/shard_map/ppermute | solution.py:24

commit v6 on v5

--- a/solution.py
+++ b/solution.py
@@ -129,11 +129,14 @@
             out_refs[part * NY + k][...] = dot(piece, wb_ref[...], 1, 0)
 
 
-def mass_kernel(place_ref, wb_ref, count_ref, emb_ref, keep_ref, send_ref, emb_t_ref, turned_ref):
+def mass_kernel(wb_ref, count_ref, emb_ref, keep_ref, send_ref):
     half, width = keep_ref.shape[0], emb_ref.shape[1]
     for ref, start in ((send_ref, half), (keep_ref, 0)):
         ref[:, :width] = dot(wb_ref[start : start + half, :], emb_ref[...], 1, 0)
         ref[:, width:] = count_ref[start : start + half, :]
+
+
+def turn_kernel(place_ref, after_ref, emb_ref, emb_t_ref, turned_ref):
     share = emb_t_ref.shape[0]
     turned_ref[...] = emb_ref[...].T
     first = (place_ref[1] * NZH + place_ref[3]) * share
@@ -152,8 +155,18 @@
     out_ref[...] = (total[:, :width] + old_ref[...]) / (total[:, width : width + 1] + 1.0)
 
 
+def after_kernel(after_ref, a_ref, out_ref):
+    out_ref[...] = a_ref[...]
+
+
 def add_kernel(a_ref, b_ref, c_ref, d_ref, out_ref):
     out_ref[...] = (a_ref[...] + b_ref[...]) + (c_ref[...] + d_ref[...])
+
+
+def row_of_owner(owner):
+    rest, zl = divmod(owner, NZL)
+    x, core = divmod(rest, NC)
+    return (x * NZL + zl) * NC + core
 
 
 def pieces(v):
@@ -197,8 +210,7 @@
         count = high[o : o + 1] + (high[o + depth : o + depth + 1] + high[o + 2 * depth : o + 2 * depth + 1])
         for d in range(depth):
             owner, slot = divmod(m * depth + d, 3)
-            core, xz = divmod(owner, NX * NZL)
-            row = xz * NC + core
+            row = row_of_owner(owner)
             out_ref[row, slot : slot + 1, :] = mass[d : d + 1]
             out_ref[row, slot + 3 : slot + 4, :] = count
 
@@ -211,7 +223,7 @@
     copy.start()
     total = jnp.sum(parts_ref[...], axis=0)
     copy.wait()
-    row = ((c * NX + x) * NZL + zl) * 3
+    row = ((x * NC + c) * NZL + zl) * 3
     old = jnp.concatenate([books_ref[pl.ds(row + i, 1), :] for i in range(3)], axis=0)
     new = (total[:3] + old) / (total[3:6] + 1.0)
     tile = jnp.concatenate([new[:, :128], new[:, 128:], jnp.zeros((2, 128), F32)], axis=0)
@@ -221,24 +233,26 @@
 
 def books_kernel(place_ref, mine_ref, theirs_ref, out_ref):
     core = place_ref[4]
-    count = mine_ref.shape[0]
-    group = NX * NZL
-
-    def place(first_ref, second_ref):
-        for side, ref in ((0, first_ref), (1, second_ref)):
-            for i in range(count):
-                cent, xz = divmod(i, group)
-                row = (cent * NC + side) * group * 3 + xz * 3
-                out_ref[row : row + 3, :128] = ref[i, :3, :]
-                out_ref[row : row + 3, 128:] = ref[i, 3:6, :]
+    cents = NY * NZH
+    size = NC * NZL * 3
+
+    def place(refs):
+        for kx, cent in itertools.product(range(NX), range(cents)):
+            first = (kx * cents + cent) * NZL
+            tiles = [ref[first + zl] for ref in refs for zl in range(NZL)]
+            low = jnp.concatenate([tile[:3] for tile in tiles], axis=0)
+            high = jnp.concatenate([tile[3:6] for tile in tiles], axis=0)
+            row = (cent * NX + kx) * size
+            out_ref[row : row + size, :128] = low
+            out_ref[row : row + size, 128:] = high
 
     @pl.when(core == 0)
     def _():
-        place(mine_ref, theirs_ref)
+        place((mine_ref, theirs_ref))
 
     @pl.when(core == 1)
     def _():
-        place(theirs_ref, mine_ref)
+        place((theirs_ref, mine_ref))
 
 
 def centroids_kernel(place_ref, mine_ref, theirs_ref, out_ref):
@@ -288,22 +302,29 @@
     steps = (1, -1, 2)
     got = [hop(theirs[k % NY], along_y(k)) for k in steps]
     got_mine = [hop(mine[k % NY], along_y(k)) for k in steps]
-    peer = hop(call(add_kernel, shape((share, rows_here)), (theirs[0], *got)), other_zh)
-
-    keep, send, emb_t = call(
+    total = call(add_kernel, shape((share, rows_here)), (theirs[0], *got))
+    peer = hop(total, other_zh)
+    emb_t = call(
+        turn_kernel,
+        shape((share, rows_here)),
+        (place, total, embeddings),
+        smem=1,
+        hbm_in=1,
+        scratch=(pltpu.VMEM((width, rows_here), BF16),),
+    )
+
+    keep, send = call(
         mass_kernel,
-        (shape((held // 2, width + 128)),) * 2 + (shape((share, rows_here)),),
-        (place, wb, counts, embeddings),
-        smem=1,
-        scratch=(pltpu.VMEM((width, rows_here), BF16),),
+        (shape((held // 2, width + 128)),) * 2,
+        (wb, counts, embeddings),
         flops=2 * rows_here * held * width,
     )
-    for step, move in enumerate((other_core, along_x(2), along_x(1), along_zl(2))):
+    for move in (other_core, along_x(2), along_x(1)):
         half = keep.shape[0] // 2
         got = hop(send, move)
         keep, send = call(halve_kernel, (shape((half, width + 128)),) * 2, (keep, got), limit=4)
-        if step == 2:
-            send, peer = lax.optimization_barrier((send, peer))
+    send, peer = lax.optimization_barrier((send, peer))
+    got = hop(send, along_zl(2))
     peers = NX * NZL
 
     per = subspaces // cents
@@ -316,30 +337,40 @@
         scratch=(pltpu.VMEM((per, depth, codes), F32), pltpu.SemaphoreType.DMA),
         flops=64 * rows_here * per * codes * 64,
     )
-    sums, keep = lax.optimization_barrier((sums, keep))
+    sums, got = lax.optimization_barrier((sums, got))
+    half = keep.shape[0] // 2
+    keep, send = call(halve_kernel, (shape((half, width + 128)),) * 2, (keep, got), limit=4)
     new = call(
         centroid_kernel, shape((half, width)), (keep, hop(send, along_zl(1)), old), limit=4
     )
     new_z = jnp.concatenate([new] + [hop(new, along_zl(k)) for k in (1, 2, 3)], axis=0)
     all_parts = lax.all_to_all(sums, "rows", 0, 0, tiled=True)
-    same_core = [
-        [flat(xx, yy, zz, hh, cc) for yy in range(NY) for hh in range(NZH) for xx in range(NX) for zz in range(NZL)]
+    same_line = [
+        [flat(xx, yy, zz, hh, cc) for yy in range(NY) for hh in range(NZH) for zz in range(NZL)]
+        for xx in range(NX)
         for cc in range(NC)
     ]
     tile = call(
         update_kernel,
-        shape((cents * peers, 8, 128)),
+        shape((cents * NZL, 8, 128)),
         (place, codebooks.reshape(subspaces * depth, codes), all_parts),
         smem=1,
         hbm_in=1,
         scratch=(pltpu.VMEM((share, codes), F32), pltpu.SemaphoreType.DMA),
     )
+    new_z = call(after_kernel, shape((4 * half, width)), (tile, new_z), hbm_in=1)
     new_x = jnp.concatenate([new_z] + [hop(new_z, along_x(k)) for k in (1, 2, 3)], axis=0)
     new_other = hop(new_x, other_core)
     new_centroids = call(
         centroids_kernel, shape((held, width)), (place, new_x, new_other), smem=1
     )
-    tiles = lax.all_to_all(tile, BOTH, 0, 0, tiled=True, axis_index_groups=same_core)
+    line = lax.all_to_all(tile, BOTH, 0, 0, tiled=True, axis_index_groups=same_line)
+    across = [
+        [(xx * NZL + zz) * NC + cc for xx in range(NX)] for zz in range(NZL) for cc in range(NC)
+    ]
+    lines = jnp.broadcast_to(line[None], (NX,) + line.shape)
+    tiles = lax.all_to_all(lines, "rows", 0, 0, tiled=True, axis_index_groups=across)
+    tiles = tiles.reshape((NX * line.shape[0],) + line.shape[1:])
     tiles_other = hop(tiles, other_core)
     new_books = call(
         books_kernel, shape((subspaces * depth, codes)), (place, tiles, tiles_other), smem=1

time: 138 us -> 137 us (level)
  waiting for transfers between devices: 43.5 us -> 38.8 us
  starting transfers between devices: 52.8 us -> 55.2 us
    ppermute x20, waiting for transfers between devices: 42.3 us -> 28.5 us  [hop(): return lax.ppermute(value, BOTH, pairs)]
    all_to_all x1 -> x2, waiting for transfers between devices: 0.24 us -> 9.26 us  [the longest x1 5.73 us: body(): lax.all_to_all(tile, BOTH, 0, 0, tiled=True, axis_index_groups=same_line)]
    ppermute x20, starting transfers between devices: 34.7 us -> 37.3 us  [hop(): return lax.ppermute(value, BOTH, pairs)]
    pallas_call x13 -> x15, Pallas kernels: 17 us -> 17.3 us  [call(): pl.pallas_call(kernel, out_shape=out, in_specs=specs, out_specs=jax.tree....]
    all_to_all x1 -> x2, starting transfers between devices: 10.3 us -> 10.1 us  [the longest x1 5.91 us: body(): lax.all_to_all(tile, BOTH, 0, 0, tiled=True, axis_index_groups=same_line)]
  transfers between devices with their start and end apart: 22 -> 23, of which waited for: 8 -> 7; matrix products, arithmetic and copies ran while one was open for 0% -> 1% of each run, Pallas kernels for 7% -> 8%
where the time goes in v6:
time: 137 us; the launch traced here: 136 us
  starting transfers between devices  55.2 us (40%)
  waiting for transfers between devices  38.8 us (28%)
  blocking collectives  20.7 us (15%)
  Pallas kernels  17.3 us (13%)
  local copies, waits for them, and re-layouts  3.47 us (3%)
    ppermute x20, starting transfers between devices, hop(): return lax.ppermute(value, BOTH, pairs)  37.3 us
    ppermute x20, waiting for transfers between devices, hop(): return lax.ppermute(value, BOTH, pairs)  28.5 us
    all_to_all x1, blocking collectives, body(): stats = lax.all_to_all(stat, 'cent', 0, 0, tiled=True)  20.7 us
    pallas_call x15, Pallas kernels, call(): pl.pallas_call(kernel, out_shape=out, in_specs=specs, out_specs=jax.tree....  17.3 us
    all_to_all x1, starting transfers between devices, body(): all_parts = lax.all_to_all(sums, 'rows', 0, 0, tiled=True)  7.8 us
    all_to_all x1, starting transfers between devices, body(): lax.all_to_all(tile, BOTH, 0, 0, tiled=True, axis_index_groups=same_line)  5.91 us
    all_to_all x1, waiting for transfers between devices, body(): lax.all_to_all(tile, BOTH, 0, 0, tiled=True, axis_index_groups=same_line)  5.73 us
    all_to_all x1, starting transfers between devices, body(): lax.all_to_all(lines, 'rows', 0, 0, tiled=True, axis_index_groups=across)  4.17 us
  transfers between devices with their start and end apart: 23, of which 7 were waited for; matrix products, arithmetic and copies ran while one was open for 1% of the time, Pallas kernels for 8%

profile of v6, /device:TPU:1, one launch (start us, length us, event | category | flops | bytes accessed | tf_op | source)
XLA Modules:
  0.0 136.3 jit_solution(5640624968643945058)
XLA Ops:
  0.7 0.1 stack.23.place_ref
  0.8 1.4 %copy-done = bf16[1024,768]{1,0:T(8,128)(2,1)S(1)} copy-done((bf16[1024,768]{1,0:T(8,128)(2,1)S(1)}, bf16[1024,768]{1,0:T(8,128)(2,1)}, u32[]{:S(2)}) %copy-start) | copy-done | bytes 1572888
  2.2 1.1 copy-done.3
  3.3 2.1 %shard_map.50 = (f32[512,1024]{1,0:T(8,128)S(1)}, f32[8,16,128]{2,1,0:T(8,128)S(1)}, bf16[768,512]{1,0:T(8,128)(2,1)S(1)}, f32[16,768]{1,0:T(8,128)S(1)}) custom-call(s32[5]{0:T(128)S(1)} %stack.23.place_ref, bf16[1024,768]{1,0:T(8,128)(2,1)S(1)} %copy-done, bf16[512,768]{1,0:T(8,128)(2,1)S(1)} %copy-done.3), custom_call_target="tpu_custom_call" | custom-call | flops 805306368 | bytes 4718632 | tf_op jit(solution)/shard_map/pallas_call | solution.py:52
  5.4 0.0 copy-start.1
  5.4 20.7 %all_to_all.20.stat_ref = f32[8,16,128]{2,1,0:T(8,128)S(1)} all-to-all(f32[8,16,128]{2,1,0:T(8,128)S(1)} %get-tuple-element.31.mine_ref), channel_id=1, replica_groups=mesh['rows'=32,'cent'=8] {'cent'}, dimensions={0} | all-to-all | bytes 131072 | tf_op jit(solution)/shard_map/all_to_all | solution.py:293
  26.1 2.2 %shard_map.51 = (bf16[512,1024]{1,0:T(8,128)(2,1)S(1)}, f32[512,128]{1,0:T(8,128)S(1)}, f32[96,1024]{1,0:T(8,128)S(1)}, f32[96,1024]{1,0:T(8,128)S(1)}, f32[96,1...) custom-call(s32[5]{0:T(128)S(1)} %stack.23.place_ref, ...), custom_call_target="tpu_custom_call" | custom-call | flops 805306368 | bytes 6029352 | tf_op jit(solution)/shard_map/pallas_call | solution.py:52
  28.3 1.0 shard_map.54
  29.3 2.2 %collective-permute-start.6 = (f32[256,896]{1,0:T(8,128)S(1)}, f32[256,896]{1,0:T(8,128)S(1)}, u32[]{:S(2)}, u32[]{:S(2)}) collective-permute-start(f32[256,896]{1,0:T(8,128)S(1)} %get-tuple-element.44), channel_id=1, source_target_pairs={{0,8},{8,0},{1,9},{9,1},{16,24},{24,16},{17,25},{25,17},{32,40},{4... | collective-permute-start | bytes 2752520 | tf_op jit(solution)/shard_map/ppermute | solution.py:24
  31.5 0.3 collective-permute-start
  31.8 2.4 %collective-permute-start.1 = (f32[96,1024]{1,0:T(8,128)S(1)}, f32[96,1024]{1,0:T(8,128)S(1)}, u32[]{:S(2)}, u32[]{:S(2)}) collective-permute-start(f32[96,1024]{1,0:T(8,128)S(1)} %get-tuple-element.35), channel_id=1, source_target_pairs={{0,6},{8,14},{1,7},{9,15},{16,22},{24,30},{17,23},{25,31},{32,38},... | collective-permute-start | bytes 1179656 | tf_op jit(solution)/shard_map/ppermute | solution.py:24
  34.2 0.0 collective-permute-start.2
  34.2 0.0 collective-permute-done.6.got_ref
  34.2 0.1 shard_map.55
  34.3 2.8 %collective-permute-start.7 = (f32[128,896]{1,0:T(8,128)S(1)}, f32[128,896]{1,0:T(8,128)S(1)}, u32[]{:S(2)}, u32[]{:S(2)}) collective-permute-start(f32[128,896]{1,0:T(8,128)S(1)} %get-tuple-element.46), channel_id=1, source_target_pairs={{0,128},{8,136},{1,129},{9,137},{16,144},{24,152},{17,145},{25,153... | collective-permute-start | bytes 1376264 | tf_op jit(solution)/shard_map/ppermute | solution.py:24
  37.1 14.7 %collective-permute-done.b_ref = f32[96,1024]{1,0:T(8,128)S(1)} collective-permute-done((f32[96,1024]{1,0:T(8,128)S(1)}, f32[96,1024]{1,0:T(8,128)S(1)}, u32[]{:S(2)}, u32[]{:S(2)}) %collective-permute-start) | collective-permute-done | bytes 393248 | tf_op jit(solution)/shard_map/ppermute | solution.py:24
  51.8 0.0 collective-permute-done.1.c_ref
  51.8 0.0 collective-permute-done.2.d_ref
  51.8 0.1 shard_map.52.after_ref
  51.9 0.6 collective-permute-start.9
  52.4 0.6 collective-permute-start.3
  53.0 2.1 %collective-permute-start.4 = (f32[96,1024]{1,0:T(8,128)S(1)}, f32[96,1024]{1,0:T(8,128)S(1)}, u32[]{:S(2)}, u32[]{:S(2)}) collective-permute-start(f32[96,1024]{1,0:T(8,128)S(1)} %get-tuple-element.39), channel_id=1, source_target_pairs={{0,6},{8,14},{1,7},{9,15},{16,22},{24,30},{17,23},{25,31},{32,38},... | collective-permute-start | bytes 1179656 | tf_op jit(solution)/shard_map/ppermute | solution.py:24
  55.1 0.9 collective-permute-start.5
  56.0 0.0 collective-permute-done.7.got_ref
  56.0 0.1 shard_map.56
  56.1 0.0 copy-start.2
  56.1 1.3 collective-permute-start.8
  57.4 1.1 shard_map.53.emb_t_ref
  58.4 2.9 %collective-permute-done.8.got_ref = f32[64,896]{1,0:T(8,128)S(1)} collective-permute-done((f32[64,896]{1,0:T(8,128)S(1)}, f32[64,896]{1,0:T(8,128)S(1)}, u32[]{:S(2)}, u32[]{:S(2)}) %collective-permute-start.8) | collective-permute-done | bytes 229408 | tf_op jit(solution)/shard_map/ppermute | solution.py:24
  61.4 6.2 %collective-permute-done.9.e_ref = f32[96,1024]{1,0:T(8,128)S(1)} collective-permute-done((f32[96,1024]{1,0:T(8,128)S(1)}, f32[96,1024]{1,0:T(8,128)S(1)}, u32[]{:S(2)}, u32[]{:S(2)}) %collective-permute-start.9) | collective-permute-done | bytes 393248 | tf_op jit(solution)/shard_map/ppermute | solution.py:24
  67.6 7.8 %collective-permute-start.10 = (f32[32,896]{1,0:T(8,128)S(1)}, f32[32,896]{1,0:T(8,128)S(1)}, u32[]{:S(2)}, u32[]{:S(2)}) collective-permute-start(f32[32,896]{1,0:T(8,128)S(1)} %get-tuple-element.51), channel_id=1, source_target_pairs={{0,32},{8,40},{1,33},{9,41},{16,48},{24,56},{17,49},{25,57},{32,0}... | collective-permute-start | bytes 344072 | tf_op jit(solution)/shard_map/ppermute | solution.py:24
  75.3 0.0 collective-permute-done.3.b_ref
  75.3 0.0 collective-permute-done.4.c_ref
  75.3 0.0 collective-permute-done.5.d_ref
  75.3 5.8 %shard_map.58 = f32[32,8,256]{2,1,0:T(8,128)} custom-call(s32[5]{0:T(128)S(1)} %stack.23.place_ref, f32[96,8,256]{2,1,0:T(8,128)S(1)} %copy-done.2, f32[96,1024]{1,0:T(8,128)S(1)} %shard_map.53.emb_t_ref, f32[96,1024]{1,0:T(8,128)S(1)} %get-tuple-element.37.a_ref, f32[96,1024]{1,0:T(8,128)S(1)} %collective-permute-done.3.b_ref, ...), custom_call_target="tpu_custom_call" | custom-call | flops 12884901888 | bytes 6291496 | tf_op jit(solution)/shard_map/pallas_call | solution.py:52
  81.2 0.0 collective-permute-done.10.got_ref
  81.2 7.8 %all-to-all-start.1 = ((f32[32,8,256]{2,1,0:T(8,128)}), f32[32,8,256]{2,1,0:T(8,128)S(1)}, u32[]{:S(2)}, u32[]{:S(2)}) async-start(f32[32,8,256]{2,1,0:T(8,128)} %shard_map.58), calls=%async_computation.1 | async-start | bytes 524288 | tf_op jit(solution)/shard_map/all_to_all | solution.py:347
  89.0 1.5 %collective-permute-start.11 = (f32[16,896]{1,0:T(8,128)S(1)}, f32[16,896]{1,0:T(8,128)S(1)}, u32[]{:S(2)}, u32[]{:S(2)}) collective-permute-start(f32[16,896]{1,0:T(8,128)S(1)} %get-tuple-element.56), channel_id=1, source_target_pairs={{0,16},{8,24},{1,17},{9,25},{16,0},{24,8},{17,1},{25,9},{32,48},{4... | collective-permute-start | bytes 172040 | tf_op jit(solution)/shard_map/ppermute | solution.py:24
  90.5 4.7 %collective-permute-done.11.got_ref = f32[16,896]{1,0:T(8,128)S(1)} collective-permute-done((f32[16,896]{1,0:T(8,128)S(1)}, f32[16,896]{1,0:T(8,128)S(1)}, u32[]{:S(2)}, u32[]{:S(2)}) %collective-permute-start.11) | collective-permute-done | bytes 57376 | tf_op jit(solution)/shard_map/ppermute | solution.py:24
  95.2 0.1 shard_map.61
  95.3 3.5 %collective-permute-start.14 = (f32[16,768]{1,0:T(8,128)S(1)}, f32[16,768]{1,0:T(8,128)S(1)}, u32[]{:S(2)}, u32[]{:S(2)}) collective-permute-start(f32[16,768]{1,0:T(8,128)S(1)} %shard_map.61), channel_id=1, source_target_pairs={{0,48},{8,56},{1,49},{9,57},{16,32},{24,40},{17,33},{25,41},{32,16... | collective-permute-start | bytes 147464 | tf_op jit(solution)/shard_map/ppermute | solution.py:24
  98.8 0.2 collective-permute-start.13
  99.0 0.2 collective-permute-start.12
  99.2 1.0 all-to-all-done.1.parts_ref
  100.2 1.4 %shard_map.59.after_ref = f32[32,8,128]{2,1,0:T(8,128)} custom-call(s32[5]{0:T(128)S(1)} %stack.23.place_ref, f32[768,256]{1,0:T(8,128)S(1)} %bitcast.10, f32[32,8,256]{2,1,0:T(8,128)S(1)} %all-to-all-done.1.parts_ref), custom_call_target="tpu_custom_call" | custom-call | bytes 2097192 | tf_op jit(solution)/shard_map/pallas_call | solution.py:52
  101.6 5.9 %all-to-all-start.2 = ((f32[32,8,128]{2,1,0:T(8,128)}), f32[32,8,128]{2,1,0:T(8,128)S(1)}, u32[]{:S(2)}, u32[]{:S(2)}) async-start(f32[32,8,128]{2,1,0:T(8,128)} %shard_map.59.after_ref), calls=%async_computation.2 | async-start | bytes 262144 | tf_op jit(solution)/shard_map/all_to_all | solution.py:367
  107.5 0.0 collective-permute-done.14
  107.5 0.0 collective-permute-done.13
  107.5 0.0 collective-permute-done.12
  107.6 2.6 %collective-permute-start.17 = (f32[64,768]{1,0:T(8,128)S(1)}, f32[64,768]{1,0:T(8,128)S(1)}, u32[]{:S(2)}, u32[]{:S(2)}) collective-permute-start(f32[64,768]{1,0:T(8,128)S(1)} %shard_map.62), channel_id=1, source_target_pairs={{0,192},{8,200},{1,193},{9,201},{16,208},{24,216},{17,209},{25,217... | collective-permute-start | bytes 589832 | tf_op jit(solution)/shard_map/ppermute | solution.py:24
  110.2 0.6 collective-permute-start.16
  110.8 0.2 collective-permute-start.15
  110.9 5.7 %all-to-all-done.2 = f32[32,8,128]{2,1,0:T(8,128)S(1)} async-done(((f32[32,8,128]{2,1,0:T(8,128)}), f32[32,8,128]{2,1,0:T(8,128)S(1)}, u32[]{:S(2)}, u32[]{:S(2)}) %all-to-all-start.2) | async-done | bytes 131104 | tf_op jit(solution)/shard_map/all_to_all | solution.py:367
  116.6 0.8 broadcast_in_dim.2
  117.5 4.2 %all-to-all-start.3 = ((f32[4,32,8,128]{3,2,1,0:T(8,128)}), f32[4,32,8,128]{3,2,1,0:T(8,128)S(1)}, u32[]{:S(2)}, u32[]{:S(2)}) async-start(f32[4,32,8,128]{3,2,1,0:T(8,128)} %broadcast_in_dim.2), calls=%async_computation.3 | async-start | bytes 1048576 | tf_op jit(solution)/shard_map/all_to_all | solution.py:372
  121.6 0.0 collective-permute-done.17
  121.7 0.0 collective-permute-done.16
  121.7 0.1 pad_maximum_fusion.mine_ref
  121.7 3.3 %collective-permute-start.18 = (f32[256,768]{1,0:T(8,128)S(1)}, f32[256,768]{1,0:T(8,128)S(1)}, u32[]{:S(2)}, u32[]{:S(2)}) collective-permute-start(f32[256,768]{1,0:T(8,128)S(1)} %pad_maximum_fusion.mine_ref), channel_id=1, source_target_pairs={{0,8},{8,0},{1,9},{9,1},{16,24},{24,16},{17,25},{25,17},{32,40},{4... | collective-permute-start | bytes 2359304 | tf_op jit(solution)/shard_map/ppermute | solution.py:24
  125.0 3.5 %all-to-all-done.3 = f32[4,32,8,128]{3,2,1,0:T(8,128)S(1)} async-done(((f32[4,32,8,128]{3,2,1,0:T(8,128)}), f32[4,32,8,128]{3,2,1,0:T(8,128)S(1)}, u32[]{:S(2)}, u32[]{:S(2)}) %all-to-all-start.3) | async-done | bytes 524320 | tf_op jit(solution)/shard_map/all_to_all | solution.py:372
  128.6 4.4 %collective-permute-start.19 = (f32[128,8,128]{2,1,0:T(8,128)S(1)}, f32[128,8,128]{2,1,0:T(8,128)S(1)}, u32[]{:S(2)}, u32[]{:S(2)}) collective-permute-start(f32[128,8,128]{2,1,0:T(8,128)S(1)} %bitcast.8), channel_id=1, source_target_pairs={{0,8},{8,0},{1,9},{9,1},{16,24},{24,16},{17,25},{25,17},{32,40},{4... | collective-permute-start | bytes 1572872 | tf_op jit(solution)/shard_map/ppermute | solution.py:24
  133.0 1.8 %shard_map.63 = f32[512,768]{1,0:T(8,128)} custom-call(s32[5]{0:T(128)S(1)} %stack.23.place_ref, f32[256,768]{1,0:T(8,128)S(1)} %pad_maximum_fusion.mine_ref, f32[256,768]{1,0:T(8,128)S(1)} %collective-permute-done.18.theirs_ref), custom_call_target="tpu_custom_call" | custom-call | bytes 3145768 | tf_op jit(solution)/shard_map/pallas_call | solution.py:52
  134.8 0.0 collective-permute-done.19.theirs_ref
  134.8 1.6 %shard_map.64 = f32[768,256]{1,0:T(8,128)} custom-call(s32[5]{0:T(128)S(1)} %stack.23.place_ref, f32[128,8,128]{2,1,0:T(8,128)S(1)} %bitcast.9, f32[128,8,128]{2,1,0:T(8,128)S(1)} %collective-permute-done.19.theirs_ref), custom_call_target="tpu_custom_call" | custom-call | bytes 2097192 | tf_op jit(solution)/shard_map/pallas_call | solution.py:52
  (10 shorter events, 0.1 us)
Async XLA Ops:
  0.8 1.4 %copy-start = (bf16[1024,768]{1,0:T(8,128)(2,1)S(1)}, bf16[1024,768]{1,0:T(8,128)(2,1)}, u32[]{:S(2)}) copy-start(bf16[1024,768]{1,0:T(8,128)(2,1)} %emb_ref.5) | copy-start | bytes 4718596
  2.2 1.1 copy-start.3
  5.4 22.9 %copy-start.1 = (bf16[1024,768]{1,0:T(8,128)(2,1)S(1)}, bf16[1024,768]{1,0:T(8,128)(2,1)}, u32[]{:S(2)}) copy-start(bf16[1024,768]{1,0:T(8,128)(2,1)} %emb_ref.5) | copy-start | bytes 4718596
  29.3 4.9 %collective-permute-start.6 = (f32[256,896]{1,0:T(8,128)S(1)}, f32[256,896]{1,0:T(8,128)S(1)}, u32[]{:S(2)}, u32[]{:S(2)}) collective-permute-start(f32[256,896]{1,0:T(8,128)S(1)} %get-tuple-element.44), channel_id=1, source_target_pairs={{0,8},{8,0},{1,9},{9,1},{16,24},{24,16},{17,25},{25,17},{32,40},{4... | collective-permute-start | bytes 2752520 | tf_op jit(solution)/shard_map/ppermute | solution.py:24
  31.5 20.3 %collective-permute-start = (f32[96,1024]{1,0:T(8,128)S(1)}, f32[96,1024]{1,0:T(8,128)S(1)}, u32[]{:S(2)}, u32[]{:S(2)}) collective-permute-start(f32[96,1024]{1,0:T(8,128)S(1)} %get-tuple-element.34), channel_id=1, source_target_pairs={{0,2},{8,10},{1,3},{9,11},{16,18},{24,26},{17,19},{25,27},{32,34},... | collective-permute-start | bytes 1179656 | tf_op jit(solution)/shard_map/ppermute | solution.py:24
  31.8 20.0 %collective-permute-start.1 = (f32[96,1024]{1,0:T(8,128)S(1)}, f32[96,1024]{1,0:T(8,128)S(1)}, u32[]{:S(2)}, u32[]{:S(2)}) collective-permute-start(f32[96,1024]{1,0:T(8,128)S(1)} %get-tuple-element.35), channel_id=1, source_target_pairs={{0,6},{8,14},{1,7},{9,15},{16,22},{24,30},{17,23},{25,31},{32,38},... | collective-permute-start | bytes 1179656 | tf_op jit(solution)/shard_map/ppermute | solution.py:24
  34.2 17.6 %collective-permute-start.2 = (f32[96,1024]{1,0:T(8,128)S(1)}, f32[96,1024]{1,0:T(8,128)S(1)}, u32[]{:S(2)}, u32[]{:S(2)}) collective-permute-start(f32[96,1024]{1,0:T(8,128)S(1)} %get-tuple-element.36), channel_id=1, source_target_pairs={{0,4},{8,12},{1,5},{9,13},{16,20},{24,28},{17,21},{25,29},{32,36},... | collective-permute-start | bytes 1179656 | tf_op jit(solution)/shard_map/ppermute | solution.py:24
  34.3 21.7 %collective-permute-start.7 = (f32[128,896]{1,0:T(8,128)S(1)}, f32[128,896]{1,0:T(8,128)S(1)}, u32[]{:S(2)}, u32[]{:S(2)}) collective-permute-start(f32[128,896]{1,0:T(8,128)S(1)} %get-tuple-element.46), channel_id=1, source_target_pairs={{0,128},{8,136},{1,129},{9,137},{16,144},{24,152},{17,145},{25,153... | collective-permute-start | bytes 1376264 | tf_op jit(solution)/shard_map/ppermute | solution.py:24
  51.9 15.7 %collective-permute-start.9 = (f32[96,1024]{1,0:T(8,128)S(1)}, f32[96,1024]{1,0:T(8,128)S(1)}, u32[]{:S(2)}, u32[]{:S(2)}) collective-permute-start(f32[96,1024]{1,0:T(8,128)S(1)} %shard_map.52.after_ref), channel_id=1, source_target_pairs={{0,1},{8,9},{1,0},{9,8},{16,17},{24,25},{17,16},{25,24},{32,33},{4... | collective-permute-start | bytes 1179656 | tf_op jit(solution)/shard_map/ppermute | solution.py:24
  52.4 22.9 %collective-permute-start.3 = (f32[96,1024]{1,0:T(8,128)S(1)}, f32[96,1024]{1,0:T(8,128)S(1)}, u32[]{:S(2)}, u32[]{:S(2)}) collective-permute-start(f32[96,1024]{1,0:T(8,128)S(1)} %get-tuple-element.38), channel_id=1, source_target_pairs={{0,2},{8,10},{1,3},{9,11},{16,18},{24,26},{17,19},{25,27},{32,34},... | collective-permute-start | bytes 1179656 | tf_op jit(solution)/shard_map/ppermute | solution.py:24
  53.0 22.3 %collective-permute-start.4 = (f32[96,1024]{1,0:T(8,128)S(1)}, f32[96,1024]{1,0:T(8,128)S(1)}, u32[]{:S(2)}, u32[]{:S(2)}) collective-permute-start(f32[96,1024]{1,0:T(8,128)S(1)} %get-tuple-element.39), channel_id=1, source_target_pairs={{0,6},{8,14},{1,7},{9,15},{16,22},{24,30},{17,23},{25,31},{32,38},... | collective-permute-start | bytes 1179656 | tf_op jit(solution)/shard_map/ppermute | solution.py:24
  55.1 20.2 %collective-permute-start.5 = (f32[96,1024]{1,0:T(8,128)S(1)}, f32[96,1024]{1,0:T(8,128)S(1)}, u32[]{:S(2)}, u32[]{:S(2)}) collective-permute-start(f32[96,1024]{1,0:T(8,128)S(1)} %get-tuple-element.40), channel_id=1, source_target_pairs={{0,4},{8,12},{1,5},{9,13},{16,20},{24,28},{17,21},{25,29},{32,36},... | collective-permute-start | bytes 1179656 | tf_op jit(solution)/shard_map/ppermute | solution.py:24
  56.1 19.3 %copy-start.2 = (f32[96,8,256]{2,1,0:T(8,128)S(1)}, f32[96,8,256]{2,1,0:T(8,128)}, u32[]{:S(2)}) copy-start(f32[96,8,256]{2,1,0:T(8,128)} %all_books_ref.1) | copy-start | bytes 2359300
  56.1 5.3 %collective-permute-start.8 = (f32[64,896]{1,0:T(8,128)S(1)}, f32[64,896]{1,0:T(8,128)S(1)}, u32[]{:S(2)}, u32[]{:S(2)}) collective-permute-start(f32[64,896]{1,0:T(8,128)S(1)} %get-tuple-element.48), channel_id=1, source_target_pairs={{0,64},{8,72},{1,65},{9,73},{16,80},{24,88},{17,81},{25,89},{32,96... | collective-permute-start | bytes 688136 | tf_op jit(solution)/shard_map/ppermute | solution.py:24
  67.6 13.6 %collective-permute-start.10 = (f32[32,896]{1,0:T(8,128)S(1)}, f32[32,896]{1,0:T(8,128)S(1)}, u32[]{:S(2)}, u32[]{:S(2)}) collective-permute-start(f32[32,896]{1,0:T(8,128)S(1)} %get-tuple-element.51), channel_id=1, source_target_pairs={{0,32},{8,40},{1,33},{9,41},{16,48},{24,56},{17,49},{25,57},{32,0}... | collective-permute-start | bytes 344072 | tf_op jit(solution)/shard_map/ppermute | solution.py:24
  81.2 19.0 %all-to-all-start.1 = ((f32[32,8,256]{2,1,0:T(8,128)}), f32[32,8,256]{2,1,0:T(8,128)S(1)}, u32[]{:S(2)}, u32[]{:S(2)}) async-start(f32[32,8,256]{2,1,0:T(8,128)} %shard_map.58), calls=%async_computation.1 | async-start | bytes 524288 | tf_op jit(solution)/shard_map/all_to_all | solution.py:347
  89.0 6.2 %collective-permute-start.11 = (f32[16,896]{1,0:T(8,128)S(1)}, f32[16,896]{1,0:T(8,128)S(1)}, u32[]{:S(2)}, u32[]{:S(2)}) collective-permute-start(f32[16,896]{1,0:T(8,128)S(1)} %get-tuple-element.56), channel_id=1, source_target_pairs={{0,16},{8,24},{1,17},{9,25},{16,0},{24,8},{17,1},{25,9},{32,48},{4... | collective-permute-start | bytes 172040 | tf_op jit(solution)/shard_map/ppermute | solution.py:24
  95.3 12.2 %collective-permute-start.14 = (f32[16,768]{1,0:T(8,128)S(1)}, f32[16,768]{1,0:T(8,128)S(1)}, u32[]{:S(2)}, u32[]{:S(2)}) collective-permute-start(f32[16,768]{1,0:T(8,128)S(1)} %shard_map.61), channel_id=1, source_target_pairs={{0,48},{8,56},{1,49},{9,57},{16,32},{24,40},{17,33},{25,41},{32,16... | collective-permute-start | bytes 147464 | tf_op jit(solution)/shard_map/ppermute | solution.py:24
  98.8 8.7 %collective-permute-start.13 = (f32[16,768]{1,0:T(8,128)S(1)}, f32[16,768]{1,0:T(8,128)S(1)}, u32[]{:S(2)}, u32[]{:S(2)}) collective-permute-start(f32[16,768]{1,0:T(8,128)S(1)} %shard_map.61), channel_id=1, source_target_pairs={{0,32},{8,40},{1,33},{9,41},{16,48},{24,56},{17,49},{25,57},{32,0}... | collective-permute-start | bytes 147464 | tf_op jit(solution)/shard_map/ppermute | solution.py:24
  99.0 8.5 %collective-permute-start.12 = (f32[16,768]{1,0:T(8,128)S(1)}, f32[16,768]{1,0:T(8,128)S(1)}, u32[]{:S(2)}, u32[]{:S(2)}) collective-permute-start(f32[16,768]{1,0:T(8,128)S(1)} %shard_map.61), channel_id=1, source_target_pairs={{0,16},{8,24},{1,17},{9,25},{16,0},{24,8},{17,1},{25,9},{32,48},{4... | collective-permute-start | bytes 147464 | tf_op jit(solution)/shard_map/ppermute | solution.py:24
  101.6 15.1 %all-to-all-start.2 = ((f32[32,8,128]{2,1,0:T(8,128)}), f32[32,8,128]{2,1,0:T(8,128)S(1)}, u32[]{:S(2)}, u32[]{:S(2)}) async-start(f32[32,8,128]{2,1,0:T(8,128)} %shard_map.59.after_ref), calls=%async_computation.2 | async-start | bytes 262144 | tf_op jit(solution)/shard_map/all_to_all | solution.py:367
  107.6 14.1 %collective-permute-start.17 = (f32[64,768]{1,0:T(8,128)S(1)}, f32[64,768]{1,0:T(8,128)S(1)}, u32[]{:S(2)}, u32[]{:S(2)}) collective-permute-start(f32[64,768]{1,0:T(8,128)S(1)} %shard_map.62), channel_id=1, source_target_pairs={{0,192},{8,200},{1,193},{9,201},{16,208},{24,216},{17,209},{25,217... | collective-permute-start | bytes 589832 | tf_op jit(solution)/shard_map/ppermute | solution.py:24
  110.2 11.5 %collective-permute-start.16 = (f32[64,768]{1,0:T(8,128)S(1)}, f32[64,768]{1,0:T(8,128)S(1)}, u32[]{:S(2)}, u32[]{:S(2)}) collective-permute-start(f32[64,768]{1,0:T(8,128)S(1)} %shard_map.62), channel_id=1, source_target_pairs={{0,128},{8,136},{1,129},{9,137},{16,144},{24,152},{17,145},{25,153... | collective-permute-start | bytes 589832 | tf_op jit(solution)/shard_map/ppermute | solution.py:24
  110.8 10.9 %collective-permute-start.15 = (f32[64,768]{1,0:T(8,128)S(1)}, f32[64,768]{1,0:T(8,128)S(1)}, u32[]{:S(2)}, u32[]{:S(2)}) collective-permute-start(f32[64,768]{1,0:T(8,128)S(1)} %shard_map.62), channel_id=1, source_target_pairs={{0,64},{8,72},{1,65},{9,73},{16,80},{24,88},{17,81},{25,89},{32,96... | collective-permute-start | bytes 589832 | tf_op jit(solution)/shard_map/ppermute | solution.py:24
  117.5 11.1 %all-to-all-start.3 = ((f32[4,32,8,128]{3,2,1,0:T(8,128)}), f32[4,32,8,128]{3,2,1,0:T(8,128)S(1)}, u32[]{:S(2)}, u32[]{:S(2)}) async-start(f32[4,32,8,128]{3,2,1,0:T(8,128)} %broadcast_in_dim.2), calls=%async_computation.3 | async-start | bytes 1048576 | tf_op jit(solution)/shard_map/all_to_all | solution.py:372
  121.7 11.2 %collective-permute-start.18 = (f32[256,768]{1,0:T(8,128)S(1)}, f32[256,768]{1,0:T(8,128)S(1)}, u32[]{:S(2)}, u32[]{:S(2)}) collective-permute-start(f32[256,768]{1,0:T(8,128)S(1)} %pad_maximum_fusion.mine_ref), channel_id=1, source_target_pairs={{0,8},{8,0},{1,9},{9,1},{16,24},{24,16},{17,25},{25,17},{32,40},{4... | collective-permute-start | bytes 2359304 | tf_op jit(solution)/shard_map/ppermute | solution.py:24
  128.6 6.2 %collective-permute-start.19 = (f32[128,8,128]{2,1,0:T(8,128)S(1)}, f32[128,8,128]{2,1,0:T(8,128)S(1)}, u32[]{:S(2)}, u32[]{:S(2)}) collective-permute-start(f32[128,8,128]{2,1,0:T(8,128)S(1)} %bitcast.8), channel_id=1, source_target_pairs={{0,8},{8,0},{1,9},{9,1},{16,24},{24,16},{17,25},{25,17},{32,40},{4... | collective-permute-start | bytes 1572872 | tf_op jit(solution)/shard_map/ppermute | solution.py:24

commit v7 on v6

--- a/solution.py
+++ b/solution.py
@@ -299,7 +299,7 @@
         flops=2 * rows_here * held * width,
     )
     wb, counts, theirs, mine = outs[0], outs[1], outs[2:6], outs[6:10]
-    steps = (1, -1, 2)
+    steps = (2, 1, -1)
     got = [hop(theirs[k % NY], along_y(k)) for k in steps]
     got_mine = [hop(mine[k % NY], along_y(k)) for k in steps]
     total = call(add_kernel, shape((share, rows_here)), (theirs[0], *got))

time: 137 us -> 136 us (level)
    all_to_all x1, starting transfers between devices: 5.91 us -> 4.5 us  [body(): lax.all_to_all(tile, BOTH, 0, 0, tiled=True, axis_index_groups=same_line)]
  transfers between devices with their start and end apart: 23 -> 23, of which waited for: 7 -> 8; matrix products, arithmetic and copies ran while one was open for 1% -> 1% of each run, Pallas kernels for 8% -> 8%
where the time goes in v7:
time: 136 us
  starting transfers between devices  54.1 us (40%)
  waiting for transfers between devices  39.1 us (29%)
  blocking collectives  20.7 us (15%)
  Pallas kernels  17.3 us (13%)
  local copies, waits for them, and re-layouts  3.47 us (3%)
    ppermute x20, starting transfers between devices, hop(): return lax.ppermute(value, BOTH, pairs)  38 us
    ppermute x20, waiting for transfers between devices, hop(): return lax.ppermute(value, BOTH, pairs)  28.9 us
    all_to_all x1, blocking collectives, body(): stats = lax.all_to_all(stat, 'cent', 0, 0, tiled=True)  20.7 us
    pallas_call x15, Pallas kernels, call(): pl.pallas_call(kernel, out_shape=out, in_specs=specs, out_specs=jax.tree....  17.3 us
    all_to_all x1, starting transfers between devices, body(): all_parts = lax.all_to_all(sums, 'rows', 0, 0, tiled=True)  7.4 us
    all_to_all x1, waiting for transfers between devices, body(): lax.all_to_all(tile, BOTH, 0, 0, tiled=True, axis_index_groups=same_line)  5.73 us
    all_to_all x1, starting transfers between devices, body(): lax.all_to_all(tile, BOTH, 0, 0, tiled=True, axis_index_groups=same_line)  4.5 us
    all_to_all x1, starting transfers between devices, body(): lax.all_to_all(lines, 'rows', 0, 0, tiled=True, axis_index_groups=across)  4.17 us
  transfers between devices with their start and end apart: 23, of which 8 were waited for; matrix products, arithmetic and copies ran while one was open for 1% of the time, Pallas kernels for 8%

profile of v7, /device:TPU:1, one launch (start us, length us, event | category | flops | bytes accessed | tf_op | source)
XLA Modules:
  0.0 135.6 jit_solution(71657180524821568)
XLA Ops:
  0.7 0.1 stack.23.place_ref
  0.8 1.4 %copy-done = bf16[1024,768]{1,0:T(8,128)(2,1)S(1)} copy-done((bf16[1024,768]{1,0:T(8,128)(2,1)S(1)}, bf16[1024,768]{1,0:T(8,128)(2,1)}, u32[]{:S(2)}) %copy-start) | copy-done | bytes 1572888
  2.2 1.1 copy-done.3
  3.3 2.1 %shard_map.50 = (f32[512,1024]{1,0:T(8,128)S(1)}, f32[8,16,128]{2,1,0:T(8,128)S(1)}, bf16[768,512]{1,0:T(8,128)(2,1)S(1)}, f32[16,768]{1,0:T(8,128)S(1)}) custom-call(s32[5]{0:T(128)S(1)} %stack.23.place_ref, bf16[1024,768]{1,0:T(8,128)(2,1)S(1)} %copy-done, bf16[512,768]{1,0:T(8,128)(2,1)S(1)} %copy-done.3), custom_call_target="tpu_custom_call" | custom-call | flops 805306368 | bytes 4718632 | tf_op jit(solution)/shard_map/pallas_call | solution.py:52
  5.4 0.0 copy-start.1
  5.4 20.7 %all_to_all.20.stat_ref = f32[8,16,128]{2,1,0:T(8,128)S(1)} all-to-all(f32[8,16,128]{2,1,0:T(8,128)S(1)} %get-tuple-element.31.mine_ref), channel_id=1, replica_groups=mesh['rows'=32,'cent'=8] {'cent'}, dimensions={0} | all-to-all | bytes 131072 | tf_op jit(solution)/shard_map/all_to_all | solution.py:293
  26.1 2.2 %shard_map.51 = (bf16[512,1024]{1,0:T(8,128)(2,1)S(1)}, f32[512,128]{1,0:T(8,128)S(1)}, f32[96,1024]{1,0:T(8,128)S(1)}, f32[96,1024]{1,0:T(8,128)S(1)}, f32[96,1...) custom-call(s32[5]{0:T(128)S(1)} %stack.23.place_ref, ...), custom_call_target="tpu_custom_call" | custom-call | flops 805306368 | bytes 6029352 | tf_op jit(solution)/shard_map/pallas_call | solution.py:52
  28.3 1.0 shard_map.54
  29.3 2.2 %collective-permute-start.6 = (f32[256,896]{1,0:T(8,128)S(1)}, f32[256,896]{1,0:T(8,128)S(1)}, u32[]{:S(2)}, u32[]{:S(2)}) collective-permute-start(f32[256,896]{1,0:T(8,128)S(1)} %get-tuple-element.44), channel_id=1, source_target_pairs={{0,8},{8,0},{1,9},{9,1},{16,24},{24,16},{17,25},{25,17},{32,40},{4... | collective-permute-start | bytes 2752520 | tf_op jit(solution)/shard_map/ppermute | solution.py:24
  31.5 1.0 collective-permute-start
  32.5 0.5 collective-permute-start.1
  33.0 2.2 %collective-permute-start.2 = (f32[96,1024]{1,0:T(8,128)S(1)}, f32[96,1024]{1,0:T(8,128)S(1)}, u32[]{:S(2)}, u32[]{:S(2)}) collective-permute-start(f32[96,1024]{1,0:T(8,128)S(1)} %get-tuple-element.36), channel_id=1, source_target_pairs={{0,6},{8,14},{1,7},{9,15},{16,22},{24,30},{17,23},{25,31},{32,38},... | collective-permute-start | bytes 1179656 | tf_op jit(solution)/shard_map/ppermute | solution.py:24
  35.2 0.0 collective-permute-done.6.got_ref
  35.2 0.1 shard_map.55
  35.3 2.8 %collective-permute-start.7 = (f32[128,896]{1,0:T(8,128)S(1)}, f32[128,896]{1,0:T(8,128)S(1)}, u32[]{:S(2)}, u32[]{:S(2)}) collective-permute-start(f32[128,896]{1,0:T(8,128)S(1)} %get-tuple-element.46), channel_id=1, source_target_pairs={{0,128},{8,136},{1,129},{9,137},{16,144},{24,152},{17,145},{25,153... | collective-permute-start | bytes 1376264 | tf_op jit(solution)/shard_map/ppermute | solution.py:24
  38.1 5.6 %collective-permute-done.b_ref = f32[96,1024]{1,0:T(8,128)S(1)} collective-permute-done((f32[96,1024]{1,0:T(8,128)S(1)}, f32[96,1024]{1,0:T(8,128)S(1)}, u32[]{:S(2)}, u32[]{:S(2)}) %collective-permute-start) | collective-permute-done | bytes 393248 | tf_op jit(solution)/shard_map/ppermute | solution.py:24
  43.7 8.8 %collective-permute-done.1.c_ref = f32[96,1024]{1,0:T(8,128)S(1)} collective-permute-done((f32[96,1024]{1,0:T(8,128)S(1)}, f32[96,1024]{1,0:T(8,128)S(1)}, u32[]{:S(2)}, u32[]{:S(2)}) %collective-permute-start.1) | collective-permute-done | bytes 393248 | tf_op jit(solution)/shard_map/ppermute | solution.py:24
  52.5 0.0 collective-permute-done.2.d_ref
  52.5 0.1 shard_map.52.after_ref
  52.6 0.6 collective-permute-start.9
  53.1 0.7 collective-permute-start.3
  53.8 0.7 collective-permute-start.4
  54.6 2.0 %collective-permute-start.5 = (f32[96,1024]{1,0:T(8,128)S(1)}, f32[96,1024]{1,0:T(8,128)S(1)}, u32[]{:S(2)}, u32[]{:S(2)}) collective-permute-start(f32[96,1024]{1,0:T(8,128)S(1)} %get-tuple-element.40), channel_id=1, source_target_pairs={{0,6},{8,14},{1,7},{9,15},{16,22},{24,30},{17,23},{25,31},{32,38},... | collective-permute-start | bytes 1179656 | tf_op jit(solution)/shard_map/ppermute | solution.py:24
  56.5 0.0 collective-permute-done.7.got_ref
  56.5 0.1 shard_map.56
  56.6 0.0 copy-start.2
  56.6 1.3 collective-permute-start.8
  57.9 1.1 shard_map.53.emb_t_ref
  59.0 3.0 %collective-permute-done.8.got_ref = f32[64,896]{1,0:T(8,128)S(1)} collective-permute-done((f32[64,896]{1,0:T(8,128)S(1)}, f32[64,896]{1,0:T(8,128)S(1)}, u32[]{:S(2)}, u32[]{:S(2)}) %collective-permute-start.8) | collective-permute-done | bytes 229408 | tf_op jit(solution)/shard_map/ppermute | solution.py:24
  62.0 6.7 %collective-permute-done.9.e_ref = f32[96,1024]{1,0:T(8,128)S(1)} collective-permute-done((f32[96,1024]{1,0:T(8,128)S(1)}, f32[96,1024]{1,0:T(8,128)S(1)}, u32[]{:S(2)}, u32[]{:S(2)}) %collective-permute-start.9) | collective-permute-done | bytes 393248 | tf_op jit(solution)/shard_map/ppermute | solution.py:24
  68.7 7.7 %collective-permute-start.10 = (f32[32,896]{1,0:T(8,128)S(1)}, f32[32,896]{1,0:T(8,128)S(1)}, u32[]{:S(2)}, u32[]{:S(2)}) collective-permute-start(f32[32,896]{1,0:T(8,128)S(1)} %get-tuple-element.51), channel_id=1, source_target_pairs={{0,32},{8,40},{1,33},{9,41},{16,48},{24,56},{17,49},{25,57},{32,0}... | collective-permute-start | bytes 344072 | tf_op jit(solution)/shard_map/ppermute | solution.py:24
  76.4 0.0 collective-permute-done.3.b_ref
  76.4 0.0 collective-permute-done.4.c_ref
  76.4 0.0 collective-permute-done.5.d_ref
  76.4 5.8 %shard_map.58 = f32[32,8,256]{2,1,0:T(8,128)} custom-call(s32[5]{0:T(128)S(1)} %stack.23.place_ref, f32[96,8,256]{2,1,0:T(8,128)S(1)} %copy-done.2, f32[96,1024]{1,0:T(8,128)S(1)} %shard_map.53.emb_t_ref, f32[96,1024]{1,0:T(8,128)S(1)} %get-tuple-element.37.a_ref, f32[96,1024]{1,0:T(8,128)S(1)} %collective-permute-done.3.b_ref, ...), custom_call_target="tpu_custom_call" | custom-call | flops 12884901888 | bytes 6291496 | tf_op jit(solution)/shard_map/pallas_call | solution.py:52
  82.2 0.0 collective-permute-done.10.got_ref
  82.2 7.4 %all-to-all-start.1 = ((f32[32,8,256]{2,1,0:T(8,128)}), f32[32,8,256]{2,1,0:T(8,128)S(1)}, u32[]{:S(2)}, u32[]{:S(2)}) async-start(f32[32,8,256]{2,1,0:T(8,128)} %shard_map.58), calls=%async_computation.1 | async-start | bytes 524288 | tf_op jit(solution)/shard_map/all_to_all | solution.py:347
  89.7 1.5 %collective-permute-start.11 = (f32[16,896]{1,0:T(8,128)S(1)}, f32[16,896]{1,0:T(8,128)S(1)}, u32[]{:S(2)}, u32[]{:S(2)}) collective-permute-start(f32[16,896]{1,0:T(8,128)S(1)} %get-tuple-element.56), channel_id=1, source_target_pairs={{0,16},{8,24},{1,17},{9,25},{16,0},{24,8},{17,1},{25,9},{32,48},{4... | collective-permute-start | bytes 172040 | tf_op jit(solution)/shard_map/ppermute | solution.py:24
  91.2 4.7 %collective-permute-done.11.got_ref = f32[16,896]{1,0:T(8,128)S(1)} collective-permute-done((f32[16,896]{1,0:T(8,128)S(1)}, f32[16,896]{1,0:T(8,128)S(1)}, u32[]{:S(2)}, u32[]{:S(2)}) %collective-permute-start.11) | collective-permute-done | bytes 57376 | tf_op jit(solution)/shard_map/ppermute | solution.py:24
  95.9 0.1 shard_map.61
  95.9 3.5 %collective-permute-start.14 = (f32[16,768]{1,0:T(8,128)S(1)}, f32[16,768]{1,0:T(8,128)S(1)}, u32[]{:S(2)}, u32[]{:S(2)}) collective-permute-start(f32[16,768]{1,0:T(8,128)S(1)} %shard_map.61), channel_id=1, source_target_pairs={{0,48},{8,56},{1,49},{9,57},{16,32},{24,40},{17,33},{25,41},{32,16... | collective-permute-start | bytes 147464 | tf_op jit(solution)/shard_map/ppermute | solution.py:24
  99.5 0.2 collective-permute-start.13
  99.7 0.2 collective-permute-start.12
  99.9 1.0 all-to-all-done.1.parts_ref
  100.9 1.4 %shard_map.59.after_ref = f32[32,8,128]{2,1,0:T(8,128)} custom-call(s32[5]{0:T(128)S(1)} %stack.23.place_ref, f32[768,256]{1,0:T(8,128)S(1)} %bitcast.10, f32[32,8,256]{2,1,0:T(8,128)S(1)} %all-to-all-done.1.parts_ref), custom_call_target="tpu_custom_call" | custom-call | bytes 2097192 | tf_op jit(solution)/shard_map/pallas_call | solution.py:52
  102.3 4.5 %all-to-all-start.2 = ((f32[32,8,128]{2,1,0:T(8,128)}), f32[32,8,128]{2,1,0:T(8,128)S(1)}, u32[]{:S(2)}, u32[]{:S(2)}) async-start(f32[32,8,128]{2,1,0:T(8,128)} %shard_map.59.after_ref), calls=%async_computation.2 | async-start | bytes 262144 | tf_op jit(solution)/shard_map/all_to_all | solution.py:367
  106.8 0.0 collective-permute-done.14
  106.8 0.0 collective-permute-done.13
  106.8 0.0 collective-permute-done.12
  106.8 2.6 %collective-permute-start.17 = (f32[64,768]{1,0:T(8,128)S(1)}, f32[64,768]{1,0:T(8,128)S(1)}, u32[]{:S(2)}, u32[]{:S(2)}) collective-permute-start(f32[64,768]{1,0:T(8,128)S(1)} %shard_map.62), channel_id=1, source_target_pairs={{0,192},{8,200},{1,193},{9,201},{16,208},{24,216},{17,209},{25,217... | collective-permute-start | bytes 589832 | tf_op jit(solution)/shard_map/ppermute | solution.py:24
  109.5 0.6 collective-permute-start.16
  110.0 0.2 collective-permute-start.15
  110.2 5.7 %all-to-all-done.2 = f32[32,8,128]{2,1,0:T(8,128)S(1)} async-done(((f32[32,8,128]{2,1,0:T(8,128)}), f32[32,8,128]{2,1,0:T(8,128)S(1)}, u32[]{:S(2)}, u32[]{:S(2)}) %all-to-all-start.2) | async-done | bytes 131104 | tf_op jit(solution)/shard_map/all_to_all | solution.py:367
  115.9 0.8 broadcast_in_dim.2
  116.7 4.2 %all-to-all-start.3 = ((f32[4,32,8,128]{3,2,1,0:T(8,128)}), f32[4,32,8,128]{3,2,1,0:T(8,128)S(1)}, u32[]{:S(2)}, u32[]{:S(2)}) async-start(f32[4,32,8,128]{3,2,1,0:T(8,128)} %broadcast_in_dim.2), calls=%async_computation.3 | async-start | bytes 1048576 | tf_op jit(solution)/shard_map/all_to_all | solution.py:372
  120.9 0.0 collective-permute-done.17
  120.9 0.0 collective-permute-done.16
  120.9 0.1 pad_maximum_fusion.mine_ref
  121.0 3.3 %collective-permute-start.18 = (f32[256,768]{1,0:T(8,128)S(1)}, f32[256,768]{1,0:T(8,128)S(1)}, u32[]{:S(2)}, u32[]{:S(2)}) collective-permute-start(f32[256,768]{1,0:T(8,128)S(1)} %pad_maximum_fusion.mine_ref), channel_id=1, source_target_pairs={{0,8},{8,0},{1,9},{9,1},{16,24},{24,16},{17,25},{25,17},{32,40},{4... | collective-permute-start | bytes 2359304 | tf_op jit(solution)/shard_map/ppermute | solution.py:24
  124.3 3.5 %all-to-all-done.3 = f32[4,32,8,128]{3,2,1,0:T(8,128)S(1)} async-done(((f32[4,32,8,128]{3,2,1,0:T(8,128)}), f32[4,32,8,128]{3,2,1,0:T(8,128)S(1)}, u32[]{:S(2)}, u32[]{:S(2)}) %all-to-all-start.3) | async-done | bytes 524320 | tf_op jit(solution)/shard_map/all_to_all | solution.py:372
  127.9 4.4 %collective-permute-start.19 = (f32[128,8,128]{2,1,0:T(8,128)S(1)}, f32[128,8,128]{2,1,0:T(8,128)S(1)}, u32[]{:S(2)}, u32[]{:S(2)}) collective-permute-start(f32[128,8,128]{2,1,0:T(8,128)S(1)} %bitcast.8), channel_id=1, source_target_pairs={{0,8},{8,0},{1,9},{9,1},{16,24},{24,16},{17,25},{25,17},{32,40},{4... | collective-permute-start | bytes 1572872 | tf_op jit(solution)/shard_map/ppermute | solution.py:24
  132.2 1.8 %shard_map.63 = f32[512,768]{1,0:T(8,128)} custom-call(s32[5]{0:T(128)S(1)} %stack.23.place_ref, f32[256,768]{1,0:T(8,128)S(1)} %pad_maximum_fusion.mine_ref, f32[256,768]{1,0:T(8,128)S(1)} %collective-permute-done.18.theirs_ref), custom_call_target="tpu_custom_call" | custom-call | bytes 3145768 | tf_op jit(solution)/shard_map/pallas_call | solution.py:52
  134.0 0.0 collective-permute-done.19.theirs_ref
  134.0 1.6 %shard_map.64 = f32[768,256]{1,0:T(8,128)} custom-call(s32[5]{0:T(128)S(1)} %stack.23.place_ref, f32[128,8,128]{2,1,0:T(8,128)S(1)} %bitcast.9, f32[128,8,128]{2,1,0:T(8,128)S(1)} %collective-permute-done.19.theirs_ref), custom_call_target="tpu_custom_call" | custom-call | bytes 2097192 | tf_op jit(solution)/shard_map/pallas_call | solution.py:52
  (10 shorter events, 0.1 us)
Async XLA Ops:
  0.8 1.4 %copy-start = (bf16[1024,768]{1,0:T(8,128)(2,1)S(1)}, bf16[1024,768]{1,0:T(8,128)(2,1)}, u32[]{:S(2)}) copy-start(bf16[1024,768]{1,0:T(8,128)(2,1)} %emb_ref.5) | copy-start | bytes 4718596
  2.2 1.1 copy-start.3
  5.4 22.9 %copy-start.1 = (bf16[1024,768]{1,0:T(8,128)(2,1)S(1)}, bf16[1024,768]{1,0:T(8,128)(2,1)}, u32[]{:S(2)}) copy-start(bf16[1024,768]{1,0:T(8,128)(2,1)} %emb_ref.5) | copy-start | bytes 4718596
  29.3 5.9 %collective-permute-start.6 = (f32[256,896]{1,0:T(8,128)S(1)}, f32[256,896]{1,0:T(8,128)S(1)}, u32[]{:S(2)}, u32[]{:S(2)}) collective-permute-start(f32[256,896]{1,0:T(8,128)S(1)} %get-tuple-element.44), channel_id=1, source_target_pairs={{0,8},{8,0},{1,9},{9,1},{16,24},{24,16},{17,25},{25,17},{32,40},{4... | collective-permute-start | bytes 2752520 | tf_op jit(solution)/shard_map/ppermute | solution.py:24
  31.5 12.2 %collective-permute-start = (f32[96,1024]{1,0:T(8,128)S(1)}, f32[96,1024]{1,0:T(8,128)S(1)}, u32[]{:S(2)}, u32[]{:S(2)}) collective-permute-start(f32[96,1024]{1,0:T(8,128)S(1)} %get-tuple-element.34), channel_id=1, source_target_pairs={{0,4},{8,12},{1,5},{9,13},{16,20},{24,28},{17,21},{25,29},{32,36},... | collective-permute-start | bytes 1179656 | tf_op jit(solution)/shard_map/ppermute | solution.py:24
  32.5 20.0 %collective-permute-start.1 = (f32[96,1024]{1,0:T(8,128)S(1)}, f32[96,1024]{1,0:T(8,128)S(1)}, u32[]{:S(2)}, u32[]{:S(2)}) collective-permute-start(f32[96,1024]{1,0:T(8,128)S(1)} %get-tuple-element.35), channel_id=1, source_target_pairs={{0,2},{8,10},{1,3},{9,11},{16,18},{24,26},{17,19},{25,27},{32,34},... | collective-permute-start | bytes 1179656 | tf_op jit(solution)/shard_map/ppermute | solution.py:24
  33.0 19.5 %collective-permute-start.2 = (f32[96,1024]{1,0:T(8,128)S(1)}, f32[96,1024]{1,0:T(8,128)S(1)}, u32[]{:S(2)}, u32[]{:S(2)}) collective-permute-start(f32[96,1024]{1,0:T(8,128)S(1)} %get-tuple-element.36), channel_id=1, source_target_pairs={{0,6},{8,14},{1,7},{9,15},{16,22},{24,30},{17,23},{25,31},{32,38},... | collective-permute-start | bytes 1179656 | tf_op jit(solution)/shard_map/ppermute | solution.py:24
  35.3 21.3 %collective-permute-start.7 = (f32[128,896]{1,0:T(8,128)S(1)}, f32[128,896]{1,0:T(8,128)S(1)}, u32[]{:S(2)}, u32[]{:S(2)}) collective-permute-start(f32[128,896]{1,0:T(8,128)S(1)} %get-tuple-element.46), channel_id=1, source_target_pairs={{0,128},{8,136},{1,129},{9,137},{16,144},{24,152},{17,145},{25,153... | collective-permute-start | bytes 1376264 | tf_op jit(solution)/shard_map/ppermute | solution.py:24
  52.6 16.1 %collective-permute-start.9 = (f32[96,1024]{1,0:T(8,128)S(1)}, f32[96,1024]{1,0:T(8,128)S(1)}, u32[]{:S(2)}, u32[]{:S(2)}) collective-permute-start(f32[96,1024]{1,0:T(8,128)S(1)} %shard_map.52.after_ref), channel_id=1, source_target_pairs={{0,1},{8,9},{1,0},{9,8},{16,17},{24,25},{17,16},{25,24},{32,33},{4... | collective-permute-start | bytes 1179656 | tf_op jit(solution)/shard_map/ppermute | solution.py:24
  53.1 23.3 %collective-permute-start.3 = (f32[96,1024]{1,0:T(8,128)S(1)}, f32[96,1024]{1,0:T(8,128)S(1)}, u32[]{:S(2)}, u32[]{:S(2)}) collective-permute-start(f32[96,1024]{1,0:T(8,128)S(1)} %get-tuple-element.38), channel_id=1, source_target_pairs={{0,4},{8,12},{1,5},{9,13},{16,20},{24,28},{17,21},{25,29},{32,36},... | collective-permute-start | bytes 1179656 | tf_op jit(solution)/shard_map/ppermute | solution.py:24
  53.8 22.6 %collective-permute-start.4 = (f32[96,1024]{1,0:T(8,128)S(1)}, f32[96,1024]{1,0:T(8,128)S(1)}, u32[]{:S(2)}, u32[]{:S(2)}) collective-permute-start(f32[96,1024]{1,0:T(8,128)S(1)} %get-tuple-element.39), channel_id=1, source_target_pairs={{0,2},{8,10},{1,3},{9,11},{16,18},{24,26},{17,19},{25,27},{32,34},... | collective-permute-start | bytes 1179656 | tf_op jit(solution)/shard_map/ppermute | solution.py:24
  54.6 21.8 %collective-permute-start.5 = (f32[96,1024]{1,0:T(8,128)S(1)}, f32[96,1024]{1,0:T(8,128)S(1)}, u32[]{:S(2)}, u32[]{:S(2)}) collective-permute-start(f32[96,1024]{1,0:T(8,128)S(1)} %get-tuple-element.40), channel_id=1, source_target_pairs={{0,6},{8,14},{1,7},{9,15},{16,22},{24,30},{17,23},{25,31},{32,38},... | collective-permute-start | bytes 1179656 | tf_op jit(solution)/shard_map/ppermute | solution.py:24
  56.6 19.8 %copy-start.2 = (f32[96,8,256]{2,1,0:T(8,128)S(1)}, f32[96,8,256]{2,1,0:T(8,128)}, u32[]{:S(2)}) copy-start(f32[96,8,256]{2,1,0:T(8,128)} %all_books_ref.1) | copy-start | bytes 2359300
  56.6 5.4 %collective-permute-start.8 = (f32[64,896]{1,0:T(8,128)S(1)}, f32[64,896]{1,0:T(8,128)S(1)}, u32[]{:S(2)}, u32[]{:S(2)}) collective-permute-start(f32[64,896]{1,0:T(8,128)S(1)} %get-tuple-element.48), channel_id=1, source_target_pairs={{0,64},{8,72},{1,65},{9,73},{16,80},{24,88},{17,81},{25,89},{32,96... | collective-permute-start | bytes 688136 | tf_op jit(solution)/shard_map/ppermute | solution.py:24
  68.7 13.5 %collective-permute-start.10 = (f32[32,896]{1,0:T(8,128)S(1)}, f32[32,896]{1,0:T(8,128)S(1)}, u32[]{:S(2)}, u32[]{:S(2)}) collective-permute-start(f32[32,896]{1,0:T(8,128)S(1)} %get-tuple-element.51), channel_id=1, source_target_pairs={{0,32},{8,40},{1,33},{9,41},{16,48},{24,56},{17,49},{25,57},{32,0}... | collective-permute-start | bytes 344072 | tf_op jit(solution)/shard_map/ppermute | solution.py:24
  82.2 18.6 %all-to-all-start.1 = ((f32[32,8,256]{2,1,0:T(8,128)}), f32[32,8,256]{2,1,0:T(8,128)S(1)}, u32[]{:S(2)}, u32[]{:S(2)}) async-start(f32[32,8,256]{2,1,0:T(8,128)} %shard_map.58), calls=%async_computation.1 | async-start | bytes 524288 | tf_op jit(solution)/shard_map/all_to_all | solution.py:347
  89.7 6.2 %collective-permute-start.11 = (f32[16,896]{1,0:T(8,128)S(1)}, f32[16,896]{1,0:T(8,128)S(1)}, u32[]{:S(2)}, u32[]{:S(2)}) collective-permute-start(f32[16,896]{1,0:T(8,128)S(1)} %get-tuple-element.56), channel_id=1, source_target_pairs={{0,16},{8,24},{1,17},{9,25},{16,0},{24,8},{17,1},{25,9},{32,48},{4... | collective-permute-start | bytes 172040 | tf_op jit(solution)/shard_map/ppermute | solution.py:24
  95.9 10.8 %collective-permute-start.14 = (f32[16,768]{1,0:T(8,128)S(1)}, f32[16,768]{1,0:T(8,128)S(1)}, u32[]{:S(2)}, u32[]{:S(2)}) collective-permute-start(f32[16,768]{1,0:T(8,128)S(1)} %shard_map.61), channel_id=1, source_target_pairs={{0,48},{8,56},{1,49},{9,57},{16,32},{24,40},{17,33},{25,41},{32,16... | collective-permute-start | bytes 147464 | tf_op jit(solution)/shard_map/ppermute | solution.py:24
  99.5 7.3 %collective-permute-start.13 = (f32[16,768]{1,0:T(8,128)S(1)}, f32[16,768]{1,0:T(8,128)S(1)}, u32[]{:S(2)}, u32[]{:S(2)}) collective-permute-start(f32[16,768]{1,0:T(8,128)S(1)} %shard_map.61), channel_id=1, source_target_pairs={{0,32},{8,40},{1,33},{9,41},{16,48},{24,56},{17,49},{25,57},{32,0}... | collective-permute-start | bytes 147464 | tf_op jit(solution)/shard_map/ppermute | solution.py:24
  99.7 7.1 %collective-permute-start.12 = (f32[16,768]{1,0:T(8,128)S(1)}, f32[16,768]{1,0:T(8,128)S(1)}, u32[]{:S(2)}, u32[]{:S(2)}) collective-permute-start(f32[16,768]{1,0:T(8,128)S(1)} %shard_map.61), channel_id=1, source_target_pairs={{0,16},{8,24},{1,17},{9,25},{16,0},{24,8},{17,1},{25,9},{32,48},{4... | collective-permute-start | bytes 147464 | tf_op jit(solution)/shard_map/ppermute | solution.py:24
  102.3 13.7 %all-to-all-start.2 = ((f32[32,8,128]{2,1,0:T(8,128)}), f32[32,8,128]{2,1,0:T(8,128)S(1)}, u32[]{:S(2)}, u32[]{:S(2)}) async-start(f32[32,8,128]{2,1,0:T(8,128)} %shard_map.59.after_ref), calls=%async_computation.2 | async-start | bytes 262144 | tf_op jit(solution)/shard_map/all_to_all | solution.py:367
  106.8 14.1 %collective-permute-start.17 = (f32[64,768]{1,0:T(8,128)S(1)}, f32[64,768]{1,0:T(8,128)S(1)}, u32[]{:S(2)}, u32[]{:S(2)}) collective-permute-start(f32[64,768]{1,0:T(8,128)S(1)} %shard_map.62), channel_id=1, source_target_pairs={{0,192},{8,200},{1,193},{9,201},{16,208},{24,216},{17,209},{25,217... | collective-permute-start | bytes 589832 | tf_op jit(solution)/shard_map/ppermute | solution.py:24
  109.5 11.5 %collective-permute-start.16 = (f32[64,768]{1,0:T(8,128)S(1)}, f32[64,768]{1,0:T(8,128)S(1)}, u32[]{:S(2)}, u32[]{:S(2)}) collective-permute-start(f32[64,768]{1,0:T(8,128)S(1)} %shard_map.62), channel_id=1, source_target_pairs={{0,128},{8,136},{1,129},{9,137},{16,144},{24,152},{17,145},{25,153... | collective-permute-start | bytes 589832 | tf_op jit(solution)/shard_map/ppermute | solution.py:24
  110.0 10.9 %collective-permute-start.15 = (f32[64,768]{1,0:T(8,128)S(1)}, f32[64,768]{1,0:T(8,128)S(1)}, u32[]{:S(2)}, u32[]{:S(2)}) collective-permute-start(f32[64,768]{1,0:T(8,128)S(1)} %shard_map.62), channel_id=1, source_target_pairs={{0,64},{8,72},{1,65},{9,73},{16,80},{24,88},{17,81},{25,89},{32,96... | collective-permute-start | bytes 589832 | tf_op jit(solution)/shard_map/ppermute | solution.py:24
  116.7 11.1 %all-to-all-start.3 = ((f32[4,32,8,128]{3,2,1,0:T(8,128)}), f32[4,32,8,128]{3,2,1,0:T(8,128)S(1)}, u32[]{:S(2)}, u32[]{:S(2)}) async-start(f32[4,32,8,128]{3,2,1,0:T(8,128)} %broadcast_in_dim.2), calls=%async_computation.3 | async-start | bytes 1048576 | tf_op jit(solution)/shard_map/all_to_all | solution.py:372
  121.0 11.2 %collective-permute-start.18 = (f32[256,768]{1,0:T(8,128)S(1)}, f32[256,768]{1,0:T(8,128)S(1)}, u32[]{:S(2)}, u32[]{:S(2)}) collective-permute-start(f32[256,768]{1,0:T(8,128)S(1)} %pad_maximum_fusion.mine_ref), channel_id=1, source_target_pairs={{0,8},{8,0},{1,9},{9,1},{16,24},{24,16},{17,25},{25,17},{32,40},{4... | collective-permute-start | bytes 2359304 | tf_op jit(solution)/shard_map/ppermute | solution.py:24
  127.9 6.2 %collective-permute-start.19 = (f32[128,8,128]{2,1,0:T(8,128)S(1)}, f32[128,8,128]{2,1,0:T(8,128)S(1)}, u32[]{:S(2)}, u32[]{:S(2)}) collective-permute-start(f32[128,8,128]{2,1,0:T(8,128)S(1)} %bitcast.8), channel_id=1, source_target_pairs={{0,8},{8,0},{1,9},{9,1},{16,24},{24,16},{17,25},{25,17},{32,40},{4... | collective-permute-start | bytes 1572872 | tf_op jit(solution)/shard_map/ppermute | solution.py:24
